TPU v7x, 32 devices: a whole 2x2x4 slice. The times are simulated.
32 devices in a mesh: space: 8 (over z, y), wt: 4 (over x, core).
Axes of the slice: x: 2, y: 2, z: 4, core: 2. Of those that a mesh axis runs over, the one named last changes fastest.
Arguments:
- features: bfloat16 [12288, 256], P(('space', 'wt')), may hold values from -6 to 6
- distances: float32 [12288, 64], P(('space', 'wt')), may hold values from 0.9 to 5.9
- neighbours: int32 [12288, 64], P(('space', 'wt')), may hold values from 0 to 575, as said below
- counts: int32 [12288], P(('space', 'wt')), may hold values from 1 to 64, as said below
- rbf_weight: bfloat16 [600, 256], P('wt'), may hold values from -3 to 3
- query_weight: bfloat16 [256, 256], P('wt'), may hold values from -0.375 to 0.375
- key_weight: bfloat16 [256, 256], P('wt'), may hold values from -0.375 to 0.375
- value_weight: bfloat16 [256, 256], P('wt'), may hold values from -0.375 to 0.375
- out_weight: bfloat16 [256, 256], P('wt'), may hold values from -1.5 to 1.5
- gate_weight: bfloat16 [256, 1024], P('wt'), may hold values from -0.375 to 0.375
- up_weight: bfloat16 [256, 1024], P('wt'), may hold values from -0.375 to 0.375
- down_weight: bfloat16 [1024, 256], P('wt'), may hold values from -0.1875 to 0.1875
- attn_gain: bfloat16 [256], P('wt'), may hold values from 0.5 to 1.5
- ffn_gain: bfloat16 [256], P('wt'), may hold values from 0.5 to 1.5
- readout: bfloat16 [256], P('wt'), may hold values from -0.375 to 0.375
- grad_out: bfloat16 [12288, 256], P(('space', 'wt')), may hold values from -6 to 6
- grad_energy: float32 [12288], P(('space', 'wt')), may hold values from -6 to 6
Outputs:
- activations: float32 [12288, 256], P(('space', 'wt'))
- energy: float32 [12288], P(('space', 'wt'))
- grad_features: float32 [12288, 256], P(('space', 'wt'))
- grad_rbf_weight: float32 [600, 256], P('wt')
- grad_query_weight: float32 [256, 256], P('wt')
- grad_key_weight: float32 [256, 256], P('wt')
- grad_value_weight: float32 [256, 256], P('wt')
- grad_out_weight: float32 [256, 256], P('wt')
- grad_gate_weight: float32 [256, 1024], P('wt')
- grad_up_weight: float32 [256, 1024], P('wt')
- grad_down_weight: float32 [1024, 256], P('wt')
- grad_attn_gain: float32 [256], P('wt')
- grad_ffn_gain: float32 [256], P('wt')
- grad_readout: float32 [256], P('wt')
Inputs may be any that keep to these rules, and one draw needn't show every extreme that they name: `neighbours`: rows of the lookup table of 576 rows. The atom at place p of its region names only rows p to p + 192; atoms of the first region never name the table's lower 96 rows and atoms of the last region never its upper 96 rows. `counts`: regions differ widely in their mean count.
All inputs are finite; a program needn't handle non-finite values.
Results may differ from a plain program's by a relative error of at most 0.014.
Values may be sent and summed in bfloat16 or wider, within the bound.
No kernel may reach another device: no remote copies, remote signals or barrier semaphores. Data moves between devices by JAX's collectives and lax.ppermute only.
A program may use at most 256 MiB of HBM per device.

v0:
```python
import jax
import jax.numpy as jnp
from jax import lax
from jax.sharding import PartitionSpec as P

HEADS = 8
HALO = 96


EPSILON = 1e-06
CUTOFF = 6.0


def padded(value, sides, width):
    for axis, dim in sides:
        size, length = (lax.axis_size(axis), value.shape[dim])
        up = [(i, (i + 1) % size) for i in range(size - 1)]
        down = [(j, i) for i, j in up]
        last = lax.slice_in_dim(value, length - width, length, axis=dim)
        initial = lax.slice_in_dim(value, 0, width, axis=dim)
        before = lax.ppermute(last, axis, up)
        after = lax.ppermute(initial, axis, down)
        value = jnp.concatenate([before, value, after], axis=dim)
    return value


def from_behind(value, axis, by):
    length = lax.axis_size(axis)
    pairs = [(i, i + by) for i in range(length) if 0 <= i + by < length]
    return lax.ppermute(value, axis, pairs)


def radial_basis(distances, basis_count):
    centers = jnp.arange(basis_count, dtype=jnp.float32) * (CUTOFF / basis_count)
    spread = 2.0 * CUTOFF / basis_count
    envelope = 0.5 * (jnp.cos(jnp.pi * distances / CUTOFF) + 1.0)
    return (
        jnp.exp(-0.5 * jnp.square((distances[..., None] - centers) / spread)) * envelope[..., None]
    )


def matmul(left, right):
    return jnp.dot(left, right, preferred_element_type=jnp.float32)


def matmul_left(left, right):
    return lax.dot_general(
        left, right, (((0,), (0,)), ((), ())), preferred_element_type=jnp.float32
    )


def matmul_right(left, right):
    return lax.dot_general(
        left, right, (((1,), (1,)), ((), ())), preferred_element_type=jnp.float32
    )


def norm_back(grad_normed, normed_rows, inverse):
    return inverse * (
        grad_normed - normed_rows * jnp.mean(grad_normed * normed_rows, -1, keepdims=True)
    )


def local(
    features,
    distances,
    neighbours,
    counts,
    rbf_weight,
    query_weight,
    key_weight,
    value_weight,
    out_weight,
    gate_weight,
    up_weight,
    down_weight,
    attn_gain,
    ffn_gain,
    readout,
    grad_out,
    grad_energy,
):
    w_rbf, w_query, w_key, w_value, w_out, w_gate, w_up, w_down, gain_attn, gain_ffn, w_read = (
        lax.all_gather(rbf_weight, "wt", axis=0, tiled=True),
        lax.all_gather(query_weight, "wt", axis=0, tiled=True),
        lax.all_gather(key_weight, "wt", axis=0, tiled=True),
        lax.all_gather(value_weight, "wt", axis=0, tiled=True),
        lax.all_gather(out_weight, "wt", axis=0, tiled=True),
        lax.all_gather(gate_weight, "wt", axis=0, tiled=True),
        lax.all_gather(up_weight, "wt", axis=0, tiled=True),
        lax.all_gather(down_weight, "wt", axis=0, tiled=True),
        lax.all_gather(attn_gain, "wt", axis=0, tiled=True),
        lax.all_gather(ffn_gain, "wt", axis=0, tiled=True),
        lax.all_gather(readout, "wt", axis=0, tiled=True),
    )
    atom_count, model_width = features.shape
    slot_count = neighbours.shape[1]
    basis_count = w_rbf.shape[0]
    hidden_count = w_gate.shape[1]
    head_size = model_width // HEADS
    edge_count = atom_count * slot_count
    score_scale = head_size ** (-0.5)
    gain_one = gain_attn.astype(jnp.float32)
    gain_two = gain_ffn.astype(jnp.float32)
    read_vector = w_read.astype(jnp.float32)
    extended = padded(features, ((("space", "wt"), 0),), HALO)
    ext_float = extended.astype(jnp.float32)
    inverse_one = lax.rsqrt(jnp.mean(ext_float * ext_float, -1, keepdims=True) + EPSILON)
    normed_one = ext_float * inverse_one
    lookup = (normed_one * gain_one).astype(jnp.bfloat16)
    basis_rows = (
        radial_basis(distances, basis_count).astype(jnp.bfloat16).reshape(edge_count, basis_count)
    )
    flat_rows = neighbours.reshape(-1)
    edge_input = (lookup[flat_rows].astype(jnp.float32) + matmul(basis_rows, w_rbf)).astype(
        jnp.bfloat16
    )
    own_lookup = lookup[HALO : HALO + atom_count]
    queries = matmul(own_lookup, w_query).astype(jnp.bfloat16)
    key_value_w = jnp.concatenate([w_key, w_value], 1)
    keyvals = matmul(edge_input, key_value_w).astype(jnp.bfloat16)
    key_heads = keyvals[:, :model_width].reshape(atom_count, slot_count, HEADS, head_size)
    value_heads = keyvals[:, model_width:].reshape(atom_count, slot_count, HEADS, head_size)
    query_heads = queries.reshape(atom_count, HEADS, head_size)
    scores = (
        jnp.einsum("ahd,akhd->ahk", query_heads, key_heads, preferred_element_type=jnp.float32)
        * score_scale
    )
    usable = jnp.arange(slot_count, dtype=jnp.int32)[None, None, :] < counts[:, None, None]
    scores = jnp.where(usable, scores, -1e30)
    soft_weights = jax.nn.softmax(scores, -1)
    soft_low = soft_weights.astype(jnp.bfloat16)
    attended = jnp.einsum(
        "ahk,akhd->ahd", soft_low, value_heads, preferred_element_type=jnp.float32
    )
    attended = attended.astype(jnp.bfloat16).reshape(atom_count, model_width)
    residual = features.astype(jnp.float32) + matmul(attended, w_out)
    inverse_two = lax.rsqrt(jnp.mean(residual * residual, -1, keepdims=True) + EPSILON)
    normed_two = residual * inverse_two
    hidden_in = (normed_two * gain_two).astype(jnp.bfloat16)
    gate_up_w = jnp.concatenate([w_gate, w_up], 1)
    gate_up = matmul(hidden_in, gate_up_w)
    gate_pre = gate_up[:, :hidden_count]
    up_pre = gate_up[:, hidden_count:]
    sigmoid_gate = jax.nn.sigmoid(gate_pre)
    silu_gate = gate_pre * sigmoid_gate
    activated = (silu_gate * up_pre).astype(jnp.bfloat16)
    outputs = residual + matmul(activated, w_down)
    energy = jnp.sum(outputs * read_vector, -1)
    grad_act = grad_out.astype(jnp.float32) + grad_energy[:, None] * read_vector
    grad_read = jnp.sum(grad_energy[:, None] * outputs, 0)
    grad_branch = grad_act.astype(jnp.bfloat16)
    grad_down = matmul_left(activated, grad_branch)
    grad_activated = matmul_right(grad_branch, w_down)
    grad_gate = grad_activated * up_pre * sigmoid_gate * (1.0 + gate_pre * (1.0 - sigmoid_gate))
    grad_upper = grad_activated * silu_gate
    grad_gate_up = jnp.concatenate([grad_gate, grad_upper], 1).astype(jnp.bfloat16)
    grad_gate_up_w = matmul_left(hidden_in, grad_gate_up)
    grad_hidden = matmul_right(grad_gate_up, gate_up_w).astype(jnp.bfloat16).astype(jnp.float32)
    grad_gain_two = jnp.sum(grad_hidden * normed_two, 0)
    grad_residual = grad_act + norm_back(grad_hidden * gain_two, normed_two, inverse_two)
    grad_proj = grad_residual.astype(jnp.bfloat16)
    grad_outw = matmul_left(attended, grad_proj)
    grad_attended = (
        matmul_right(grad_proj, w_out).astype(jnp.bfloat16).reshape(atom_count, HEADS, head_size)
    )
    grad_soft = jnp.einsum(
        "ahd,akhd->ahk", grad_attended, value_heads, preferred_element_type=jnp.float32
    )
    grad_values = jnp.einsum(
        "ahk,ahd->akhd", soft_low, grad_attended, preferred_element_type=jnp.float32
    )
    grad_scores = (
        soft_weights
        * (grad_soft - jnp.sum(soft_weights * grad_soft, -1, keepdims=True))
        * score_scale
    )
    grad_queries = jnp.einsum("ahk,akhd->ahd", grad_scores, key_heads.astype(jnp.float32))
    grad_queries = grad_queries.astype(jnp.bfloat16).reshape(atom_count, model_width)
    grad_keys = jnp.einsum("ahk,ahd->akhd", grad_scores, query_heads.astype(jnp.float32))
    grad_keyvals = jnp.concatenate(
        [grad_keys.reshape(edge_count, model_width), grad_values.reshape(edge_count, model_width)],
        1,
    ).astype(jnp.bfloat16)
    grad_kv_w = matmul_left(edge_input, grad_keyvals)
    grad_edge = matmul_right(grad_keyvals, key_value_w).astype(jnp.bfloat16)
    grad_rbfw = matmul_left(basis_rows, grad_edge)
    grad_queryw = matmul_left(own_lookup, grad_queries)
    grad_lookup = jax.ops.segment_sum(
        grad_edge.astype(jnp.float32), flat_rows, num_segments=atom_count + 2 * HALO
    )
    grad_lookup = grad_lookup.at[HALO : HALO + atom_count].add(matmul_right(grad_queries, w_query))
    grad_gain_one = jnp.sum(grad_lookup * normed_one, 0)
    grad_extended = norm_back(grad_lookup * gain_one, normed_one, inverse_one)
    from_upper = from_behind(grad_extended[:HALO], ("space", "wt"), -1)
    from_lower = from_behind(
        grad_extended[HALO + atom_count :].astype(jnp.bfloat16), ("space", "wt"), 1
    ).astype(jnp.float32)
    grad_features = grad_residual + grad_extended[HALO : HALO + atom_count]
    grad_features = grad_features.at[:HALO].add(from_lower)
    grad_features = grad_features.at[atom_count - HALO :].add(from_upper)
    partials = (
        grad_rbfw,
        grad_queryw,
        grad_kv_w[:, :model_width],
        grad_kv_w[:, model_width:],
        grad_outw,
        grad_gate_up_w[:, :hidden_count],
        grad_gate_up_w[:, hidden_count:],
        grad_down,
        grad_gain_one,
        grad_gain_two,
        grad_read,
    )
    summed = lax.psum(
        (
            partials[0],
            partials[1],
            partials[2],
            partials[3],
            partials[4],
            partials[5],
            partials[6],
            partials[7],
            partials[8],
            partials[9],
            partials[10],
        ),
        "space",
    )
    shards = (
        lax.psum_scatter(summed[0], "wt", scatter_dimension=0, tiled=True),
        lax.psum_scatter(summed[1], "wt", scatter_dimension=0, tiled=True),
        lax.psum_scatter(summed[2], "wt", scatter_dimension=0, tiled=True),
        lax.psum_scatter(summed[3], "wt", scatter_dimension=0, tiled=True),
        lax.psum_scatter(summed[4], "wt", scatter_dimension=0, tiled=True),
        lax.psum_scatter(summed[5], "wt", scatter_dimension=0, tiled=True),
        lax.psum_scatter(summed[6], "wt", scatter_dimension=0, tiled=True),
        lax.psum_scatter(summed[7], "wt", scatter_dimension=0, tiled=True),
        lax.psum_scatter(summed[8], "wt", scatter_dimension=0, tiled=True),
        lax.psum_scatter(summed[9], "wt", scatter_dimension=0, tiled=True),
        lax.psum_scatter(summed[10], "wt", scatter_dimension=0, tiled=True),
    )
    return (
        outputs,
        energy,
        grad_features,
        shards[0],
        shards[1],
        shards[2],
        shards[3],
        shards[4],
        shards[5],
        shards[6],
        shards[7],
        shards[8],
        shards[9],
        shards[10],
    )


def solution(mesh):
    in_specs = (
        P(("space", "wt"), None),
        P(("space", "wt"), None),
        P(("space", "wt"), None),
        P(("space", "wt")),
        P("wt", None),
        P("wt", None),
        P("wt", None),
        P("wt", None),
        P("wt", None),
        P("wt", None),
        P("wt", None),
        P("wt", None),
        P("wt"),
        P("wt"),
        P("wt"),
        P(("space", "wt"), None),
        P(("space", "wt")),
    )
    out_specs = (
        P(("space", "wt"), None),
        P(("space", "wt")),
        P(("space", "wt"), None),
        P("wt", None),
        P("wt", None),
        P("wt", None),
        P("wt", None),
        P("wt", None),
        P("wt", None),
        P("wt", None),
        P("wt", None),
        P("wt"),
        P("wt"),
        P("wt"),
    )
    return jax.shard_map(local, mesh=mesh, in_specs=in_specs, out_specs=out_specs, check_vma=False)
```

profile of v0, /device:TPU:0, one launch (start us, length us, event | category | flops | bytes accessed | tf_op | source)
XLA Modules:
  0.0 1063.5 jit_solution(14116061780657212769)
XLA Ops:
  91.1 96.7 %gather_fusion = bf16[24576,256]{1,0:T(8,128)(2,1)} fusion(bf16[576,256]{1,0:T(8,128)(2,1)S(1)} %fusion.40, s32[24576]{0:T(1024)S(1)} %broadcast_clamp_fusion), kind=kCustom, calls=%fused_computation | custom fusion | bytes 25264128 | tf_op jit(solution)/shard_map/gather | solution.py:115
  187.9 25.1 %fusion.4 = bf16[24576,256]{1,0:T(8,128)(2,1)} fusion(bf16[600,256]{1,0:T(8,128)(2,1)S(1)} %reshape.256, f32[24576]{0:T(1024)S(1)} %mul.195, f32[600]{0:T(1024)S(1)} %iota_multiply_fusion, f32[24576]{0:T(1024)S(1)} %sub.41, bf16[24576,256]{1,0:T(8,128)(2,1)} %gather_fusion), kind=kOutput, calls=%fused_computation.10 | convolution fusion | flops 7657095168 | bytes 25672032 | tf_op jit(solution)/shard_map/dot_general | solution.py:43
  212.9 21.2 %convolution_convert_fusion = bf16[24576,512]{1,0:T(8,128)(2,1)} fusion(bf16[24576,256]{1,0:T(8,128)(2,1)} %fusion.4, bf16[256,512]{1,0:T(8,128)(2,1)S(1)} %constant_dynamic-update-slice_fusion), kind=kOutput, calls=%fused_computation.8 | convolution fusion | flops 6455033856 | bytes 38010880 | tf_op jit(solution)/shard_map/dot_general | solution.py:43
  234.2 16.9 %fusion.76 = (bf16[24576,256]{1,0:T(8,128)(2,1)}, bf16[24576,256]{1,0:T(8,128)(2,1)}) fusion(bf16[24576,512]{1,0:T(8,128)(2,1)} %convolution_convert_fusion), kind=kLoop, calls=%fused_computation.125 | loop fusion | bytes 50331648 | tf_op jit(solution)/shard_map/slice | solution.py:122
  251.1 16.7 %copy.49 = bf16[24576,256]{0,1:T(8,128)(2,1)} copy(bf16[24576,256]{1,0:T(8,128)(2,1)} %get-tuple-element.73) | data formatting | bytes 25165824 | tf_op jit(solution)/shard_map/slice | solution.py:122
  267.8 34.4 %reshape.222 = bf16[384,64,8,32]{1,0,3,2:T(8,128)(2,1)} reshape(bf16[24576,256]{0,1:T(8,128)(2,1)} %copy.49) | data formatting | bytes 25165824 | tf_op jit(solution)/shard_map/reshape | solution.py:122
  302.2 76.6 %fusion.16 = f32[384,8,1,64]{3,2,1,0:T(1,128)} fusion(bf16[384,8,32,1]{2,3,1,0:T(2,128)(2,1)S(1)} %copy.52, bf16[384,64,8,32]{1,0,3,2:T(8,128)(2,1)} %reshape.222), kind=kOutput, calls=%fused_computation.23 | convolution fusion | flops 12582912 | bytes 13565952 | tf_op jit(solution)/shard_map/ahd,akhd->ahk/dot_general | solution.py:126
  385.5 16.7 %copy.50 = bf16[24576,256]{0,1:T(8,128)(2,1)} copy(bf16[24576,256]{1,0:T(8,128)(2,1)} %get-tuple-element.74) | data formatting | bytes 25165824 | tf_op jit(solution)/shard_map/slice | solution.py:123
  402.2 34.3 %reshape.223 = bf16[384,64,8,32]{1,0,3,2:T(8,128)(2,1)} reshape(bf16[24576,256]{0,1:T(8,128)(2,1)} %copy.50) | data formatting | bytes 25165824 | tf_op jit(solution)/shard_map/reshape | solution.py:123
  436.5 57.4 %fusion.12 = bf16[384,8,1,32]{3,2,1,0:T(2,128)(2,1)} fusion(bf16[384,64,8,32]{1,0,3,2:T(8,128)(2,1)} %reshape.223, bf16[384,8,64,1]{2,0,1,3:T(8,128)(2,1)} %get-tuple-element.81), kind=kOutput, calls=%fused_computation.19 | convolution fusion | flops 12582912 | bytes 13172736 | tf_op jit(solution)/shard_map/ahk,akhd->ahd/dot_general | solution.py:133
  510.9 72.4 %fusion.10 = f32[384,8,1,64]{3,2,1,0:T(1,128)} fusion(bf16[384,8,32,1]{2,3,1,0:T(2,128)(2,1)} %copy.58, bf16[384,64,8,32]{1,0,3,2:T(8,128)(2,1)} %reshape.223), kind=kOutput, calls=%fused_computation.17 | convolution fusion | flops 12582912 | bytes 13565952 | tf_op jit(solution)/shard_map/ahd,akhd->ahk/dot_general | solution.py:167
  587.0 55.9 %fusion.14 = bf16[384,8,1,32]{3,2,1,0:T(2,128)(2,1)} fusion(bf16[384,64,8,32]{1,0,3,2:T(8,128)(2,1)} %reshape.222, f32[384,8,64,1]{2,0,1,3:T(8,128)S(1)} %bitcast.82), kind=kOutput, calls=%fused_computation.21 | convolution fusion | flops 12582912 | bytes 13565952 | tf_op jit(solution)/shard_map/ahk,akhd->ahd/dot_general | solution.py:178
  642.8 16.0 %fusion.6 = bf16[384,64,8,32]{1,0,3,2:T(8,128)(2,1)} fusion(f32[384,8,64]{2,0,1:T(8,128)S(1)} %fusion.21, f32[384,8,32]{0,2,1:T(8,128)S(1)} %copy-done.14), kind=kLoop, calls=%fused_computation.13 | loop fusion | flops 12582912 | bytes 13762560 | tf_op jit(solution)/shard_map/ahk,ahd->akhd/transpose | solution.py:180
  658.9 32.8 %reshape.226 = bf16[24576,256]{0,1:T(8,128)(2,1)} reshape(bf16[384,64,8,32]{1,0,3,2:T(8,128)(2,1)} %fusion.6) | data formatting | bytes 25165824 | tf_op jit(solution)/shard_map/reshape | solution.py:182
  702.3 15.9 %fusion.7 = bf16[384,64,8,32]{1,0,3,2:T(8,128)(2,1)} fusion(f32[384,8,64]{2,0,1:T(8,128)S(1)} %get-tuple-element.80, f32[384,8,32]{0,2,1:T(8,128)S(1)} %copy-done.15), kind=kLoop, calls=%fused_computation.14 | loop fusion | flops 12582912 | bytes 13762560 | tf_op jit(solution)/shard_map/ahk,ahd->akhd/transpose | solution.py:170
  721.6 32.9 %reshape.227 = bf16[24576,256]{0,1:T(8,128)(2,1)} reshape(bf16[384,64,8,32]{1,0,3,2:T(8,128)(2,1)} %fusion.7) | data formatting | bytes 25165824 | tf_op jit(solution)/shard_map/reshape | solution.py:182
  755.5 10.6 constant_dynamic-update-slice_fusion.4
  766.1 14.9 %fusion.81 = f32[256,512]{1,0:T(8,128)S(1)} fusion(bf16[24576,256]{1,0:T(8,128)(2,1)} %fusion.4, bf16[24576,512]{0,1:T(8,128)(2,1)} %constant_dynamic-update-slice_fusion.4), kind=kOutput, calls=%fused_computation.130 | convolution fusion | flops 6442450944 | bytes 38273024 | tf_op jit(solution)/shard_map/dot_general | solution.py:47
  789.0 14.5 %convolution_convert_fusion.1 = bf16[24576,256]{1,0:T(8,128)(2,1)} fusion(bf16[24576,512]{0,1:T(8,128)(2,1)} %constant_dynamic-update-slice_fusion.4, bf16[256,512]{1,0:T(8,128)(2,1)S(1)} %copy-done.30), kind=kOutput, calls=%fused_computation.11 | convolution fusion | flops 6448742400 | bytes 38010880 | tf_op jit(solution)/shard_map/dot_general | solution.py:53
  803.8 19.4 %fusion.5 = f32[600,256]{1,0:T(8,128)S(1)} fusion(bf16[24576,256]{1,0:T(8,128)(2,1)} %convolution_convert_fusion.1, f32[24576]{0:T(1024)S(1)} %copy-done.32, f32[600]{0:T(1024)S(1)} %copy-done.44, f32[24576]{0:T(1024)S(1)} %copy-done.34), kind=kOutput, calls=%fused_computation.12 | convolution fusion | flops 7638220800 | bytes 13396320 | tf_op jit(solution)/shard_map/dot_general | solution.py:47
  823.3 11.8 %fusion = f32[152,256]{1,0:T(8,128)S(1)} fusion(f32[600,256]{1,0:T(8,128)S(1)} %fusion.5), kind=kCustom, calls=%all-reduce-scatter | all-reduce-scatter fusion | flops 155649 | bytes 770560
  836.5 120.5 %scatter_custom_fusion = f32[576,256]{1,0:T(8,128)S(1)} fusion(s32[24576]{0:T(1024)S(1)} %reshape.239, bf16[24576,256]{1,0:T(8,128)(2,1)} %convolution_convert_fusion.1, f32[]{:T(128)} %constant.108.clone.1), kind=kCustom, calls=%fused_computation.15 | custom fusion | flops 12582912 | bytes 13172740 | tf_op jit(solution)/shard_map/scatter-add | solution.py:189
  970.8 22.6 %all-reduce.8 = (f32[64]{0:T(128)}, f32[64]{0:T(128)}, f32[64]{0:T(128)}) all-reduce(f32[64]{0:T(128)S(1)} %dynamic-slice.30, f32[64]{0:T(128)S(1)} %dynamic-slice.32, f32[64]{0:T(128)S(1)} %dynamic-slice.34), channel_id=1, replica_groups=mesh['space'=8,'wt'=4] {'space'}, use_global_device_ids=true, to_apply=%region_26.27 | all-reduce | flops 192 | bytes 1536 | tf_op jit(solution)/shard_map/psum | solution.py:215
  993.5 50.4 %all-reduce.14.cloned.1.call-done = (f32[150,256]{1,0:T(8,128)}, f32[64,256]{1,0:T(8,128)}, f32[64,256]{1,0:T(8,128)}, f32[64,256]{1,0:T(8,128)}, f32[64,256]{1,...) async-done(((f32[150,256]{1,0:T(8,128)}, f32[64,256]{1,0:T(8,128)}, f32[64,256]{1,0:T(8,128)}, f32[64,256]{1,0:T(8,128)}, ...) | async-done | bytes 1202192 | tf_op jit(solution)/shard_map/psum | solution.py:215
  (214 shorter events, 159.7 us)
Async XLA Ops:
  7.2 951.0 %reduce-scatter.16.cloned.1.call-start = ((), (), s32[]{:S(2)}) async-start(), calls=%async_computation.10 | async-start | bytes 327680 | tf_op jit(solution)/shard_map/reduce_scatter | solution.py:236
  8.1 78.5 %collective-permute-start = (bf16[96,256]{1,0:T(8,128)(2,1)S(1)}, bf16[96,256]{1,0:T(8,128)(2,1)S(1)}, u32[]{:S(2)}, u32[]{:S(2)}) collective-permute-start(bf16[96,256]{1,0:T(8,128)(2,1)S(1)} %get-tuple-element.84), channel_id=1, source_target_pairs={{0,1},{1,2},{2,3},{3,4},{4,5},{5,6},{6,7},{7,8},{8,9},{9,10},{10,1... | collective-permute-start | bytes 147464 | tf_op jit(solution)/shard_map/ppermute | solution.py:21
  10.4 76.1 %collective-permute-start.1 = (bf16[96,256]{1,0:T(8,128)(2,1)S(1)}, bf16[96,256]{1,0:T(8,128)(2,1)S(1)}, u32[]{:S(2)}, u32[]{:S(2)}) collective-permute-start(bf16[96,256]{1,0:T(8,128)(2,1)S(1)} %get-tuple-element.85), channel_id=1, source_target_pairs={{1,0},{2,1},{3,2},{4,3},{5,4},{6,5},{7,6},{8,7},{9,8},{10,9},{11,1... | collective-permute-start | bytes 147464 | tf_op jit(solution)/shard_map/ppermute | solution.py:22
  11.7 176.1 %copy-start.43 = (f32[600]{0:T(1024)}, f32[600]{0:T(1024)S(1)}, u32[]{:S(2)}) copy-start(f32[600]{0:T(1024)S(1)} %iota_multiply_fusion) | copy-start | bytes 7204
  31.0 156.9 %copy-start.31 = (f32[24576]{0:T(1024)}, f32[24576]{0:T(1024)S(1)}, u32[]{:S(2)}) copy-start(f32[24576]{0:T(1024)S(1)} %mul.195) | copy-start | bytes 294916
  49.3 138.5 %copy-start.33 = (f32[24576]{0:T(1024)}, f32[24576]{0:T(1024)S(1)}, u32[]{:S(2)}) copy-start(f32[24576]{0:T(1024)S(1)} %sub.41) | copy-start | bytes 294916
  507.2 451.0 %reduce-scatter.10.cloned.1.call-start = ((), (), s32[]{:S(2)}) async-start(), calls=%async_computation.7 | async-start | bytes 327680 | tf_op jit(solution)/shard_map/reduce_scatter | solution.py:233
  755.5 202.7 %reduce-scatter.14.cloned.1.call-start = ((), (), s32[]{:S(2)}) async-start(), calls=%async_computation.9 | async-start | bytes 327680 | tf_op jit(solution)/shard_map/reduce_scatter | solution.py:235
  781.9 176.3 %reduce-scatter.12.cloned.1.call-start = ((), (), s32[]{:S(2)}) async-start(), calls=%async_computation.8 | async-start | bytes 327680 | tf_op jit(solution)/shard_map/reduce_scatter | solution.py:234
  782.5 175.7 %reduce-scatter.20.cloned.1.call-start = ((), (), s32[]{:S(2)}) async-start(), calls=%async_computation.12 | async-start | bytes 1310720 | tf_op jit(solution)/shard_map/reduce_scatter | solution.py:238
  785.9 172.3 %reduce-scatter.18.cloned.1.call-start = ((), (), s32[]{:S(2)}) async-start(), calls=%async_computation.11 | async-start | bytes 1310720 | tf_op jit(solution)/shard_map/reduce_scatter | solution.py:237
  789.0 169.3 %reduce-scatter.22.cloned.1.call-start = ((), (), s32[]{:S(2)}) async-start(), calls=%async_computation.13 | async-start | bytes 1310720 | tf_op jit(solution)/shard_map/reduce_scatter | solution.py:239
  803.5 240.4 %all-reduce.14.cloned.1.call-start = ((), (), s32[]{:S(2)}) async-start(), calls=%async_computation.14 | async-start | bytes 2408448 | tf_op jit(solution)/shard_map/psum | solution.py:215
  823.2 135.1 %copy-start.5 = (bf16[384,256]{1,0:T(8,128)(2,1)S(1)}, bf16[384,256]{1,0:T(8,128)(2,1)}, u32[]{:S(2)}) copy-start(bf16[384,256]{1,0:T(8,128)(2,1)} %param.23) | copy-start | bytes 589828
  823.2 135.1 %copy-start.21 = (bf16[96,256]{1,0:T(8,128)(2,1)S(1)}, bf16[96,256]{1,0:T(8,128)(2,1)}, u32[]{:S(2)}) copy-start(bf16[96,256]{1,0:T(8,128)(2,1)} %copy-done.20) | copy-start | bytes 147460
  823.2 135.1 %copy-start.23 = (bf16[96,256]{1,0:T(8,128)(2,1)S(1)}, bf16[96,256]{1,0:T(8,128)(2,1)}, u32[]{:S(2)}) copy-start(bf16[96,256]{1,0:T(8,128)(2,1)} %copy-done.22) | copy-start | bytes 147460
  823.3 135.1 %copy-start.36 = (f32[576]{0:T(1024)S(1)}, f32[576]{0:T(1024)}, u32[]{:S(2)}) copy-start(f32[576]{0:T(1024)} %copy-done.35) | copy-start | bytes 6916
  823.3 135.1 %copy-start.39 = (f32[256]{0:T(256)S(1)}, f32[256]{0:T(256)}, u32[]{:S(2)}) copy-start(f32[256]{0:T(256)} %copy-done.38) | copy-start | bytes 3076
  823.3 138.9 %copy-start.3 = (f32[384,256]{1,0:T(8,128)S(1)}, f32[384,256]{1,0:T(8,128)}, u32[]{:S(2)}) copy-start(f32[384,256]{1,0:T(8,128)} %copy-done.2) | copy-start | bytes 1179652
  823.3 139.0 %copy-start.42 = (f32[256]{0:T(256)S(1)}, f32[256]{0:T(256)}, u32[]{:S(2)}) copy-start(f32[256]{0:T(256)} %get-tuple-element.54) | copy-start | bytes 3076
  823.3 139.0 %copy-start.45 = (f32[256]{0:T(256)S(1)}, f32[256]{0:T(256)}, u32[]{:S(2)}) copy-start(f32[256]{0:T(256)} %get-tuple-element.52) | copy-start | bytes 3076
  835.2 122.1 %collective-permute-start.4 = (f32[6,256]{1,0:T(8,128)S(1)}, f32[6,256]{1,0:T(8,128)S(1)}, u32[]{:S(2)}, u32[]{:S(2)}) collective-permute-start(f32[6,256]{1,0:T(8,128)S(1)} %slice.134), channel_id=1, source_target_pairs={{0,1},{1,2},{2,3},{4,5},{5,6},{6,7},{8,9},{9,10},{10,11},{12,13},{... | collective-permute-start | bytes 18440
  958.9 34.6 %collective-permute-start.2 = (bf16[96,256]{1,0:T(8,128)(2,1)S(1)}, bf16[96,256]{1,0:T(8,128)(2,1)S(1)}, u32[]{:S(2)}, u32[]{:S(2)}) collective-permute-start(bf16[96,256]{1,0:T(8,128)(2,1)S(1)} %slice.156), channel_id=1, source_target_pairs={{0,1},{1,2},{2,3},{3,4},{4,5},{5,6},{6,7},{7,8},{8,9},{9,10},{10,1... | collective-permute-start | bytes 147464 | tf_op jit(solution)/shard_map/ppermute | solution.py:30
  969.6 23.9 %collective-permute-start.3 = (f32[96,256]{1,0:T(8,128)S(1)}, f32[96,256]{1,0:T(8,128)S(1)}, u32[]{:S(2)}, u32[]{:S(2)}) collective-permute-start(f32[96,256]{1,0:T(8,128)S(1)} %slice.129), channel_id=1, source_target_pairs={{1,0},{2,1},{3,2},{4,3},{5,4},{6,5},{7,6},{8,7},{9,8},{10,9},{11,1... | collective-permute-start | bytes 294920 | tf_op jit(solution)/shard_map/ppermute | solution.py:30
  (35 other events, 1252.2 us)
Sparse Core Ops, SparseCore 0:
  507.3 20.5 reduce-scatter.15
  755.6 20.5 reduce-scatter.9
  782.0 20.4 reduce-scatter.13
  805.0 20.0 reduce-scatter.11
  827.4 24.8 reduce-scatter.19
  854.9 24.8 reduce-scatter.17
  882.3 24.8 reduce-scatter.21
  958.4 85.4 all-reduce.13
where the time goes:
time: 1070 us; the launch traced here: 1060 us
  matrix products  371 us (35%)
  local copies, waits for them, and re-layouts  338 us (32%)
  other arithmetic  171 us (16%)
  blocking collectives  106 us (10%)
  waiting for transfers between devices  51.1 us (5%)
  between operations  17.3 us (2%)
    scatter-add x1, other arithmetic, local(): jax.ops.segment_sum(grad_edge.astype(jnp.float32), flat_rows, num_segment...  120 us
    gather x1, local copies, waits for them, and re-layouts, local(): lookup[flat_rows].astype(jnp.float32) + matmul(basis_rows, w_rbf)  96.7 us
    dot_general x1, matrix products, local(): jnp.einsum('ahd,akhd->ahk', query_heads, key_heads, preferred_element_typ...  76.6 us
    dot_general x1, matrix products, local(): jnp.einsum('ahd,akhd->ahk', grad_attended, value_heads, preferred_element...  72.4 us
    dot_general x1, matrix products, local(): jnp.einsum('ahk,akhd->ahd', soft_low, value_heads, preferred_element_type...  57.4 us
    dot_general x1, matrix products, local(): jnp.einsum('ahk,akhd->ahd', grad_scores, key_heads.astype(jnp.float32))  55.9 us
    psum x1, waiting for transfers between devices, local(): lax.psum((partials[0], partials[1], partials[2], partials[3], partials[4]...  50.4 us
    dot_general x6, matrix products, matmul(): return jnp.dot(left, right, preferred_element_type=jnp.float32)  50.3 us
  transfers between devices with their start and end apart: 13, of which 1 were waited for; matrix products, arithmetic and copies ran while one was open for 43% of the time, Pallas kernels for 0%

commit v1 on v0

v1 whole, which is shorter than its diff:
```python
import functools
import math

import jax
import jax.numpy as jnp
from jax import lax
from jax.experimental import pallas as pl
from jax.experimental.pallas import tpu as pltpu
from jax.sharding import PartitionSpec as P

HEADS = 8
HALO = 96
EPSILON = 1e-06
CUTOFF = 6.0

BLOCK = 64
PAIRS = BLOCK // 2
LANES = 128
TILE = 256
GROUP = 1024

BF16 = jnp.bfloat16
F32 = jnp.float32


def nn(a, b):
    return lax.dot_general(a, b, (((1,), (0,)), ((), ())), preferred_element_type=F32)


def nt(a, b):
    return lax.dot_general(a, b, (((1,), (1,)), ((), ())), preferred_element_type=F32)


def tn(a, b):
    return lax.dot_general(a, b, (((0,), (0,)), ((), ())), preferred_element_type=F32)


def round_up(value, step):
    return -(-value // step) * step


def rms(value):
    inverse = lax.rsqrt(jnp.mean(value * value, -1, keepdims=True) + EPSILON)
    return value * inverse, inverse


def norm_back(grad_normed, normed_rows, inverse):
    return inverse * (
        grad_normed - normed_rows * jnp.mean(grad_normed * normed_rows, -1, keepdims=True)
    )


def pair_rows(block):
    return jnp.concatenate([block[:PAIRS], block[PAIRS:]], axis=1)


def head_of_lane(width):
    return lax.broadcasted_iota(jnp.int32, (1, width), 1) // (width // HEADS)


def spread_heads(rows, out_ref):
    atoms, width = rows.shape
    heads = head_of_lane(width)
    for start in range(0, atoms, PAIRS):
        block, side = start // BLOCK, (start % BLOCK) // PAIRS
        part = rows[start : start + PAIRS]
        for head in range(HEADS):
            place = block * BLOCK * HEADS + side * HEADS + head
            kept = jnp.where(heads == head, part, 0.0)
            for half in range(width // LANES):
                out_ref[half, pl.ds(place, PAIRS, stride=2 * HEADS), :] = kept[
                    :, half * LANES : (half + 1) * LANES
                ]


def wide(ref, rows=slice(None)):
    return jnp.concatenate([ref[half, rows, :] for half in range(ref.shape[0])], axis=1)


def gather_heads(rows_ref, weight, atoms):
    width = weight.shape[1]
    heads = head_of_lane(width)
    total = None
    for head in range(HEADS):
        parts = []
        for start in range(0, atoms, PAIRS):
            block, side = start // BLOCK, (start % BLOCK) // PAIRS
            place = block * BLOCK * HEADS + side * HEADS + head
            parts.append(wide(rows_ref, pl.ds(place, PAIRS, stride=2 * HEADS)))
        left = jnp.concatenate(parts, axis=0).astype(BF16)
        right = jnp.where(heads == head, weight, jnp.zeros_like(weight))
        term = nn(left, right)
        total = term if total is None else total + term
    return total


def half_sums(value, low_half, op, neutral):
    low = op(jnp.where(low_half, value, neutral), axis=1, keepdims=True)
    high = op(jnp.where(low_half, neutral, value), axis=1, keepdims=True)
    return jnp.where(low_half, low, high)


def write_onehot(neighbours_ref, first_row, onehot_ref):
    rows = onehot_ref.shape[0]
    relative = pair_rows(neighbours_ref[...]) - first_row
    relative = relative.astype(F32)
    places = lax.broadcasted_iota(jnp.int32, (rows, LANES), 0).astype(F32)
    for pair in range(PAIRS):
        hit = places == relative[pair : pair + 1, :]
        onehot_ref[:, pair * LANES : (pair + 1) * LANES] = jnp.where(hit, 1.0, 0.0).astype(BF16)


def diagonal(tile, low_half):
    first = jnp.where(low_half, tile[0:8, :LANES], tile[8:16, :LANES])
    second = jnp.where(low_half, tile[16:24, LANES:], tile[24:32, LANES:])
    return first, second


def block_rows(value, low_half):
    zero = jnp.zeros_like(value)
    return jnp.concatenate(
        [jnp.where(low_half, value, zero), jnp.where(low_half, zero, value)], axis=0
    ).astype(BF16)


def basis_kernel(shard, padded, spread, step, dist_ref, out_ref, scaled_ref, env_ref):
    dist = pair_rows(dist_ref[...])
    factor = math.sqrt(0.5 / math.log(2.0)) / spread
    scaled_ref[...] = dist * factor
    env_ref[...] = 0.5 * (jnp.cos(jnp.pi * dist / CUTOFF) + 1.0)
    rows = out_ref.shape[0]
    iota = lax.broadcasted_iota(jnp.int32, (16, LANES), 0).astype(F32) * (step * factor)

    @pl.loop(0, PAIRS)
    def _(pair):
        base = scaled_ref[pl.ds(pair, 1), :] - iota
        envelope = jnp.broadcast_to(env_ref[pl.ds(pair, 1), :], (16, LANES))
        lanes = pl.ds(pl.multiple_of(pair * LANES, LANES), LANES)
        for row in range(0, rows, 16):
            center = (row // padded) * shard + row % padded
            delta = base - (center * step * factor)
            value = jnp.exp2(-(delta * delta)) * envelope
            out_ref[row : row + 16, lanes] = value.astype(BF16)


def basis_call(distances, shard, padded, members, basis_count):
    atoms, slots = distances.shape
    blocks = atoms // BLOCK
    rows = members * padded
    edges = BLOCK * slots
    return pl.pallas_call(
        functools.partial(
            basis_kernel, shard, padded, 2.0 * CUTOFF / basis_count, CUTOFF / basis_count
        ),
        grid=(blocks,),
        out_shape=jax.ShapeDtypeStruct((blocks, rows, edges), BF16),
        in_specs=[pl.BlockSpec((BLOCK, slots), lambda b: (b, 0))],
        out_specs=pl.BlockSpec((None, rows, edges), lambda b: (b, 0, 0)),
        scratch_shapes=[pltpu.VMEM((PAIRS, LANES), F32), pltpu.VMEM((PAIRS, LANES), F32)],
        compiler_params=pltpu.CompilerParams(vmem_limit_bytes=40 * 2**20),
        cost_estimate=pl.CostEstimate(
            flops=8 * atoms * slots * rows,
            bytes_accessed=2 * atoms * slots * rows,
            transcendentals=atoms * slots * rows,
        ),
        name="radial_basis",
    )(distances)


def place_shards(index_ref, packs, row, count, stride, out_ref):
    me = index_ref[0]
    for offset, pack in enumerate(packs):
        owner = lax.bitwise_xor(me, offset)
        start = pl.multiple_of(owner * stride, 16)
        out_ref[pl.ds(start, count), :] = pack[row : row + count, :]


def vector_of(packs, row):
    total = packs[0][row : row + 1, :].astype(F32)
    for pack in packs[1:]:
        total = total + pack[row : row + 1, :].astype(F32)
    return total


def forward_kernel(
    padded,
    quarter,
    scale,
    index_ref,
    counts_ref,
    features_ref,
    before_ref,
    after_ref,
    pack0,
    pack1,
    pack2,
    pack3,
    neighbours_ref,
    basis_ref,
    edge_ref,
    soft_ref,
    attended_ref,
    pooled_ref,
    lookup_ref,
    query_ref,
    kvq_ref,
    weight_t,
    assembled,
    spread,
    keyed,
    onehot,
    bands,
    pooled,
):
    step = pl.program_id(0)
    packs = (pack0, pack1, pack2, pack3)
    atoms, width = features_ref.shape
    low_half = lax.broadcasted_iota(jnp.int32, (1, LANES), 1) < LANES // 2
    lane = lax.broadcasted_iota(jnp.int32, (1, LANES), 1)
    edges = basis_ref.shape[1]

    @pl.when(step == 0)
    def _():
        place_shards(index_ref, packs, 0, padded, padded, assembled)
        weight_t[...] = assembled[...].astype(F32).T.astype(BF16)
        for which in range(3):
            place_shards(
                index_ref, packs, padded + which * quarter, quarter, quarter, kvq_ref.at[which]
            )
        gain = vector_of(packs, padded + 3 * quarter)
        for ref, start in ((before_ref, 0), (features_ref, HALO), (after_ref, HALO + atoms)):
            normed, _ = rms(ref[...].astype(F32))
            lookup_ref[start : start + ref.shape[0], :] = (normed * gain).astype(BF16)
        query = nn(lookup_ref[HALO : HALO + atoms, :], kvq_ref[0]).astype(BF16)
        query_ref[...] = query
        spread_heads(query.astype(F32), spread)
        keyed[...] = (nt(wide(spread).astype(BF16), kvq_ref[1]) * scale).astype(BF16)
        bands[...] = jnp.zeros_like(bands)

    first_row = step * BLOCK
    write_onehot(neighbours_ref, first_row, onehot)
    window = lookup_ref[pl.ds(pl.multiple_of(first_row, BLOCK), onehot.shape[0]), :]
    window_t = window.astype(F32).T.astype(BF16)
    for group in range(edges // GROUP):
        part = slice(group * GROUP, (group + 1) * GROUP)
        edge_ref[:, part] = (
            nn(weight_t[...], basis_ref[:, part]) + nn(window_t, onehot[:, part])
        ).astype(BF16)
    rows = BLOCK * HEADS
    base = pl.multiple_of(step * rows, rows)
    for tile in range(edges // TILE):
        part = slice(tile * TILE, (tile + 1) * TILE)
        left = keyed[pl.ds(base + tile * 32, 32), :]
        both = diagonal(nn(left, edge_ref[:, part]), low_half)
        for side, score in enumerate(both):
            pair = 2 * tile + side
            low_count = counts_ref[step * BLOCK + pair]
            high_count = counts_ref[step * BLOCK + PAIRS + pair]
            usable = lane < jnp.where(low_half, low_count, high_count + LANES // 2)
            score = jnp.where(usable, score, -1e30)
            top = half_sums(score, low_half, jnp.max, -jnp.inf)
            power = jnp.exp(score - top)
            soft = power / half_sums(power, low_half, jnp.sum, 0.0)
            soft_ref[:, pair * LANES : (pair + 1) * LANES] = soft
            bands[tile, side * 16 : side * 16 + 16, side * LANES : (side + 1) * LANES] = (
                block_rows(soft, low_half)
            )
        result = nt(bands[tile], edge_ref[:, part])
        for half in range(width // LANES):
            pooled[half, pl.ds(base + tile * 32, 32), :] = result[
                :, half * LANES : (half + 1) * LANES
            ]

    @pl.when(step == pl.num_programs(0) - 1)
    def _():
        attended_ref[...] = gather_heads(pooled, kvq_ref[2], atoms).astype(BF16)
        pooled_ref[...] = wide(pooled).astype(BF16)


def forward_call(index, counts, features, before, after, packs, neighbours, basis, padded, quarter):
    atoms, width = features.shape
    slots = neighbours.shape[1]
    blocks, rows, edges = basis.shape
    table = atoms + 2 * HALO
    full = lambda shape: pl.BlockSpec(shape, lambda b: (0,) * len(shape))
    head_rows = atoms * HEADS
    window = BLOCK + 2 * HALO
    return pl.pallas_call(
        functools.partial(forward_kernel, padded, quarter, (width // HEADS) ** -0.5),
        grid=(blocks,),
        out_shape=(
            jax.ShapeDtypeStruct((blocks, width, edges), BF16),
            jax.ShapeDtypeStruct((blocks, HEADS, edges), F32),
            jax.ShapeDtypeStruct((atoms, width), BF16),
            jax.ShapeDtypeStruct((head_rows, width), BF16),
            jax.ShapeDtypeStruct((table, width), BF16),
            jax.ShapeDtypeStruct((atoms, width), BF16),
            jax.ShapeDtypeStruct((3, width, width), BF16),
        ),
        in_specs=[
            pl.BlockSpec(memory_space=pltpu.SMEM),
            pl.BlockSpec(memory_space=pltpu.SMEM),
            full((atoms, width)),
            full((HALO, width)),
            full((HALO, width)),
        ]
        + [full(pack.shape) for pack in packs]
        + [
            pl.BlockSpec((BLOCK, slots), lambda b: (b, 0)),
            pl.BlockSpec((None, rows, edges), lambda b: (b, 0, 0)),
        ],
        out_specs=(
            pl.BlockSpec((None, width, edges), lambda b: (b, 0, 0)),
            pl.BlockSpec((None, HEADS, edges), lambda b: (b, 0, 0)),
            full((atoms, width)),
            full((head_rows, width)),
            full((table, width)),
            full((atoms, width)),
            full((3, width, width)),
        ),
        scratch_shapes=[
            pltpu.VMEM((width, rows), BF16),
            pltpu.VMEM((rows, width), BF16),
            pltpu.VMEM((width // LANES, head_rows, LANES), F32),
            pltpu.VMEM((head_rows, width), BF16),
            pltpu.VMEM((window, edges), BF16),
            pltpu.VMEM((edges // TILE, 32, TILE), BF16),
            pltpu.VMEM((width // LANES, head_rows, LANES), F32),
        ],
        compiler_params=pltpu.CompilerParams(vmem_limit_bytes=58 * 2**20),
        cost_estimate=pl.CostEstimate(
            flops=2 * atoms * slots * width * (rows + window + 64),
            bytes_accessed=2 * atoms * slots * (rows + width),
            transcendentals=atoms * slots * HEADS,
        ),
        name="attention_forward",
    )(index, counts, features, before, after, *packs, neighbours, basis)


def ffn_kernel(
    quarter,
    small_row,
    index_ref,
    features_ref,
    attended_ref,
    grad_out_ref,
    grad_energy_ref,
    small0,
    small1,
    small2,
    small3,
    pack0,
    pack1,
    pack2,
    pack3,
    out_ref,
    energy_ref,
    grad_residual_ref,
    grad_attended_ref,
    grads_ref,
    sums_ref,
    w_gate,
    w_up,
    w_down,
    w_out,
):
    small = (small0, small1, small2, small3)
    packs = (pack0, pack1, pack2, pack3)
    atoms, width = features_ref.shape
    parts = w_gate.shape[1] // width
    down_rows = w_down.shape[0] // 4
    me = index_ref[0]
    for offset, pack in enumerate(packs):
        owner = lax.bitwise_xor(me, offset)
        rows = pl.ds(pl.multiple_of(owner * quarter, 16), quarter)
        for part in range(parts):
            lanes = slice(part * width, (part + 1) * width)
            w_gate[rows, lanes] = pack[part * quarter : (part + 1) * quarter, :]
            w_up[rows, lanes] = pack[(parts + part) * quarter : (parts + part + 1) * quarter, :]
        start = 2 * parts * quarter
        w_down[pl.ds(pl.multiple_of(owner * down_rows, 16), down_rows), :] = pack[
            start : start + down_rows, :
        ]
        w_out[rows, :] = pack[start + down_rows : start + down_rows + quarter, :]
    gain = vector_of(small, small_row + 1)
    readout = vector_of(small, small_row + 2)

    attended = attended_ref[...]
    residual = features_ref[...].astype(F32) + nn(attended, w_out[...])
    normed, inverse = rms(residual)
    hidden = (normed * gain).astype(BF16)
    gate = nn(hidden, w_gate[...])
    up = nn(hidden, w_up[...])
    sigmoid = jax.nn.sigmoid(gate)
    silu = gate * sigmoid
    activated = (silu * up).astype(BF16)
    outputs = residual + nn(activated, w_down[...])
    out_ref[...] = outputs
    energy_ref[...] = jnp.sum(outputs * readout, -1, keepdims=True)
    grad_energy = grad_energy_ref[...]
    grad_act = grad_out_ref[...].astype(F32) + grad_energy * readout
    grad_branch = grad_act.astype(BF16)
    grad_down = tn(activated, grad_branch)
    grad_activated = nt(grad_branch, w_down[...])
    grad_gate = (grad_activated * up * sigmoid * (1.0 + gate * (1.0 - sigmoid))).astype(BF16)
    grad_up = (grad_activated * silu).astype(BF16)
    grad_gate_w = tn(hidden, grad_gate)
    grad_up_w = tn(hidden, grad_up)
    grad_hidden = (nt(grad_gate, w_gate[...]) + nt(grad_up, w_up[...])).astype(BF16).astype(F32)
    grad_residual = grad_act + norm_back(grad_hidden * gain, normed, inverse)
    grad_residual_ref[...] = grad_residual
    grad_proj = grad_residual.astype(BF16)
    grad_attended_ref[...] = nt(grad_proj, w_out[...]).astype(BF16)
    grad_out_w = tn(attended, grad_proj)
    for owner in range(4):
        rows = slice(owner * quarter, (owner + 1) * quarter)
        for part in range(parts):
            lanes = slice(part * width, (part + 1) * width)
            grads_ref[owner, part * quarter : (part + 1) * quarter, :] = grad_gate_w[
                rows, lanes
            ].astype(BF16)
            grads_ref[owner, (parts + part) * quarter : (parts + part + 1) * quarter, :] = (
                grad_up_w[rows, lanes].astype(BF16)
            )
        start = 2 * parts * quarter
        grads_ref[owner, start : start + down_rows, :] = grad_down[
            owner * down_rows : (owner + 1) * down_rows, :
        ].astype(BF16)
        grads_ref[owner, start + down_rows : start + down_rows + quarter, :] = grad_out_w[
            rows, :
        ].astype(BF16)
    sums_ref[...] = jnp.zeros_like(sums_ref)
    sums_ref[1:2, :] = jnp.sum(grad_hidden * normed, 0, keepdims=True)
    sums_ref[2:3, :] = jnp.sum(grad_energy * outputs, 0, keepdims=True)


def ffn_call(index, features, attended, grad_out, grad_energy, small, packs, hidden, quarter, row):
    atoms, width = features.shape
    vmem = pl.BlockSpec(memory_space=pltpu.VMEM)
    return pl.pallas_call(
        functools.partial(ffn_kernel, quarter, row),
        out_shape=(
            jax.ShapeDtypeStruct((atoms, width), F32),
            jax.ShapeDtypeStruct((atoms, 1), F32),
            jax.ShapeDtypeStruct((atoms, width), F32),
            jax.ShapeDtypeStruct((atoms, width), BF16),
            jax.ShapeDtypeStruct((4,) + packs[0].shape, BF16),
            jax.ShapeDtypeStruct((8, width), F32),
        ),
        in_specs=[pl.BlockSpec(memory_space=pltpu.SMEM)] + [vmem] * 12,
        out_specs=(vmem,) * 6,
        scratch_shapes=[
            pltpu.VMEM((width, hidden), BF16),
            pltpu.VMEM((width, hidden), BF16),
            pltpu.VMEM((hidden, width), BF16),
            pltpu.VMEM((width, width), BF16),
        ],
        compiler_params=pltpu.CompilerParams(vmem_limit_bytes=58 * 2**20),
        cost_estimate=pl.CostEstimate(
            flops=18 * atoms * width * hidden, bytes_accessed=2**23, transcendentals=atoms * hidden
        ),
        name="feed_forward",
    )(index, features, attended, grad_out, grad_energy, *small, *packs)


def backward_kernel(
    padded,
    quarter,
    scale,
    gain_row,
    features_ref,
    before_ref,
    after_ref,
    small0,
    small1,
    small2,
    small3,
    lookup_ref,
    query_ref,
    kvq_ref,
    pooled_ref,
    grad_attended_ref,
    grad_residual_ref,
    sums_ref,
    neighbours_ref,
    basis_ref,
    edge_ref,
    soft_ref,
    grads_ref,
    grad_own_ref,
    grad_halo_ref,
    spread_q,
    spread_g,
    valued,
    mixed_t,
    onehot,
    bands,
    grad_edge,
    pooled,
    grad_rbf,
    grad_lookup,
):
    step = pl.program_id(0)
    small = (small0, small1, small2, small3)
    atoms, width = features_ref.shape
    low_half = lax.broadcasted_iota(jnp.int32, (1, LANES), 1) < LANES // 2
    edges = basis_ref.shape[1]
    group_rows = GROUP // 64 * HEADS
    groups = edges // GROUP

    @pl.when(step == 0)
    def _():
        spread_heads(query_ref[...].astype(F32), pooled)
        spread_q[...] = wide(pooled).astype(BF16)
        spread_heads(grad_attended_ref[...].astype(F32), pooled)
        spread_g[...] = wide(pooled).astype(BF16)
        valued[...] = nt(spread_g[...], kvq_ref[2]).astype(BF16)
        for group in range(mixed_t.shape[0]):
            rows = slice(group * group_rows, (group + 1) * group_rows)
            mixed_t[group, :, :group_rows] = (nt(kvq_ref[1], spread_q[rows, :]) * scale).astype(
                BF16
            )
            mixed_t[group, :, group_rows:] = nt(kvq_ref[2], spread_g[rows, :]).astype(BF16)
        bands[...] = jnp.zeros_like(bands)
        grad_rbf[...] = jnp.zeros_like(grad_rbf)
        grad_lookup[...] = jnp.zeros_like(grad_lookup)

    first_row = step * BLOCK
    write_onehot(neighbours_ref, first_row, onehot)
    rows = BLOCK * HEADS
    base = pl.multiple_of(step * rows, rows)
    for tile in range(edges // TILE):
        part = slice(tile * TILE, (tile + 1) * TILE)
        group, place = tile * TILE // GROUP, tile * TILE % GROUP
        left = valued[pl.ds(base + tile * 32, 32), :]
        both = diagonal(nn(left, edge_ref[:, part]), low_half)
        for side, grad_soft in enumerate(both):
            pair = 2 * tile + side
            soft = soft_ref[:, pair * LANES : (pair + 1) * LANES]
            mean = half_sums(soft * grad_soft, low_half, jnp.sum, 0.0)
            grad_score = soft * (grad_soft - mean)
            lanes = slice(place + side * LANES, place + (side + 1) * LANES)
            row = place // TILE * 32 + side * 16
            bands[group, row : row + 16, lanes] = block_rows(grad_score, low_half)
            bands[group, group_rows + row : group_rows + row + 16, lanes] = block_rows(
                soft, low_half
            )
        row = place // TILE * 32
        result = nt(bands[group, row : row + 32, place : place + TILE], edge_ref[:, part])
        for half in range(width // LANES):
            pooled[half, pl.ds(base + tile * 32, 32), :] = result[
                :, half * LANES : (half + 1) * LANES
            ]
    for group in range(groups):
        part = slice(group * GROUP, (group + 1) * GROUP)
        grad_edge[:, part] = nn(mixed_t[step * groups + group], bands[group]).astype(BF16)
    grad_rbf[...] += nt(basis_ref[...], grad_edge[...])
    place = pl.ds(pl.multiple_of(first_row, BLOCK), onehot.shape[0])
    grad_lookup[place, :] += nt(onehot[...], grad_edge[...])

    @pl.when(step == pl.num_programs(0) - 1)
    def _():
        own = slice(HALO, HALO + atoms)
        grad_query = (gather_heads(pooled, kvq_ref[1], atoms) * scale).astype(BF16)
        grad_key_w = tn(wide(pooled).astype(BF16), spread_q[...]) * scale
        grad_value_w = tn(pooled_ref[...], spread_g[...])
        grad_query_w = tn(lookup_ref[own, :], grad_query)
        grad_lookup[own, :] += nt(grad_query, kvq_ref[0])
        gain = vector_of(small, gain_row)
        grad_gain = jnp.zeros((1, width), F32)
        places = (
            (before_ref, 0, grad_halo_ref.at[0]),
            (features_ref, HALO, grad_own_ref),
            (after_ref, HALO + atoms, grad_halo_ref.at[1]),
        )
        for ref, start, out in places:
            normed, inverse = rms(ref[...].astype(F32))
            grad = grad_lookup[start : start + ref.shape[0], :]
            grad_gain = grad_gain + jnp.sum(grad * normed, 0, keepdims=True)
            back = norm_back(grad * gain, normed, inverse)
            if start == HALO:
                back = back + grad_residual_ref[...]
            out[...] = back.astype(out.dtype)
        vectors = jnp.concatenate([grad_gain, sums_ref[1:8, :], jnp.zeros((8, width), F32)], 0)
        for owner in range(4):
            rows = slice(owner * quarter, (owner + 1) * quarter)
            grads_ref[owner, :padded, :] = grad_rbf[
                owner * padded : (owner + 1) * padded, :
            ].astype(BF16)
            for which, grad in enumerate((grad_query_w, grad_key_w, grad_value_w)):
                start = padded + which * quarter
                grads_ref[owner, start : start + quarter, :] = grad[rows, :].astype(BF16)
            start = padded + 3 * quarter
            grads_ref[owner, start : start + 16, :] = vectors.astype(BF16)


def backward_call(
    features,
    before,
    after,
    small,
    lookup,
    query,
    kvq,
    pooled,
    grad_attended,
    grad_residual,
    sums,
    neighbours,
    basis,
    edge,
    soft,
    padded,
    quarter,
):
    atoms, width = features.shape
    slots = neighbours.shape[1]
    blocks, rows, edges = basis.shape
    table = atoms + 2 * HALO
    head_rows = atoms * HEADS
    window = BLOCK + 2 * HALO
    group_rows = GROUP // slots * HEADS
    full = lambda shape: pl.BlockSpec(shape, lambda b: (0,) * len(shape))
    whole = (
        (features, before, after)
        + tuple(small)
        + (lookup, query, kvq, pooled, grad_attended, grad_residual, sums)
    )
    return pl.pallas_call(
        functools.partial(
            backward_kernel, padded, quarter, (width // HEADS) ** -0.5, padded + 3 * quarter
        ),
        grid=(blocks,),
        out_shape=(
            jax.ShapeDtypeStruct((4,) + small[0].shape, BF16),
            jax.ShapeDtypeStruct((atoms, width), F32),
            jax.ShapeDtypeStruct((2, HALO, width), BF16),
        ),
        in_specs=[full(value.shape) for value in whole]
        + [
            pl.BlockSpec((BLOCK, slots), lambda b: (b, 0)),
            pl.BlockSpec((None, rows, edges), lambda b: (b, 0, 0)),
            pl.BlockSpec((None, width, edges), lambda b: (b, 0, 0)),
            pl.BlockSpec((None, HEADS, edges), lambda b: (b, 0, 0)),
        ],
        out_specs=(
            full((4,) + small[0].shape),
            full((atoms, width)),
            full((2, HALO, width)),
        ),
        scratch_shapes=[
            pltpu.VMEM((head_rows, width), BF16),
            pltpu.VMEM((head_rows, width), BF16),
            pltpu.VMEM((head_rows, width), BF16),
            pltpu.VMEM((head_rows // group_rows, width, 2 * group_rows), BF16),
            pltpu.VMEM((window, edges), BF16),
            pltpu.VMEM((edges // GROUP, 2 * group_rows, GROUP), BF16),
            pltpu.VMEM((width, edges), BF16),
            pltpu.VMEM((width // LANES, head_rows, LANES), F32),
            pltpu.VMEM((rows, width), F32),
            pltpu.VMEM((table, width), F32),
        ],
        compiler_params=pltpu.CompilerParams(vmem_limit_bytes=60 * 2**20),
        cost_estimate=pl.CostEstimate(
            flops=2 * atoms * slots * width * (rows + window + 384),
            bytes_accessed=2 * atoms * slots * (rows + width),
            transcendentals=0,
        ),
        name="attention_backward",
    )(*whole, neighbours, basis, edge, soft)


def exchange(value, axis, offset):
    size = lax.axis_size(axis)
    return lax.ppermute(value, axis, [(i, i ^ offset) for i in range(size)])


def shifted(value, by):
    axes = ("space", "wt")
    size = lax.axis_size(axes)
    pairs = [(i, i + by) for i in range(size) if 0 <= i + by < size]
    return lax.ppermute(value, axes, pairs)


def gathered(value):
    return [value] + [exchange(value, "wt", offset) for offset in range(1, lax.axis_size("wt"))]


def reduced(partials):
    me = lax.axis_index("wt")
    take = lambda owner: lax.dynamic_index_in_dim(partials, owner, 0, keepdims=False)
    total = take(me).astype(F32)
    for offset in range(1, lax.axis_size("wt")):
        total = total + exchange(take(me ^ offset), "wt", offset).astype(F32)
    offset = 1
    while offset < lax.axis_size("space"):
        sent = total.astype(BF16)
        total = sent.astype(F32) + exchange(sent, "space", offset).astype(F32)
        offset *= 2
    return total


def local(
    features,
    distances,
    neighbours,
    counts,
    rbf_weight,
    query_weight,
    key_weight,
    value_weight,
    out_weight,
    gate_weight,
    up_weight,
    down_weight,
    attn_gain,
    ffn_gain,
    readout,
    grad_out,
    grad_energy,
):
    members = lax.axis_size("wt")
    atoms, width = features.shape
    shard = rbf_weight.shape[0]
    padded = round_up(shard, 16)
    quarter = query_weight.shape[0]
    hidden = gate_weight.shape[1]
    parts = hidden // width
    me = lax.axis_index("wt").astype(jnp.int32)
    index = me[None]

    vectors = jnp.zeros((16, width), BF16)
    vectors = lax.dynamic_update_slice(
        vectors, jnp.stack([attn_gain, ffn_gain, readout]), (0, me * quarter)
    )
    small = jnp.concatenate(
        [
            jnp.pad(rbf_weight, ((0, padded - shard), (0, 0))),
            query_weight,
            key_weight,
            value_weight,
            vectors,
        ],
        0,
    )
    columns = lambda value: [value[:, part * width : (part + 1) * width] for part in range(parts)]
    large = jnp.concatenate(
        columns(gate_weight) + columns(up_weight) + [down_weight, out_weight], 0
    )
    before = shifted(features[atoms - HALO :], 1)
    after = shifted(features[:HALO], -1)
    small_all = gathered(small)
    basis = basis_call(distances, shard, padded, members, members * shard)
    large_all = gathered(large)

    edge, soft, attended, pooled, lookup, query, kvq = forward_call(
        index, counts, features, before, after, small_all, neighbours, basis, padded, quarter
    )
    gain_row = padded + 3 * quarter
    outputs, energy, grad_residual, grad_attended, large_grads, sums = ffn_call(
        index,
        features,
        attended,
        grad_out,
        grad_energy[:, None],
        small_all,
        large_all,
        hidden,
        quarter,
        gain_row,
    )
    small_grads, grad_own, grad_halo = backward_call(
        features,
        before,
        after,
        small_all,
        lookup,
        query,
        kvq,
        pooled,
        grad_attended,
        grad_residual,
        sums,
        neighbours,
        basis,
        edge,
        soft,
        padded,
        quarter,
    )
    from_upper = shifted(grad_halo[0], -1).astype(F32)
    from_lower = shifted(grad_halo[1], 1).astype(F32)
    grad_features = grad_own.at[:HALO].add(from_lower)
    grad_features = grad_features.at[atoms - HALO :].add(from_upper)
    large_sum = reduced(large_grads)
    small_sum = reduced(small_grads)
    start = 2 * parts * quarter
    down_rows = down_weight.shape[0]
    columns_of = lambda first: jnp.concatenate(
        [large_sum[first + part * quarter : first + (part + 1) * quarter] for part in range(parts)],
        1,
    )
    piece = lambda which: small_sum[padded + which * quarter : padded + (which + 1) * quarter]
    vector = lambda row: lax.dynamic_slice(small_sum[gain_row + row], (me * quarter,), (quarter,))
    return (
        outputs,
        energy[:, 0],
        grad_features,
        small_sum[:shard],
        piece(0),
        piece(1),
        piece(2),
        large_sum[start + down_rows : start + down_rows + quarter],
        columns_of(0),
        columns_of(parts * quarter),
        large_sum[start : start + down_rows],
        vector(0),
        vector(1),
        vector(2),
    )


def solution(mesh):
    rows = P(("space", "wt"), None)
    line = P(("space", "wt"))
    in_specs = (rows, rows, rows, line) + (P("wt", None),) * 8 + (P("wt"),) * 3 + (rows, line)
    out_specs = (rows, line, rows) + (P("wt", None),) * 8 + (P("wt"),) * 3
    return jax.shard_map(local, mesh=mesh, in_specs=in_specs, out_specs=out_specs, check_vma=False)
```

time: 1070 us -> 220 us (0.21)
  matrix products: 371 us -> 0 us
  local copies, waits for them, and re-layouts: 338 us -> 23.3 us
  other arithmetic: 171 us -> 8.24 us
  Pallas kernels: 0 us -> 106 us
  blocking collectives: 106 us -> 0 us
  starting transfers between devices: 10 us -> 43.1 us
  between operations: 17.3 us -> 0.94 us
  waiting for transfers between devices: 51.1 us -> 37.3 us
    dot_general x21 -> x0, matrix products: 371 us -> none  [the longest x1 76.6 us: local(): jnp.einsum('ahd,akhd->ahk', query_heads, key_heads, preferred_element_typ...]
    reshape x8 -> x0, local copies, waits for them, and re-layouts: 139 us -> none  [the longest x1 34.4 us: local(): keyvals[:, :model_width].reshape(atom_count, slot_count, HEADS, head_size)]
    scatter-add x3 -> x2, other arithmetic: 121 us -> 3.09 us  [the longest x1 1.54 us: local(): grad_features = grad_features.at[atoms - HALO:].add(from_upper)]
    pallas_call x0 -> x4, Pallas kernels: none -> 106 us  [the longest x1 41.8 us: backward_call(): pl.pallas_call(functools.partial(backward_kernel, padded, quarter, (width...]
    gather x1 -> x0, local copies, waits for them, and re-layouts: 96.7 us -> none  [local(): lookup[flat_rows].astype(jnp.float32) + matmul(basis_rows, w_rbf)]
    all_gather x8 -> x0, blocking collectives: 53.9 us -> none  [the longest x1 8.17 us: local(): lax.all_gather(down_weight, 'wt', axis=0, tiled=True)]
    psum x1 -> x0, waiting for transfers between devices: 50.4 us -> none  [local(): lax.psum((partials[0], partials[1], partials[2], partials[3], partials[4]...]
    slice x8 -> x6, local copies, waits for them, and re-layouts: 53.4 us -> 3.59 us  [the longest x1 0.83 us: local(): after = shifted(features[:HALO], -1)]
  transfers between devices with their start and end apart: 13 -> 22, of which waited for: 1 -> 8; matrix products, arithmetic and copies ran while one was open for 43% -> 10% of each run, Pallas kernels for 0% -> 26%
where the time goes in v1:
time: 220 us; the launch traced here: 219 us
  Pallas kernels  106 us (48%)
  starting transfers between devices  43.1 us (20%)
  waiting for transfers between devices  37.3 us (17%)
  local copies, waits for them, and re-layouts  23.3 us (11%)
  other arithmetic  8.24 us (4%)
    pallas_call x1, Pallas kernels, backward_call(): pl.pallas_call(functools.partial(backward_kernel, padded, quarter, (width...  41.8 us
    pallas_call x1, Pallas kernels, forward_call(): pl.pallas_call(functools.partial(forward_kernel, padded, quarter, (width...  39.7 us
    ppermute x18, waiting for transfers between devices, exchange(): return lax.ppermute(value, axis, [(i, i ^ offset) for i in range(size)])  37.3 us
    ppermute x18, starting transfers between devices, exchange(): return lax.ppermute(value, axis, [(i, i ^ offset) for i in range(size)])  37.2 us
    pallas_call x1, Pallas kernels, basis_call(): pl.pallas_call(functools.partial(basis_kernel, shard, padded, 2.0 * CUTOF...  17.4 us
    unnamed x43, local copies, waits for them, and re-layouts  13.9 us
    pallas_call x1, Pallas kernels, ffn_call(): pl.pallas_call(functools.partial(ffn_kernel, quarter, row), out_shape=(ja...  6.85 us
    ppermute x4, starting transfers between devices, shifted(): return lax.ppermute(value, axes, pairs)  5.89 us
  transfers between devices with their start and end apart: 22, of which 8 were waited for; matrix products, arithmetic and copies ran while one was open for 10% of the time, Pallas kernels for 26%

profile of v1, /device:TPU:0, one launch (start us, length us, event | category | flops | bytes accessed | tf_op | source)
XLA Modules:
  0.0 218.6 jit_solution(5678083462152639220)
XLA Ops:
  5.7 2.4 %collective-permute-start.3 = (bf16[368,256]{1,0:T(8,128)(2,1)S(1)}, bf16[368,256]{1,0:T(8,128)(2,1)S(1)}, u32[]{:S(2)}, u32[]{:S(2)}) collective-permute-start(bf16[368,256]{1,0:T(8,128)(2,1)S(1)} %constant_dynamic-update-slice_fusion.pack0.small0), channel_id=1, source_target_pairs={{0,2},{1,3},{2,0},{3,1},{4,6},{5,7},{6,4},{7,5},{8,10},{9,11},{10,... | collective-permute-start | bytes 565256 | tf_op jit(solution)/shard_map/ppermute | solution.py:675
  8.9 2.0 collective-permute-start
  22.7 17.4 %radial_basis.1.basis_ref = bf16[6,640,4096]{2,1,0:T(8,128)(2,1)} custom-call(f32[384,64]{1,0:T(8,128)S(1)} %copy.34.dist_ref), custom_call_target="tpu_custom_call" | custom-call | flops 125829120 | bytes 31457280 | tf_op jit(solution)/shard_map/radial_basis/pallas_call | solution.py:151
  40.1 2.4 %collective-permute-start.5 = (bf16[832,256]{1,0:T(8,128)(2,1)S(1)}, bf16[832,256]{1,0:T(8,128)(2,1)S(1)}, u32[]{:S(2)}, u32[]{:S(2)}) collective-permute-start(bf16[832,256]{1,0:T(8,128)(2,1)S(1)} %constant_dynamic-update-slice_fusion.4.pack0), channel_id=1, source_target_pairs={{0,1},{1,0},{2,3},{3,2},{4,5},{5,4},{6,7},{7,6},{8,9},{9,8},{10,11... | collective-permute-start | bytes 1277960 | tf_op jit(solution)/shard_map/ppermute | solution.py:675
  42.5 1.7 collective-permute-start.6
  45.1 39.7 %attention_forward.1 = (bf16[6,256,4096]{2,1,0:T(8,128)(2,1)}, f32[6,8,4096]{2,1,0:T(8,128)}, bf16[384,256]{1,0:T(8,128)(2,1)}, bf16[3072,256]{1,0:T(8,128)(2,1)...) custom-call(s32[1]{0:T(128)} %bitcast.index_ref, s32[384]{0:T(512)} %counts_ref.1, ...), custom_call_target="tpu_custom_call" | custom-call | flops 12079595520 | bytes 44040192 | tf_op jit(solution)/shard_map/attention_forward/pallas_call | solution.py:288
  85.9 6.8 %feed_forward.1 = (f32[384,256]{1,0:T(8,128)}, f32[384,1]{1,0:T(8,128)}, f32[384,256]{1,0:T(8,128)}, bf16[384,256]{1,0:T(8,128)(2,1)}, bf16[4,832,256]{2,1,0:T(8,128)(2,1)}, /*index=5*/f32[8,256]{1,0:T(8,128)}) custom-call(s32[1]{0:T(128)} %bitcast.index_ref, bf16[384,256]{1,0:T(8,128)(2,1)} %features_ref.5, ...), custom_call_target="tpu_custom_call" | custom-call | flops 1811939328 | bytes 8388608 | tf_op jit(solution)/shard_map/feed_forward/pallas_call | solution.py:440
  92.7 41.8 %attention_backward.1 = (bf16[4,368,256]{2,1,0:T(8,128)(2,1)}, f32[384,256]{1,0:T(8,128)}, bf16[2,96,256]{2,1,0:T(8,128)(2,1)}) custom-call(bf16[384,256]{1,0:T(8,128)(2,1)} %features_ref.5, bf16[96,256]{1,0:T(8,128)(2,1)} %copy-done.12, bf16[96,256]{1,0:T(8,128)(2,1)} %copy-done.13, bf16[368,256]{1,0:T(8,128)(2,1)} %copy-done.3, ...), custom_call_target="tpu_custom_call" | custom-call | flops 16106127360 | bytes 44040192 | tf_op jit(solution)/shard_map/attention_backward/pallas_call | solution.py:629
  134.5 2.0 dynamic-slice_bitcast_fusion.5
  136.8 1.7 collective-permute-start.11
  139.8 1.7 collective-permute-start.17
  141.5 1.7 reduce.4
  146.0 2.0 collective-permute-done.12
  150.6 17.2 %collective-permute-start.13 = (bf16[368,256]{1,0:T(8,128)(2,1)S(1)}, bf16[368,256]{1,0:T(8,128)(2,1)S(1)}, u32[]{:S(2)}, u32[]{:S(2)}) collective-permute-start(bf16[368,256]{1,0:T(8,128)(2,1)S(1)} %fusion.5), channel_id=1, source_target_pairs={{0,4},{4,0},{8,12},{12,8},{16,20},{20,16},{24,28},{28,24},{1,5},{5... | collective-permute-start | bytes 565256 | tf_op jit(solution)/shard_map/ppermute | solution.py:675
  167.8 1.5 add_dynamic-update-slice_fusion
  169.3 3.5 %collective-permute-done.13 = bf16[368,256]{1,0:T(8,128)(2,1)S(1)} collective-permute-done((bf16[368,256]{1,0:T(8,128)(2,1)S(1)}, bf16[368,256]{1,0:T(8,128)(2,1)S(1)}, u32[]{:S(2)}, u32[]{:S(2)}) %collective-permute-start.13) | collective-permute-done | bytes 188448 | tf_op jit(solution)/shard_map/ppermute | solution.py:675
  172.9 2.6 %collective-permute-start.14 = (bf16[368,256]{1,0:T(8,128)(2,1)S(1)}, bf16[368,256]{1,0:T(8,128)(2,1)S(1)}, u32[]{:S(2)}, u32[]{:S(2)}) collective-permute-start(bf16[368,256]{1,0:T(8,128)(2,1)S(1)} %add_convert_fusion.3), channel_id=1, source_target_pairs={{0,8},{4,12},{8,0},{12,4},{16,24},{20,28},{24,16},{28,20},{1,9},{5... | collective-permute-start | bytes 565256 | tf_op jit(solution)/shard_map/ppermute | solution.py:675
  175.8 1.7 collective-permute-start.19
  177.5 1.5 fusion.6
  179.3 3.0 %collective-permute-start.15 = (bf16[368,256]{1,0:T(8,128)(2,1)S(1)}, bf16[368,256]{1,0:T(8,128)(2,1)S(1)}, u32[]{:S(2)}, u32[]{:S(2)}) collective-permute-start(bf16[368,256]{1,0:T(8,128)(2,1)S(1)} %add_convert_fusion.2), channel_id=1, source_target_pairs={{0,16},{4,20},{8,24},{12,28},{16,0},{20,4},{24,8},{28,12},{1,17},{... | collective-permute-start | bytes 565256 | tf_op jit(solution)/shard_map/ppermute | solution.py:675
  182.3 3.5 %collective-permute-done.19 = bf16[832,256]{1,0:T(8,128)(2,1)S(1)} collective-permute-done((bf16[832,256]{1,0:T(8,128)(2,1)S(1)}, bf16[832,256]{1,0:T(8,128)(2,1)S(1)}, u32[]{:S(2)}, u32[]{:S(2)}) %collective-permute-start.19) | collective-permute-done | bytes 426016 | tf_op jit(solution)/shard_map/ppermute | solution.py:675
  186.6 2.7 %collective-permute-done.15 = bf16[368,256]{1,0:T(8,128)(2,1)S(1)} collective-permute-done((bf16[368,256]{1,0:T(8,128)(2,1)S(1)}, bf16[368,256]{1,0:T(8,128)(2,1)S(1)}, u32[]{:S(2)}, u32[]{:S(2)}) %collective-permute-start.15) | collective-permute-done | bytes 188448 | tf_op jit(solution)/shard_map/ppermute | solution.py:675
  190.0 6.8 %collective-permute-done.20 = bf16[832,256]{1,0:T(8,128)(2,1)S(1)} collective-permute-done((bf16[832,256]{1,0:T(8,128)(2,1)S(1)}, bf16[832,256]{1,0:T(8,128)(2,1)S(1)}, u32[]{:S(2)}, u32[]{:S(2)}) %collective-permute-start.20) | collective-permute-done | bytes 426016 | tf_op jit(solution)/shard_map/ppermute | solution.py:675
  199.1 17.2 %collective-permute-done.21 = bf16[832,256]{1,0:T(8,128)(2,1)S(1)} collective-permute-done((bf16[832,256]{1,0:T(8,128)(2,1)S(1)}, bf16[832,256]{1,0:T(8,128)(2,1)S(1)}, u32[]{:S(2)}, u32[]{:S(2)}) %collective-permute-start.21) | collective-permute-done | bytes 426016 | tf_op jit(solution)/shard_map/ppermute | solution.py:675
  (96 shorter events, 33.3 us)
Async XLA Ops:
  4.9 35.1 %copy-start.3 = (bf16[368,256]{1,0:T(8,128)(2,1)}, bf16[368,256]{1,0:T(8,128)(2,1)S(1)}, u32[]{:S(2)}) copy-start(bf16[368,256]{1,0:T(8,128)(2,1)S(1)} %constant_dynamic-update-slice_fusion.pack0.small0) | copy-start | bytes 565252
  4.9 39.3 %collective-permute-start.2 = (bf16[368,256]{1,0:T(8,128)(2,1)S(1)}, bf16[368,256]{1,0:T(8,128)(2,1)S(1)}, u32[]{:S(2)}, u32[]{:S(2)}) collective-permute-start(bf16[368,256]{1,0:T(8,128)(2,1)S(1)} %constant_dynamic-update-slice_fusion.pack0.small0), channel_id=1, source_target_pairs={{0,1},{1,0},{2,3},{3,2},{4,5},{5,4},{6,7},{7,6},{8,9},{9,8},{10,11... | collective-permute-start | bytes 565256 | tf_op jit(solution)/shard_map/ppermute | solution.py:675
  5.7 38.7 %collective-permute-start.3 = (bf16[368,256]{1,0:T(8,128)(2,1)S(1)}, bf16[368,256]{1,0:T(8,128)(2,1)S(1)}, u32[]{:S(2)}, u32[]{:S(2)}) collective-permute-start(bf16[368,256]{1,0:T(8,128)(2,1)S(1)} %constant_dynamic-update-slice_fusion.pack0.small0), channel_id=1, source_target_pairs={{0,2},{1,3},{2,0},{3,1},{4,6},{5,7},{6,4},{7,5},{8,10},{9,11},{10,... | collective-permute-start | bytes 565256 | tf_op jit(solution)/shard_map/ppermute | solution.py:675
  8.0 36.3 %collective-permute-start.4 = (bf16[368,256]{1,0:T(8,128)(2,1)S(1)}, bf16[368,256]{1,0:T(8,128)(2,1)S(1)}, u32[]{:S(2)}, u32[]{:S(2)}) collective-permute-start(bf16[368,256]{1,0:T(8,128)(2,1)S(1)} %constant_dynamic-update-slice_fusion.pack0.small0), channel_id=1, source_target_pairs={{0,3},{1,2},{2,1},{3,0},{4,7},{5,6},{6,5},{7,4},{8,11},{9,10},{10,... | collective-permute-start | bytes 565256 | tf_op jit(solution)/shard_map/ppermute | solution.py:675
  8.9 31.2 %collective-permute-start = (bf16[96,256]{1,0:T(8,128)(2,1)S(1)}, bf16[96,256]{1,0:T(8,128)(2,1)S(1)}, u32[]{:S(2)}, u32[]{:S(2)}) collective-permute-start(bf16[96,256]{1,0:T(8,128)(2,1)S(1)} %get-tuple-element.92), channel_id=1, source_target_pairs={{0,1},{1,2},{2,3},{3,4},{4,5},{5,6},{6,7},{7,8},{8,9},{9,10},{10,1... | collective-permute-start | bytes 147464 | tf_op jit(solution)/shard_map/ppermute | solution.py:682
  10.9 31.5 %collective-permute-start.1 = (bf16[96,256]{1,0:T(8,128)(2,1)S(1)}, bf16[96,256]{1,0:T(8,128)(2,1)S(1)}, u32[]{:S(2)}, u32[]{:S(2)}) collective-permute-start(bf16[96,256]{1,0:T(8,128)(2,1)S(1)} %get-tuple-element.91), channel_id=1, source_target_pairs={{1,0},{2,1},{3,2},{4,3},{5,4},{6,5},{7,6},{8,7},{9,8},{10,9},{11,1... | collective-permute-start | bytes 147464 | tf_op jit(solution)/shard_map/ppermute | solution.py:682
  40.1 44.7 %collective-permute-start.5 = (bf16[832,256]{1,0:T(8,128)(2,1)S(1)}, bf16[832,256]{1,0:T(8,128)(2,1)S(1)}, u32[]{:S(2)}, u32[]{:S(2)}) collective-permute-start(bf16[832,256]{1,0:T(8,128)(2,1)S(1)} %constant_dynamic-update-slice_fusion.4.pack0), channel_id=1, source_target_pairs={{0,1},{1,0},{2,3},{3,2},{4,5},{5,4},{6,7},{7,6},{8,9},{9,8},{10,11... | collective-permute-start | bytes 1277960 | tf_op jit(solution)/shard_map/ppermute | solution.py:675
  42.5 42.3 %collective-permute-start.6 = (bf16[832,256]{1,0:T(8,128)(2,1)S(1)}, bf16[832,256]{1,0:T(8,128)(2,1)S(1)}, u32[]{:S(2)}, u32[]{:S(2)}) collective-permute-start(bf16[832,256]{1,0:T(8,128)(2,1)S(1)} %constant_dynamic-update-slice_fusion.4.pack0), channel_id=1, source_target_pairs={{0,2},{1,3},{2,0},{3,1},{4,6},{5,7},{6,4},{7,5},{8,10},{9,11},{10,... | collective-permute-start | bytes 1277960 | tf_op jit(solution)/shard_map/ppermute | solution.py:675
  44.2 40.6 %collective-permute-start.7 = (bf16[832,256]{1,0:T(8,128)(2,1)S(1)}, bf16[832,256]{1,0:T(8,128)(2,1)S(1)}, u32[]{:S(2)}, u32[]{:S(2)}) collective-permute-start(bf16[832,256]{1,0:T(8,128)(2,1)S(1)} %constant_dynamic-update-slice_fusion.4.pack0), channel_id=1, source_target_pairs={{0,3},{1,2},{2,1},{3,0},{4,7},{5,6},{6,5},{7,4},{8,11},{9,10},{10,... | collective-permute-start | bytes 1277960 | tf_op jit(solution)/shard_map/ppermute | solution.py:675
  92.7 45.8 %copy-start = (bf16[4,832,256]{2,1,0:T(8,128)(2,1)S(1)}, bf16[4,832,256]{2,1,0:T(8,128)(2,1)}, u32[]{:S(2)}) copy-start(bf16[4,832,256]{2,1,0:T(8,128)(2,1)} %get-tuple-element.69) | copy-start | bytes 5111812
  136.5 6.8 %collective-permute-start.10 = (bf16[368,256]{1,0:T(8,128)(2,1)}, bf16[368,256]{1,0:T(8,128)(2,1)}, u32[]{:S(2)}, u32[]{:S(2)}) collective-permute-start(bf16[368,256]{1,0:T(8,128)(2,1)} %get-tuple-element.82), channel_id=1, source_target_pairs={{0,1},{1,0},{2,3},{3,2},{4,5},{5,4},{6,7},{7,6},{8,9},{9,8},{10,11... | collective-permute-start | bytes 565256 | tf_op jit(solution)/shard_map/ppermute | solution.py:675
  136.8 7.9 %collective-permute-start.11 = (bf16[368,256]{1,0:T(8,128)(2,1)}, bf16[368,256]{1,0:T(8,128)(2,1)}, u32[]{:S(2)}, u32[]{:S(2)}) collective-permute-start(bf16[368,256]{1,0:T(8,128)(2,1)} %get-tuple-element.84), channel_id=1, source_target_pairs={{0,2},{1,3},{2,0},{3,1},{4,6},{5,7},{6,4},{7,5},{8,10},{9,11},{10,... | collective-permute-start | bytes 565256 | tf_op jit(solution)/shard_map/ppermute | solution.py:675
  138.6 9.4 %collective-permute-start.12 = (bf16[368,256]{1,0:T(8,128)(2,1)}, bf16[368,256]{1,0:T(8,128)(2,1)}, u32[]{:S(2)}, u32[]{:S(2)}) collective-permute-start(bf16[368,256]{1,0:T(8,128)(2,1)} %get-tuple-element.83), channel_id=1, source_target_pairs={{0,3},{1,2},{2,1},{3,0},{4,7},{5,6},{6,5},{7,4},{8,11},{9,10},{10,... | collective-permute-start | bytes 565256 | tf_op jit(solution)/shard_map/ppermute | solution.py:675
  139.4 36.2 %collective-permute-start.16 = (bf16[832,256]{1,0:T(8,128)(2,1)}, bf16[832,256]{1,0:T(8,128)(2,1)S(1)}, u32[]{:S(2)}, u32[]{:S(2)}) collective-permute-start(bf16[832,256]{1,0:T(8,128)(2,1)} %get-tuple-element.70), channel_id=1, source_target_pairs={{0,1},{1,0},{2,3},{3,2},{4,5},{5,4},{6,7},{7,6},{8,9},{9,8},{10,11... | collective-permute-start | bytes 1277960 | tf_op jit(solution)/shard_map/ppermute | solution.py:675
  139.8 35.8 %collective-permute-start.17 = (bf16[832,256]{1,0:T(8,128)(2,1)S(1)}, bf16[832,256]{1,0:T(8,128)(2,1)S(1)}, u32[]{:S(2)}, u32[]{:S(2)}) collective-permute-start(bf16[832,256]{1,0:T(8,128)(2,1)S(1)} %get-tuple-element.72), channel_id=1, source_target_pairs={{0,2},{1,3},{2,0},{3,1},{4,6},{5,7},{6,4},{7,5},{8,10},{9,11},{10,... | collective-permute-start | bytes 1277960 | tf_op jit(solution)/shard_map/ppermute | solution.py:675
  143.2 32.4 %collective-permute-start.18 = (bf16[832,256]{1,0:T(8,128)(2,1)S(1)}, bf16[832,256]{1,0:T(8,128)(2,1)S(1)}, u32[]{:S(2)}, u32[]{:S(2)}) collective-permute-start(bf16[832,256]{1,0:T(8,128)(2,1)S(1)} %get-tuple-element.71), channel_id=1, source_target_pairs={{0,3},{1,2},{2,1},{3,0},{4,7},{5,6},{6,5},{7,4},{8,11},{9,10},{10,... | collective-permute-start | bytes 1277960 | tf_op jit(solution)/shard_map/ppermute | solution.py:675
  144.7 5.9 %collective-permute-start.8 = (bf16[96,256]{1,0:T(8,128)(2,1)S(1)}, bf16[96,256]{1,0:T(8,128)(2,1)S(1)}, u32[]{:S(2)}, u32[]{:S(2)}) collective-permute-start(bf16[96,256]{1,0:T(8,128)(2,1)S(1)} %get-tuple-element.94), channel_id=1, source_target_pairs={{0,1},{1,2},{2,3},{3,4},{4,5},{5,6},{6,7},{7,8},{8,9},{9,10},{10,1... | collective-permute-start | bytes 147464 | tf_op jit(solution)/shard_map/ppermute | solution.py:682
  148.0 29.5 %collective-permute-start.9 = (bf16[96,256]{1,0:T(8,128)(2,1)S(1)}, bf16[96,256]{1,0:T(8,128)(2,1)S(1)}, u32[]{:S(2)}, u32[]{:S(2)}) collective-permute-start(bf16[96,256]{1,0:T(8,128)(2,1)S(1)} %get-tuple-element.93), channel_id=1, source_target_pairs={{1,0},{2,1},{3,2},{4,3},{5,4},{6,5},{7,6},{8,7},{9,8},{10,9},{11,1... | collective-permute-start | bytes 147464 | tf_op jit(solution)/shard_map/ppermute | solution.py:682
  150.6 22.3 %collective-permute-start.13 = (bf16[368,256]{1,0:T(8,128)(2,1)S(1)}, bf16[368,256]{1,0:T(8,128)(2,1)S(1)}, u32[]{:S(2)}, u32[]{:S(2)}) collective-permute-start(bf16[368,256]{1,0:T(8,128)(2,1)S(1)} %fusion.5), channel_id=1, source_target_pairs={{0,4},{4,0},{8,12},{12,8},{16,20},{20,16},{24,28},{28,24},{1,5},{5... | collective-permute-start | bytes 565256 | tf_op jit(solution)/shard_map/ppermute | solution.py:675
  172.9 6.4 %collective-permute-start.14 = (bf16[368,256]{1,0:T(8,128)(2,1)S(1)}, bf16[368,256]{1,0:T(8,128)(2,1)S(1)}, u32[]{:S(2)}, u32[]{:S(2)}) collective-permute-start(bf16[368,256]{1,0:T(8,128)(2,1)S(1)} %add_convert_fusion.3), channel_id=1, source_target_pairs={{0,8},{4,12},{8,0},{12,4},{16,24},{20,28},{24,16},{28,20},{1,9},{5... | collective-permute-start | bytes 565256 | tf_op jit(solution)/shard_map/ppermute | solution.py:675
  175.8 10.0 %collective-permute-start.19 = (bf16[832,256]{1,0:T(8,128)(2,1)S(1)}, bf16[832,256]{1,0:T(8,128)(2,1)S(1)}, u32[]{:S(2)}, u32[]{:S(2)}) collective-permute-start(bf16[832,256]{1,0:T(8,128)(2,1)S(1)} %fusion.2), channel_id=1, source_target_pairs={{0,4},{4,0},{8,12},{12,8},{16,20},{20,16},{24,28},{28,24},{1,5},{5... | collective-permute-start | bytes 1277960 | tf_op jit(solution)/shard_map/ppermute | solution.py:675
  179.3 9.9 %collective-permute-start.15 = (bf16[368,256]{1,0:T(8,128)(2,1)S(1)}, bf16[368,256]{1,0:T(8,128)(2,1)S(1)}, u32[]{:S(2)}, u32[]{:S(2)}) collective-permute-start(bf16[368,256]{1,0:T(8,128)(2,1)S(1)} %add_convert_fusion.2), channel_id=1, source_target_pairs={{0,16},{4,20},{8,24},{12,28},{16,0},{20,4},{24,8},{28,12},{1,17},{... | collective-permute-start | bytes 565256 | tf_op jit(solution)/shard_map/ppermute | solution.py:675
  185.9 10.9 %collective-permute-start.20 = (bf16[832,256]{1,0:T(8,128)(2,1)S(1)}, bf16[832,256]{1,0:T(8,128)(2,1)S(1)}, u32[]{:S(2)}, u32[]{:S(2)}) collective-permute-start(bf16[832,256]{1,0:T(8,128)(2,1)S(1)} %add_convert_fusion.1), channel_id=1, source_target_pairs={{0,8},{4,12},{8,0},{12,4},{16,24},{20,28},{24,16},{28,20},{1,9},{5... | collective-permute-start | bytes 1277960 | tf_op jit(solution)/shard_map/ppermute | solution.py:675
  196.9 19.3 %collective-permute-start.21 = (bf16[832,256]{1,0:T(8,128)(2,1)S(1)}, bf16[832,256]{1,0:T(8,128)(2,1)S(1)}, u32[]{:S(2)}, u32[]{:S(2)}) collective-permute-start(bf16[832,256]{1,0:T(8,128)(2,1)S(1)} %add_convert_fusion), channel_id=1, source_target_pairs={{0,16},{4,20},{8,24},{12,28},{16,0},{20,4},{24,8},{28,12},{1,17},{... | collective-permute-start | bytes 1277960 | tf_op jit(solution)/shard_map/ppermute | solution.py:675
  (12 other events, 85.6 us)

commit v2 on v1

v2 whole, which is shorter than its diff:
```python
import functools
import math

import jax
import jax.numpy as jnp
from jax import lax
from jax.experimental import pallas as pl
from jax.experimental.pallas import tpu as pltpu
from jax.sharding import PartitionSpec as P

HEADS = 8
HALO = 96
EPSILON = 1e-06
CUTOFF = 6.0

BLOCK = 64
PAIRS = BLOCK // 2
LANES = 128
TILE = 256
GROUP = 1024

BF16 = jnp.bfloat16
F32 = jnp.float32


def nn(a, b):
    return lax.dot_general(a, b, (((1,), (0,)), ((), ())), preferred_element_type=F32)


def nt(a, b):
    return lax.dot_general(a, b, (((1,), (1,)), ((), ())), preferred_element_type=F32)


def tn(a, b):
    return lax.dot_general(a, b, (((0,), (0,)), ((), ())), preferred_element_type=F32)


def round_up(value, step):
    return -(-value // step) * step


def rms(value):
    inverse = lax.rsqrt(jnp.mean(value * value, -1, keepdims=True) + EPSILON)
    return value * inverse, inverse


def norm_back(grad_normed, normed_rows, inverse):
    return inverse * (
        grad_normed - normed_rows * jnp.mean(grad_normed * normed_rows, -1, keepdims=True)
    )


def pair_rows(block):
    return jnp.concatenate([block[:PAIRS], block[PAIRS:]], axis=1)


def head_of_lane(width):
    return lax.broadcasted_iota(jnp.int32, (1, width), 1) // (width // HEADS)


def spread_heads(rows, out_ref):
    atoms, width = rows.shape
    heads = head_of_lane(width)
    for start in range(0, atoms, PAIRS):
        block, side = start // BLOCK, (start % BLOCK) // PAIRS
        part = rows[start : start + PAIRS]
        for head in range(HEADS):
            place = block * BLOCK * HEADS + side * HEADS + head
            kept = jnp.where(heads == head, part, 0.0)
            for half in range(width // LANES):
                out_ref[half, pl.ds(place, PAIRS, stride=2 * HEADS), :] = kept[
                    :, half * LANES : (half + 1) * LANES
                ]


def wide(ref, rows=slice(None)):
    return jnp.concatenate([ref[half, rows, :] for half in range(ref.shape[0])], axis=1)


def gather_heads(rows_ref, weight, atoms):
    heads = head_of_lane(weight.shape[1])
    lefts, rights = [], []
    for head in range(HEADS):
        parts = []
        for start in range(0, atoms, PAIRS):
            block, side = start // BLOCK, (start % BLOCK) // PAIRS
            place = block * BLOCK * HEADS + side * HEADS + head
            parts.append(wide(rows_ref, pl.ds(place, PAIRS, stride=2 * HEADS)))
        lefts.append(jnp.concatenate(parts, axis=0).astype(BF16))
        rights.append(jnp.where(heads == head, weight, jnp.zeros_like(weight)))
    return nn(jnp.concatenate(lefts, axis=1), jnp.concatenate(rights, axis=0))


def half_max(value, low_half):
    low = jnp.max(jnp.where(low_half, value, -jnp.inf), axis=1, keepdims=True)
    high = jnp.max(jnp.where(low_half, -jnp.inf, value), axis=1, keepdims=True)
    return jnp.where(low_half, low, high)


def fetch(source, buffer, semaphores, step, first=0):
    slot = lax.rem(step, 2)
    rows = source.shape[1]
    return pltpu.make_async_copy(
        source.at[step], buffer.at[slot, pl.ds(first, rows)], semaphores.at[slot]
    )


def fetch_next(source, buffer, semaphores, step, steps, first=0):
    @pl.when(step + 1 < steps)
    def _():
        fetch(source, buffer, semaphores, step + 1, first).start()

    fetch(source, buffer, semaphores, step, first).wait()
    return buffer.at[lax.rem(step, 2)]


def write_onehot(relative_ref, window, out_ref):
    relative = relative_ref[...].astype(BF16)
    one, zero = jnp.ones((), BF16), jnp.zeros((), BF16)
    place = lax.broadcasted_iota(jnp.int32, (16, LANES), 0).astype(F32)
    for first in range(0, PAIRS, 8):
        rows = [
            jnp.broadcast_to(relative[pair : pair + 1, :], (16, LANES))
            for pair in range(first, first + 8)
        ]
        for row in range(0, window, 16):
            here = (place + float(row)).astype(BF16)
            for pair, wanted in enumerate(rows, first):
                out_ref[row : row + 16, pair * LANES : (pair + 1) * LANES] = jnp.where(
                    here == wanted, one, zero
                )


def diagonal(tile, low_half, less=None):
    parts = []
    for side in range(2):
        lanes = slice(side * LANES, (side + 1) * LANES)
        rows = [slice(side * 16 + part * 8, side * 16 + part * 8 + 8) for part in range(2)]
        both = [tile[row, lanes] if less is None else tile[row, lanes] - less[row] for row in rows]
        parts.append(jnp.where(low_half, both[0], both[1]))
    return parts


def block_rows(value, low_half):
    zero = jnp.zeros_like(value)
    return jnp.concatenate(
        [jnp.where(low_half, value, zero), jnp.where(low_half, zero, value)], axis=0
    ).astype(BF16)


def pack_kernel(
    index_ref,
    rbf_ref,
    query_ref,
    key_ref,
    value_ref,
    out_ref,
    gate_ref,
    up_ref,
    down_ref,
    attn_ref,
    ffn_ref,
    read_ref,
    features_ref,
    small_ref,
    large_ref,
    initial_ref,
    final_ref,
):
    initial_ref[...] = features_ref[:HALO, :]
    final_ref[...] = features_ref[features_ref.shape[0] - HALO :, :]
    shard, width = rbf_ref.shape
    quarter = query_ref.shape[0]
    after_rbf = round_up(shard, 16)
    rest = jnp.zeros((after_rbf - shard, width), F32)
    small_ref[:after_rbf, :] = jnp.concatenate([rbf_ref[...].astype(F32), rest], 0).astype(BF16)
    row = after_rbf
    for ref in (query_ref, key_ref, value_ref):
        small_ref[row : row + quarter, :] = ref[...]
        row += quarter
    vectors = jnp.concatenate([ref[...].astype(F32) for ref in (attn_ref, ffn_ref, read_ref)], 0)
    copies = jnp.concatenate([vectors] * (width // quarter), axis=1)
    owner = lax.broadcasted_iota(jnp.int32, (1, width), 1) // quarter
    own = jnp.where(owner == index_ref[0], copies, 0.0)
    small_ref[row : row + 16, :] = jnp.concatenate(
        [own, jnp.zeros((16 - own.shape[0], width), F32)], 0
    ).astype(BF16)
    row = 0
    for ref in (gate_ref, up_ref):
        for part in range(ref.shape[1] // width):
            large_ref[row : row + quarter, :] = ref[:, part * width : (part + 1) * width]
            row += quarter
    for ref in (down_ref, out_ref):
        large_ref[row : row + ref.shape[0], :] = ref[...]
        row += ref.shape[0]


def pack_call(index, rbf, query, key, value, out, gate, up, down, *rest):
    width = rbf.shape[1]
    quarter = query.shape[0]
    vmem = pl.BlockSpec(memory_space=pltpu.VMEM)
    small = round_up(rbf.shape[0], 16) + 3 * quarter + 16
    large = 2 * quarter * (gate.shape[1] // width) + down.shape[0] + quarter
    return pl.pallas_call(
        pack_kernel,
        out_shape=(
            jax.ShapeDtypeStruct((small, width), BF16),
            jax.ShapeDtypeStruct((large, width), BF16),
            jax.ShapeDtypeStruct((HALO, width), BF16),
            jax.ShapeDtypeStruct((HALO, width), BF16),
        ),
        in_specs=[pl.BlockSpec(memory_space=pltpu.SMEM)] + [vmem] * 12,
        out_specs=(vmem,) * 4,
        cost_estimate=pl.CostEstimate(flops=0, bytes_accessed=2**21, transcendentals=0),
        name="pack_weights",
    )(index, rbf, query, key, value, out, gate, up, down, *rest)


def basis_kernel(
    shard, padded, spread, step, dist_ref, rows_ref, out_ref, relative_ref, by_atom, scaled, envelopes
):
    block = pl.program_id(0)
    factor = math.sqrt(0.5 / math.log(2.0)) / spread

    @pl.when(block == 0)
    def _():
        by_atom[0] = dist_ref[...].T
        by_atom[1] = rows_ref[...].astype(F32).T

    place = pl.ds(pl.multiple_of(block * BLOCK, BLOCK), BLOCK)
    dist = pair_rows(by_atom[0, place, :])
    scaled[...] = dist * factor
    envelopes[...] = 0.5 * (jnp.cos(jnp.pi * dist / CUTOFF) + 1.0)
    relative_ref[...] = pair_rows(by_atom[1, place, :]) - (block * BLOCK).astype(F32)
    rows = out_ref.shape[0]
    iota = lax.broadcasted_iota(jnp.int32, (8, LANES), 0).astype(F32) * (step * factor)
    center = lambda row: ((row // padded) * shard + row % padded) * step * factor

    for first in range(0, PAIRS, 8):
        pairs = range(first, first + 8)
        bases = [scaled[pair : pair + 1, :] - iota for pair in pairs]
        heights = [jnp.broadcast_to(envelopes[pair : pair + 1, :], (16, LANES)) for pair in pairs]
        for row in range(0, rows, 16):
            for pair, base, height in zip(pairs, bases, heights):
                delta = jnp.concatenate([base - center(row), base - center(row + 8)], axis=0)
                value = jnp.exp2(-(delta * delta)) * height
                out_ref[row : row + 16, pair * LANES : (pair + 1) * LANES] = value.astype(BF16)


def basis_call(distances, neighbours, shard, padded, members, basis_count):
    slots, atoms = distances.shape
    blocks = atoms // BLOCK
    rows = members * padded
    edges = BLOCK * slots
    whole = pl.BlockSpec((slots, atoms), lambda b: (0, 0))
    return pl.pallas_call(
        functools.partial(
            basis_kernel, shard, padded, 2.0 * CUTOFF / basis_count, CUTOFF / basis_count
        ),
        grid=(blocks,),
        out_shape=(
            jax.ShapeDtypeStruct((blocks, rows, edges), BF16),
            jax.ShapeDtypeStruct((blocks, PAIRS, LANES), F32),
        ),
        in_specs=[whole, whole],
        out_specs=(
            pl.BlockSpec((None, rows, edges), lambda b: (b, 0, 0)),
            pl.BlockSpec((None, PAIRS, LANES), lambda b: (b, 0, 0)),
        ),
        scratch_shapes=[
            pltpu.VMEM((2, atoms, slots), F32),
            pltpu.VMEM((PAIRS, LANES), F32),
            pltpu.VMEM((PAIRS, LANES), F32),
        ],
        compiler_params=pltpu.CompilerParams(vmem_limit_bytes=40 * 2**20),
        cost_estimate=pl.CostEstimate(
            flops=8 * atoms * slots * rows,
            bytes_accessed=2 * atoms * slots * rows,
            transcendentals=atoms * slots * rows,
        ),
        name="radial_basis",
    )(distances, neighbours)


def place_shards(index_ref, packs, row, count, out_ref):
    me = index_ref[0]
    for offset, pack in enumerate(packs):
        owner = lax.bitwise_xor(me, offset)
        start = pl.multiple_of(owner * count, 8)
        out_ref[pl.ds(start, count), :] = pack[row : row + count, :].astype(out_ref.dtype)


def vector_of(packs, row):
    total = packs[0][row : row + 1, :].astype(F32)
    for pack in packs[1:]:
        total = total + pack[row : row + 1, :].astype(F32)
    return total


def forward_kernel(
    padded,
    quarter,
    scale,
    index_ref,
    counts_ref,
    features_ref,
    before_ref,
    after_ref,
    pack0,
    pack1,
    pack2,
    pack3,
    relative_ref,
    basis_hbm,
    edge_ref,
    power_ref,
    inverse_ref,
    pooled_ref,
    attended_ref,
    lookup_ref,
    query_ref,
    kvq_ref,
    weight_t,
    assembled,
    spread,
    keyed,
    bands,
    pooled,
    phi_buffer,
    semaphores,
):
    step = pl.program_id(0)
    steps = pl.num_programs(0)
    packs = (pack0, pack1, pack2, pack3)
    atoms, width = features_ref.shape
    low_half = lax.broadcasted_iota(jnp.int32, (1, LANES), 1) < LANES // 2
    lane = lax.broadcasted_iota(jnp.int32, (1, LANES), 1)
    edges = edge_ref.shape[1]
    window = BLOCK + 2 * HALO

    @pl.when(step == 0)
    def _():
        fetch(basis_hbm, phi_buffer, semaphores, 0, window).start()
        place_shards(index_ref, packs, 0, padded, assembled)
        weight_t[:, window:] = assembled[...].T.astype(BF16)
        start = round_up(padded, 16)
        for which in range(3):
            place_shards(index_ref, packs, start + which * quarter, quarter, kvq_ref.at[which])
        gain = vector_of(packs, start + 3 * quarter)
        for ref, start in ((before_ref, 0), (features_ref, HALO), (after_ref, HALO + atoms)):
            normed, _ = rms(ref[...].astype(F32))
            lookup_ref[start : start + ref.shape[0], :] = (normed * gain).astype(BF16)
        query = nn(lookup_ref[HALO : HALO + atoms, :], kvq_ref[0]).astype(BF16)
        query_ref[...] = query
        spread_heads(query.astype(F32), spread)
        keyed[...] = (nt(wide(spread).astype(BF16), kvq_ref[1]) * scale).astype(BF16)
        bands[...] = jnp.zeros_like(bands)

    table = lookup_ref[pl.ds(pl.multiple_of(step * BLOCK, BLOCK), window), :]
    weight_t[:, :window] = table.astype(F32).T.astype(BF16)
    phi = phi_buffer.at[lax.rem(step, 2)]
    write_onehot(relative_ref, window, phi)
    fetch_next(basis_hbm, phi_buffer, semaphores, step, steps, window)
    wide_part = 2 * GROUP
    for start in range(0, edges, wide_part):
        part = slice(start, start + wide_part)
        edge_ref[:, part] = nn(weight_t[...], phi[:, part]).astype(BF16)
    rows = BLOCK * HEADS
    base = pl.multiple_of(step * rows, rows)
    scores = []
    for tile in range(edges // TILE):
        left = keyed[pl.ds(base + tile * 32, 32), :]
        right = edge_ref[:, tile * TILE : (tile + 1) * TILE]
        for side, score in enumerate(diagonal(nn(left, right), low_half)):
            pair = 2 * tile + side
            low_count = counts_ref[step * BLOCK + pair]
            high_count = counts_ref[step * BLOCK + PAIRS + pair]
            usable = lane < jnp.where(low_half, low_count, high_count + LANES // 2)
            scores.append(jnp.where(usable, score, -1e30))
    score = jnp.concatenate(scores, axis=0)
    power = jnp.exp(score - half_max(score, low_half))
    power_ref[...] = power.astype(BF16)
    group_rows = bands.shape[1]
    pairs = GROUP // LANES
    ones = jnp.ones((GROUP, LANES), BF16)
    for pair in range(PAIRS):
        group, place = pair // pairs, pair % pairs
        bands[
            group, place * 16 : (place + 1) * 16, place * LANES : (place + 1) * LANES
        ] = block_rows(power[pair * 8 : (pair + 1) * 8], low_half)
    for group in range(edges // GROUP):
        part = slice(group * GROUP, (group + 1) * GROUP)
        band = bands[group]
        inverse = 1.0 / nn(band, ones)
        result = nt(band, edge_ref[:, part])
        rows = slice(group * group_rows, (group + 1) * group_rows)
        place = pl.ds(base + group * group_rows, group_rows)
        inverse_ref[rows, :] = inverse
        for half in range(width // LANES):
            lanes = slice(half * LANES, (half + 1) * LANES)
            value = result[:, lanes] * inverse
            pooled[half, place, :] = value
            pooled_ref[rows, lanes] = value.astype(BF16)

    @pl.when(step == steps - 1)
    def _():
        attended_ref[...] = gather_heads(pooled, kvq_ref[2], atoms).astype(BF16)


def forward_call(index, counts, features, before, after, packs, relative, basis, padded, quarter):
    atoms, width = features.shape
    blocks, rows, edges = basis.shape
    slots = edges // BLOCK
    table = atoms + 2 * HALO
    full = lambda shape: pl.BlockSpec(shape, lambda b: (0,) * len(shape))
    head_rows = atoms * HEADS
    window = BLOCK + 2 * HALO
    group_rows = GROUP // slots * HEADS
    return pl.pallas_call(
        functools.partial(forward_kernel, padded, quarter, (width // HEADS) ** -0.5),
        grid=(blocks,),
        out_shape=(
            jax.ShapeDtypeStruct((blocks, width, edges), BF16),
            jax.ShapeDtypeStruct((blocks, PAIRS * HEADS, LANES), BF16),
            jax.ShapeDtypeStruct((head_rows, LANES), F32),
            jax.ShapeDtypeStruct((head_rows, width), BF16),
            jax.ShapeDtypeStruct((atoms, width), BF16),
            jax.ShapeDtypeStruct((table, width), BF16),
            jax.ShapeDtypeStruct((atoms, width), BF16),
            jax.ShapeDtypeStruct((3, width, width), BF16),
        ),
        in_specs=[
            pl.BlockSpec(memory_space=pltpu.SMEM),
            pl.BlockSpec(memory_space=pltpu.SMEM),
            full((atoms, width)),
            full((HALO, width)),
            full((HALO, width)),
        ]
        + [full(pack.shape) for pack in packs]
        + [
            pl.BlockSpec((None, PAIRS, LANES), lambda b: (b, 0, 0)),
            pl.BlockSpec(memory_space=pl.ANY),
        ],
        out_specs=(
            pl.BlockSpec((None, width, edges), lambda b: (b, 0, 0)),
            pl.BlockSpec((None, PAIRS * HEADS, LANES), lambda b: (b, 0, 0)),
            pl.BlockSpec((BLOCK * HEADS, LANES), lambda b: (b, 0)),
            pl.BlockSpec((BLOCK * HEADS, width), lambda b: (b, 0)),
            full((atoms, width)),
            full((table, width)),
            full((atoms, width)),
            full((3, width, width)),
        ),
        scratch_shapes=[
            pltpu.VMEM((width, window + rows), BF16),
            pltpu.VMEM((rows, width), F32),
            pltpu.VMEM((width // LANES, head_rows, LANES), F32),
            pltpu.VMEM((head_rows, width), BF16),
            pltpu.VMEM((edges // GROUP, group_rows, GROUP), BF16),
            pltpu.VMEM((width // LANES, head_rows, LANES), F32),
            pltpu.VMEM((2, window + rows, edges), BF16),
            pltpu.SemaphoreType.DMA((2,)),
        ],
        compiler_params=pltpu.CompilerParams(vmem_limit_bytes=58 * 2**20),
        cost_estimate=pl.CostEstimate(
            flops=2 * atoms * slots * width * (rows + window + 64),
            bytes_accessed=2 * atoms * slots * (rows + width),
            transcendentals=atoms * slots * HEADS,
        ),
        name="attention_forward",
    )(index, counts, features, before, after, *packs, relative, basis)


def ffn_kernel(
    quarter,
    small_row,
    index_ref,
    features_ref,
    attended_ref,
    grad_out_ref,
    grad_energy_ref,
    small0,
    small1,
    small2,
    small3,
    pack0,
    pack1,
    pack2,
    pack3,
    out_ref,
    energy_ref,
    grad_residual_ref,
    grad_attended_ref,
    sums_ref,
    grads0,
    grads1,
    grads2,
    grads3,
    w_gate,
    w_up,
    w_down,
    w_out,
    g_gate,
    g_up,
    g_down,
    g_out,
):
    small = (small0, small1, small2, small3)
    packs = (pack0, pack1, pack2, pack3)
    atoms, width = features_ref.shape
    parts = w_gate.shape[1] // width
    down_rows = w_down.shape[0] // 4
    me = index_ref[0]
    for offset, pack in enumerate(packs):
        owner = lax.bitwise_xor(me, offset)
        rows = pl.ds(pl.multiple_of(owner * quarter, 16), quarter)
        for part in range(parts):
            lanes = slice(part * width, (part + 1) * width)
            w_gate[rows, lanes] = pack[part * quarter : (part + 1) * quarter, :]
            w_up[rows, lanes] = pack[(parts + part) * quarter : (parts + part + 1) * quarter, :]
        start = 2 * parts * quarter
        w_down[pl.ds(pl.multiple_of(owner * down_rows, 16), down_rows), :] = pack[
            start : start + down_rows, :
        ]
        w_out[rows, :] = pack[start + down_rows : start + down_rows + quarter, :]
    gain = vector_of(small, small_row + 1)
    readout = vector_of(small, small_row + 2)

    attended = attended_ref[...]
    residual = features_ref[...].astype(F32) + nn(attended, w_out[...])
    normed, inverse = rms(residual)
    hidden = (normed * gain).astype(BF16)
    gate = nn(hidden, w_gate[...])
    up = nn(hidden, w_up[...])
    sigmoid = jax.nn.sigmoid(gate)
    silu = gate * sigmoid
    activated = (silu * up).astype(BF16)
    outputs = residual + nn(activated, w_down[...])
    out_ref[...] = outputs
    energy = jnp.sum(outputs * readout, -1, keepdims=True)
    energy_ref[...] = jnp.broadcast_to(energy, (atoms, LANES)).T[:1, :]
    grad_energy = jnp.broadcast_to(grad_energy_ref[...], (LANES, atoms)).T[:, :1]
    grad_act = grad_out_ref[...].astype(F32) + grad_energy * readout
    grad_branch = grad_act.astype(BF16)
    g_down[...] = tn(activated, grad_branch)
    grad_activated = nt(grad_branch, w_down[...])
    grad_gate = (grad_activated * up * sigmoid * (1.0 + gate * (1.0 - sigmoid))).astype(BF16)
    grad_up = (grad_activated * silu).astype(BF16)
    g_gate[...] = tn(hidden, grad_gate)
    g_up[...] = tn(hidden, grad_up)
    grad_hidden = (nt(grad_gate, w_gate[...]) + nt(grad_up, w_up[...])).astype(BF16).astype(F32)
    grad_residual = grad_act + norm_back(grad_hidden * gain, normed, inverse)
    grad_residual_ref[...] = grad_residual
    grad_proj = grad_residual.astype(BF16)
    grad_attended_ref[...] = nt(grad_proj, w_out[...]).astype(BF16)
    g_out[...] = tn(attended, grad_proj)
    for offset, grads in enumerate((grads0, grads1, grads2, grads3)):
        owner = lax.bitwise_xor(me, offset)
        rows = pl.ds(pl.multiple_of(owner * quarter, 16), quarter)
        row = 0
        for grad in (g_gate, g_up):
            for part in range(parts):
                lanes = slice(part * width, (part + 1) * width)
                grads[row : row + quarter, :] = grad[rows, lanes].astype(BF16)
                row += quarter
        down = pl.ds(pl.multiple_of(owner * down_rows, 16), down_rows)
        grads[row : row + down_rows, :] = g_down[down, :].astype(BF16)
        row += down_rows
        grads[row : row + quarter, :] = g_out[rows, :].astype(BF16)
    sums_ref[...] = jnp.zeros_like(sums_ref)
    sums_ref[1:2, :] = jnp.sum(grad_hidden * normed, 0, keepdims=True)
    sums_ref[2:3, :] = jnp.sum(grad_energy * outputs, 0, keepdims=True)


def ffn_call(index, features, attended, grad_out, grad_energy, small, packs, hidden, quarter, row):
    atoms, width = features.shape
    vmem = pl.BlockSpec(memory_space=pltpu.VMEM)
    return pl.pallas_call(
        functools.partial(ffn_kernel, quarter, row),
        out_shape=(
            jax.ShapeDtypeStruct((atoms, width), F32),
            jax.ShapeDtypeStruct((1, atoms), F32),
            jax.ShapeDtypeStruct((atoms, width), F32),
            jax.ShapeDtypeStruct((atoms, width), BF16),
            jax.ShapeDtypeStruct((8, width), F32),
        )
        + (jax.ShapeDtypeStruct(packs[0].shape, BF16),) * 4,
        in_specs=[pl.BlockSpec(memory_space=pltpu.SMEM)] + [vmem] * 12,
        out_specs=(vmem,) * 9,
        scratch_shapes=[
            pltpu.VMEM(shape, dtype)
            for dtype in (BF16, F32)
            for shape in ((width, hidden), (width, hidden), (hidden, width), (width, width))
        ],
        compiler_params=pltpu.CompilerParams(vmem_limit_bytes=58 * 2**20),
        cost_estimate=pl.CostEstimate(
            flops=18 * atoms * width * hidden, bytes_accessed=2**23, transcendentals=atoms * hidden
        ),
        name="feed_forward",
    )(index, features, attended, grad_out, grad_energy, *small, *packs)


def score_kernel(
    quarter,
    scale,
    index_ref,
    lookup_ref,
    query_ref,
    kvq_ref,
    pooled_ref,
    inverse_ref,
    attended_ref,
    grad_attended_ref,
    power_ref,
    edge_ref,
    grad_score_ref,
    mixed_ref,
    grad_query_ref,
    grads0,
    grads1,
    grads2,
    grads3,
    spread_q,
    spread_g,
    scaled,
    valued,
    means,
    bands,
    pooled,
    weight_grad,
):
    step = pl.program_id(0)
    atoms, width = query_ref.shape
    low_half = lax.broadcasted_iota(jnp.int32, (1, LANES), 1) < LANES // 2
    edges = edge_ref.shape[1]
    group_rows = bands.shape[1]
    groups = edges // GROUP
    pairs = GROUP // LANES

    @pl.when(step == 0)
    def _():
        grad_attended = grad_attended_ref[...].astype(F32)
        product = grad_attended * attended_ref[...].astype(F32)
        high = product.astype(BF16)
        low = (product - high.astype(F32)).astype(BF16)
        heads = lax.broadcasted_iota(jnp.int32, (width, HEADS * LANES), 0) // (width // HEADS)
        copies = lax.broadcasted_iota(jnp.int32, (width, HEADS * LANES), 1) // LANES
        summing = jnp.where(heads == copies, 1.0, 0.0).astype(BF16)
        mean = nn(high, summing) + nn(low, summing)
        for start in range(0, atoms, PAIRS):
            block, side = start // BLOCK, (start % BLOCK) // PAIRS
            for head in range(HEADS):
                place = block * BLOCK * HEADS + side * HEADS + head
                means[pl.ds(place, PAIRS, stride=2 * HEADS), :] = mean[
                    start : start + PAIRS, head * LANES : (head + 1) * LANES
                ]
        inverse = inverse_ref[...]
        means[...] = means[...] * inverse
        spread_heads(query_ref[...].astype(F32), pooled)
        spread_q[...] = wide(pooled).astype(BF16)
        spread_heads(grad_attended, pooled)
        spread_g[...] = wide(pooled).astype(BF16)
        scaled[...] = (wide(pooled) * jnp.concatenate([inverse] * (width // LANES), axis=1)).astype(
            BF16
        )
        valued[...] = nt(scaled[...], kvq_ref[2]).astype(BF16)
        bands[...] = jnp.zeros_like(bands)

    rows = BLOCK * HEADS
    base = pl.multiple_of(step * rows, rows)
    for group in range(groups):
        place = pl.ds(base + group * group_rows, group_rows)
        mixed_ref[group, :, :group_rows] = (nt(kvq_ref[1], spread_q[place, :]) * scale).astype(BF16)
        mixed_ref[group, :, group_rows:] = nt(kvq_ref[2], scaled[place, :]).astype(BF16)
    power = power_ref[...].astype(F32)
    for tile in range(edges // TILE):
        place = pl.ds(base + tile * 32, 32)
        product = nn(valued[place, :], edge_ref[:, tile * TILE : (tile + 1) * TILE])
        for side, grad_soft in enumerate(diagonal(product, low_half, means[place, :])):
            pair = 2 * tile + side
            own = slice(pair * 8, (pair + 1) * 8)
            group, column = pair // pairs, pair % pairs
            value = power[own] * grad_soft
            grad_score_ref[own, :] = value
            bands[
                group, column * 16 : (column + 1) * 16, column * LANES : (column + 1) * LANES
            ] = block_rows(value, low_half)
    for group in range(groups):
        result = nt(bands[group], edge_ref[:, group * GROUP : (group + 1) * GROUP])
        for half in range(width // LANES):
            pooled[half, pl.ds(base + group * group_rows, group_rows), :] = result[
                :, half * LANES : (half + 1) * LANES
            ]

    @pl.when(step == pl.num_programs(0) - 1)
    def _():
        grad_query = (gather_heads(pooled, kvq_ref[1], atoms) * scale).astype(BF16)
        grad_query_ref[...] = grad_query
        weight_grad[0] = tn(lookup_ref[HALO : HALO + atoms, :], grad_query)
        weight_grad[1] = tn(wide(pooled).astype(BF16), spread_q[...]) * scale
        weight_grad[2] = tn(pooled_ref[...], spread_g[...])
        me = index_ref[0]
        for offset, grads in enumerate((grads0, grads1, grads2, grads3)):
            owner = lax.bitwise_xor(me, offset)
            rows = pl.ds(pl.multiple_of(owner * quarter, 16), quarter)
            for which in range(3):
                grads[which * quarter : (which + 1) * quarter, :] = weight_grad[
                    which, rows, :
                ].astype(BF16)


def score_call(
    index, lookup, query, kvq, pooled, inverse, attended, grad_attended, power, edge, quarter
):
    atoms, width = query.shape
    blocks, _, edges = edge.shape
    head_rows = atoms * HEADS
    group_rows = GROUP // (edges // BLOCK) * HEADS
    groups = edges // GROUP
    full = lambda shape: pl.BlockSpec(shape, lambda b: (0,) * len(shape))
    whole = (lookup, query, kvq, pooled, inverse, attended, grad_attended)
    pair_block = pl.BlockSpec((None, PAIRS * HEADS, LANES), lambda b: (b, 0, 0))
    grads = (3 * quarter, width)
    return pl.pallas_call(
        functools.partial(score_kernel, quarter, (width // HEADS) ** -0.5),
        grid=(blocks,),
        out_shape=(
            jax.ShapeDtypeStruct((blocks, PAIRS * HEADS, LANES), F32),
            jax.ShapeDtypeStruct((blocks * groups, width, 2 * group_rows), BF16),
            jax.ShapeDtypeStruct((atoms, width), BF16),
        )
        + (jax.ShapeDtypeStruct(grads, BF16),) * 4,
        in_specs=[pl.BlockSpec(memory_space=pltpu.SMEM)]
        + [full(value.shape) for value in whole]
        + [pair_block, pl.BlockSpec((None, width, edges), lambda b: (b, 0, 0))],
        out_specs=(
            pair_block,
            pl.BlockSpec((groups, width, 2 * group_rows), lambda b: (b, 0, 0)),
            full((atoms, width)),
        )
        + (full(grads),) * 4,
        scratch_shapes=[
            pltpu.VMEM((head_rows, width), BF16),
            pltpu.VMEM((head_rows, width), BF16),
            pltpu.VMEM((head_rows, width), BF16),
            pltpu.VMEM((head_rows, width), BF16),
            pltpu.VMEM((head_rows, LANES), F32),
            pltpu.VMEM((groups, group_rows, GROUP), BF16),
            pltpu.VMEM((width // LANES, head_rows, LANES), F32),
            pltpu.VMEM((3, width, width), F32),
        ],
        compiler_params=pltpu.CompilerParams(vmem_limit_bytes=58 * 2**20),
        cost_estimate=pl.CostEstimate(
            flops=2 * atoms * edges // BLOCK * width * 256,
            bytes_accessed=2 * blocks * width * edges,
            transcendentals=0,
        ),
        name="score_backward",
    )(index, *whole, power, edge)


def edge_kernel(padded, gain_row, first_block, last_block, carried, final, *refs):
    refs = list(refs)
    take = lambda count: [refs.pop(0) for _ in range(count)]
    relative_ref, power_ref, grad_score_ref, mixed_ref, basis_hbm = take(5)
    before = take(2 if carried else 0)
    if final:
        index_ref, features_ref, before_ref, after_ref, grad_query_ref, kvq_ref = take(6)
        grad_residual_ref, sums_ref = take(2)
        small = take(4)
        grad_own_ref, grad_lower_ref, grad_upper_ref = take(3)
        grads_refs = take(4)
    grad_rbf, grad_lookup = take(2)
    bands, grad_edge, phi_buffer, semaphores = take(4)
    block = pl.program_id(0) + first_block
    width, edges = grad_edge.shape
    window = BLOCK + 2 * HALO
    low_half = lax.broadcasted_iota(jnp.int32, (1, LANES), 1) < LANES // 2
    group_rows = bands.shape[1] // 2
    groups = edges // GROUP
    pairs = GROUP // LANES

    @pl.when(block == first_block)
    def _():
        fetch(basis_hbm, phi_buffer, semaphores, block, window).start()
        bands[...] = jnp.zeros_like(bands)
        if carried:
            grad_rbf[...] = before[0][...]
            grad_lookup[...] = before[1][...]
        else:
            grad_rbf[...] = jnp.zeros_like(grad_rbf)
            grad_lookup[...] = jnp.zeros_like(grad_lookup)

    power = power_ref[...].astype(F32)
    grad_score = grad_score_ref[...]
    for pair in range(PAIRS):
        group, column = pair // pairs, pair % pairs
        own = slice(pair * 8, (pair + 1) * 8)
        lanes = slice(column * LANES, (column + 1) * LANES)
        for start, value in ((0, grad_score[own]), (group_rows, power[own])):
            row = start + column * 16
            bands[group, row : row + 16, lanes] = block_rows(value, low_half)
    for group in range(groups):
        part = slice(group * GROUP, (group + 1) * GROUP)
        grad_edge[:, part] = nn(mixed_ref[group], bands[group]).astype(BF16)
    phi = phi_buffer.at[lax.rem(block, 2)]
    write_onehot(relative_ref, window, phi)
    fetch_next(basis_hbm, phi_buffer, semaphores, block, last_block, window)
    total = nt(phi[...], grad_edge[...])
    grad_lookup[pl.ds(pl.multiple_of(block * BLOCK, BLOCK), window), :] += total[:window]
    grad_rbf[...] += total[window:]

    if not final:
        return

    @pl.when(block == last_block - 1)
    def _():
        atoms = features_ref.shape[0]
        grad_lookup[HALO : HALO + atoms, :] += nt(grad_query_ref[...], kvq_ref[0])
        gain = vector_of(small, gain_row)
        grad_gain = jnp.zeros((1, width), F32)
        places = (
            (before_ref, 0, grad_lower_ref),
            (features_ref, HALO, grad_own_ref),
            (after_ref, HALO + atoms, grad_upper_ref),
        )
        for ref, start, out in places:
            normed, inverse = rms(ref[...].astype(F32))
            grad = grad_lookup[start : start + ref.shape[0], :]
            grad_gain = grad_gain + jnp.sum(grad * normed, 0, keepdims=True)
            back = norm_back(grad * gain, normed, inverse)
            if start == HALO:
                back = back + grad_residual_ref[...]
            out[...] = back.astype(out.dtype)
        vectors = jnp.concatenate([grad_gain, sums_ref[1:8, :], jnp.zeros((8, width), F32)], 0)
        after_rbf = round_up(padded, 16)
        rest = jnp.zeros((after_rbf - padded, width), F32)
        me = index_ref[0]
        for offset, grads in enumerate(grads_refs):
            owner = lax.bitwise_xor(me, offset)
            rbf = grad_rbf[pl.ds(pl.multiple_of(owner * padded, 8), padded), :]
            grads[:after_rbf, :] = jnp.concatenate([rbf, rest], 0).astype(BF16)
            grads[after_rbf:, :] = vectors.astype(BF16)


def edge_call(arrays, basis, carry, last, padded, gain_row, first_block, last_block):
    blocks, rows, edges = basis.shape
    width = arrays[3].shape[1]
    groups = edges // GROUP
    group_rows = GROUP // (edges // BLOCK) * HEADS
    table = blocks * BLOCK + 2 * HALO
    window = BLOCK + 2 * HALO
    full = lambda shape: pl.BlockSpec(shape, lambda b: (0,) * len(shape))
    here = lambda b: (b + first_block, 0, 0)
    in_specs = [
        pl.BlockSpec((None, PAIRS, LANES), here),
        pl.BlockSpec((None, PAIRS * HEADS, LANES), here),
        pl.BlockSpec((None, PAIRS * HEADS, LANES), here),
        pl.BlockSpec((groups, width, 2 * group_rows), here),
        pl.BlockSpec(memory_space=pl.ANY),
    ]
    operands = [*arrays, basis]
    sums = [(rows, width), (table, width)]
    if carry is not None:
        in_specs += [full(value.shape) for value in carry]
        operands += list(carry)
    scratch = [
        pltpu.VMEM((groups, 2 * group_rows, GROUP), BF16),
        pltpu.VMEM((width, edges), BF16),
        pltpu.VMEM((2, window + rows, edges), BF16),
        pltpu.SemaphoreType.DMA((2,)),
    ]
    if last is None:
        shapes = [(shape, F32) for shape in sums]
    else:
        in_specs += [pl.BlockSpec(memory_space=pltpu.SMEM)]
        in_specs += [full(value.shape) for value in last[1:]]
        operands += list(last)
        grads = (round_up(padded, 16) + 16, width)
        shapes = [((blocks * BLOCK, width), F32)] + [((HALO, width), BF16)] * 2 + [(grads, BF16)] * 4
        scratch = [pltpu.VMEM(shape, F32) for shape in sums] + scratch
    return pl.pallas_call(
        functools.partial(
            edge_kernel, padded, gain_row, first_block, last_block, carry is not None, last is not None
        ),
        grid=(last_block - first_block,),
        out_shape=[jax.ShapeDtypeStruct(shape, dtype) for shape, dtype in shapes],
        in_specs=in_specs,
        out_specs=[full(shape) for shape, _ in shapes],
        scratch_shapes=scratch,
        compiler_params=pltpu.CompilerParams(vmem_limit_bytes=58 * 2**20),
        cost_estimate=pl.CostEstimate(
            flops=2 * (last_block - first_block) * edges * width * (rows + window + 256),
            bytes_accessed=2 * (last_block - first_block) * rows * edges,
            transcendentals=0,
        ),
        name="edge_backward",
    )(*operands)


def large_kernel(first, second, gate, up, down, out):
    total = lambda rows: first[rows, :].astype(F32) + second[rows, :].astype(F32)
    quarter, width = out.shape
    row = 0
    for ref in (gate, up):
        for part in range(ref.shape[1] // width):
            ref[:, part * width : (part + 1) * width] = total(slice(row, row + quarter))
            row += quarter
    for ref in (down, out):
        ref[...] = total(slice(row, row + ref.shape[0]))
        row += ref.shape[0]


def large_call(first, second, quarter, hidden, down_rows):
    width = first.shape[1]
    vmem = pl.BlockSpec(memory_space=pltpu.VMEM)
    shapes = ((quarter, hidden), (quarter, hidden), (down_rows, width), (quarter, width))
    return pl.pallas_call(
        large_kernel,
        out_shape=[jax.ShapeDtypeStruct(shape, F32) for shape in shapes],
        in_specs=[vmem] * 2,
        out_specs=[vmem] * 4,
        name="feed_forward_results",
    )(first, second)


def small_kernel(
    index_ref,
    score_first,
    score_second,
    edge_first,
    edge_second,
    grad_own,
    from_lower,
    from_upper,
    rbf,
    query,
    key,
    value,
    gain_attn,
    gain_ffn,
    readout,
    features,
):
    quarter = query.shape[0]
    width = query.shape[1]
    for which, ref in enumerate((query, key, value)):
        rows = slice(which * quarter, (which + 1) * quarter)
        ref[...] = score_first[rows, :].astype(F32) + score_second[rows, :].astype(F32)
    total = edge_first[...].astype(F32) + edge_second[...].astype(F32)
    rbf[...] = total[: rbf.shape[0]]
    start = edge_first.shape[0] - 16
    me = index_ref[0]
    for which, ref in enumerate((gain_attn, gain_ffn, readout)):
        row = total[start + which : start + which + 1]
        picked = jnp.zeros((1, quarter), F32)
        for owner in range(width // quarter):
            piece = row[:, owner * quarter : (owner + 1) * quarter]
            picked = picked + jnp.where(me == owner, piece, 0.0)
        ref[...] = picked
    features[...] = grad_own[...]
    features[:HALO, :] += from_lower[...].astype(F32)
    features[features.shape[0] - HALO :, :] += from_upper[...].astype(F32)


def small_call(index, score, edge, grad_own, from_lower, from_upper, shard, quarter):
    width = grad_own.shape[1]
    vmem = pl.BlockSpec(memory_space=pltpu.VMEM)
    shapes = [(shard, width)] + [(quarter, width)] * 3 + [(1, quarter)] * 3 + [grad_own.shape]
    return pl.pallas_call(
        small_kernel,
        out_shape=[jax.ShapeDtypeStruct(shape, F32) for shape in shapes],
        in_specs=[pl.BlockSpec(memory_space=pltpu.SMEM)] + [vmem] * 7,
        out_specs=[vmem] * 8,
        name="edge_results",
    )(index, *score, *edge, grad_own, from_lower, from_upper)


def exchange(value, axis, offset):
    size = lax.axis_size(axis)
    return lax.ppermute(value, axis, [(i, i ^ offset) for i in range(size)])


def shifted(value, by):
    axes = ("space", "wt")
    size = lax.axis_size(axes)
    pairs = [(i, i + by) for i in range(size) if 0 <= i + by < size]
    return lax.ppermute(value, axes, pairs)


def gathered(value):
    return [value] + [exchange(value, "wt", offset) for offset in range(1, lax.axis_size("wt"))]


def added(*values):
    total = values[0].astype(F32)
    for value in values[1:]:
        total = total + value.astype(F32)
    return total.astype(values[0].dtype)


class Reduction:
    def __init__(self, chunks):
        self.offsets = [1 << bit for bit in range(lax.axis_size("space").bit_length() - 1)]
        self.terms = [chunks[0]] + [
            exchange(chunk, "wt", offset) for offset, chunk in enumerate(chunks[1:], 1)
        ]

    def add(self):
        if self.offsets:
            self.terms = [added(*self.terms)]

    def send(self):
        if self.offsets:
            self.terms.append(exchange(self.terms[0], "space", self.offsets.pop(0)))

    def finish(self):
        while self.offsets:
            self.add()
            self.send()
        return self.terms


def between(reductions, value):
    terms = [reduction.terms for reduction in reductions]
    terms, value = lax.optimization_barrier((terms, value))
    for reduction, own in zip(reductions, terms):
        reduction.terms = list(own)
        reduction.add()
    terms = [reduction.terms for reduction in reductions]
    terms, value = lax.optimization_barrier((terms, value))
    for reduction, own in zip(reductions, terms):
        reduction.terms = list(own)
        reduction.send()
    return value


SPLIT = (2, 2, 2)


def local(
    features,
    distances,
    neighbours,
    counts,
    rbf_weight,
    query_weight,
    key_weight,
    value_weight,
    out_weight,
    gate_weight,
    up_weight,
    down_weight,
    attn_gain,
    ffn_gain,
    readout,
    grad_out,
    grad_energy,
):
    members = lax.axis_size("wt")
    atoms, width = features.shape
    shard = rbf_weight.shape[0]
    padded = round_up(shard, 8)
    gain_row = round_up(shard, 16) + 3 * query_weight.shape[0]
    quarter = query_weight.shape[0]
    hidden = gate_weight.shape[1]
    index = lax.axis_index("wt").astype(jnp.int32)[None]

    small, large, initial, final = pack_call(
        index,
        rbf_weight,
        query_weight,
        key_weight,
        value_weight,
        out_weight,
        gate_weight,
        up_weight,
        down_weight,
        attn_gain[None],
        ffn_gain[None],
        readout[None],
        features,
    )
    small_all = gathered(small)
    before = shifted(final, 1)
    after = shifted(initial, -1)
    basis, relative = basis_call(
        distances.T, neighbours.T, shard, padded, members, members * shard
    )

    large, basis = lax.optimization_barrier((large, basis))
    large_all = gathered(large)

    edge, power, inverse, pooled, attended, lookup, query, kvq = forward_call(
        index, counts, features, before, after, small_all, relative, basis, padded, quarter
    )
    outputs, energy, grad_residual, grad_attended, sums, *large_grads = ffn_call(
        index,
        features,
        attended,
        grad_out,
        grad_energy[None, :],
        small_all,
        large_all,
        hidden,
        quarter,
        gain_row,
    )
    grad_score, mixed, grad_query, *score_grads = score_call(
        index, lookup, query, kvq, pooled, inverse, attended, grad_attended, power, edge, quarter
    )
    large_sum, score_sum = Reduction(large_grads), Reduction(score_grads)
    carry, block = None, 0
    last = (index, features, before, after, grad_query, kvq, grad_residual, sums, *small_all)
    for count in SPLIT:
        if carry is None:
            grad_score = between([large_sum], grad_score)
        else:
            carry = between([large_sum, score_sum], carry)
        final = block + count == basis.shape[0]
        carry = edge_call(
            (relative, power, grad_score, mixed),
            basis,
            carry,
            last if final else None,
            padded,
            gain_row,
            block,
            block + count,
        )
        block += count
    grad_own, grad_lower, grad_upper, *edge_grads = carry
    edge_sum = Reduction(edge_grads)
    from_upper = shifted(grad_lower, -1)
    from_lower = shifted(grad_upper, 1)
    score_sum = score_sum.finish()
    results = large_call(*large_sum.finish(), quarter, hidden, down_weight.shape[0])
    grad_gate, grad_up, grad_down, grad_out_w = between([edge_sum], results)
    edge_sum = edge_sum.finish()
    grad_rbf, grad_q, grad_k, grad_v, grad_attn, grad_ffn, grad_read, grad_features = small_call(
        index, score_sum, edge_sum, grad_own, from_lower, from_upper, shard, quarter
    )
    return (
        outputs,
        energy[0],
        grad_features,
        grad_rbf,
        grad_q,
        grad_k,
        grad_v,
        grad_out_w,
        grad_gate,
        grad_up,
        grad_down,
        grad_attn[0],
        grad_ffn[0],
        grad_read[0],
    )


def solution(mesh):
    rows = P(("space", "wt"), None)
    line = P(("space", "wt"))
    in_specs = (rows, rows, rows, line) + (P("wt", None),) * 8 + (P("wt"),) * 3 + (rows, line)
    out_specs = (rows, line, rows) + (P("wt", None),) * 8 + (P("wt"),) * 3
    return jax.shard_map(local, mesh=mesh, in_specs=in_specs, out_specs=out_specs, check_vma=False)
```

time: 220 us -> 174 us (0.79)
  the two profiles are of different devices: /device:TPU:0 before, /device:TPU:7 now
where the time goes in v2:
time: 174 us; the launch traced here: 173 us
  Pallas kernels  111 us (64%)
  starting transfers between devices  35.1 us (20%)
  waiting for transfers between devices  16.7 us (10%)
  local copies, waits for them, and re-layouts  6.89 us (4%)
  other arithmetic  2.12 us (1%)
    pallas_call x1, Pallas kernels, forward_call(): pl.pallas_call(functools.partial(forward_kernel, padded, quarter, (width...  32.5 us
    pallas_call x3, Pallas kernels, edge_call(): pl.pallas_call(functools.partial(edge_kernel, padded, gain_row, first_blo...  30.7 us
    pallas_call x1, Pallas kernels, score_call(): pl.pallas_call(functools.partial(score_kernel, quarter, (width // HEADS)...  19.8 us
    ppermute x24, starting transfers between devices, exchange(): return lax.ppermute(value, axis, [(i, i ^ offset) for i in range(size)])  19.3 us
    ppermute x4, starting transfers between devices, shifted(): return lax.ppermute(value, axes, pairs)  15.8 us
    pallas_call x1, Pallas kernels, basis_call(): pl.pallas_call(functools.partial(basis_kernel, shard, padded, 2.0 * CUTOF...  15.3 us
    ppermute x24, waiting for transfers between devices, exchange(): return lax.ppermute(value, axis, [(i, i ^ offset) for i in range(size)])  11.8 us
    pallas_call x1, Pallas kernels, ffn_call(): pl.pallas_call(functools.partial(ffn_kernel, quarter, row), out_shape=(ja...  6.87 us
  transfers between devices with their start and end apart: 28, of which 6 were waited for; matrix products, arithmetic and copies ran while one was open for 1% of the time, Pallas kernels for 58%

profile of v2, /device:TPU:7, one launch (start us, length us, event | category | flops | bytes accessed | tf_op | source)
XLA Modules:
  0.0 173.3 jit_solution(18271224246830436033)
XLA Ops:
  0.7 2.1 %pack_weights.1 = (bf16[368,256]{1,0:T(8,128)(2,1)}, bf16[832,256]{1,0:T(8,128)(2,1)}, bf16[96,256]{1,0:T(8,128)(2,1)}, bf16[96,256]{1,0:T(8,128)(2,1)}) custom-call(s32[1]{0:T(128)} %bitcast.index_ref.refs_7_, bf16[150,256]{1,0:T(8,128)(2,1)} %rbf_ref.1, bf16[64,256]{1,0:T(8,128)(2,1)} %query_ref.1, bf16[64,256]{1,0:T(8,128)(2,1)} %key_ref.1, ...), custom_call_target="tpu_custom_call" | custom-call | bytes 2097152 | tf_op jit(solution)/shard_map/pack_weights/pallas_call | solution.py:204
  4.9 3.4 %collective-permute-start = (bf16[96,256]{1,0:T(8,128)(2,1)}, bf16[96,256]{1,0:T(8,128)(2,1)S(1)}, u32[]{:S(2)}, u32[]{:S(2)}) collective-permute-start(bf16[96,256]{1,0:T(8,128)(2,1)} %get-tuple-element.111), channel_id=1, source_target_pairs={{0,1},{1,2},{2,3},{3,4},{4,5},{5,6},{6,7},{7,8},{8,9},{9,10},{10,1... | collective-permute-start | bytes 147464 | tf_op jit(solution)/shard_map/ppermute | solution.py:988
  8.3 1.9 %collective-permute-start.1 = (bf16[96,256]{1,0:T(8,128)(2,1)}, bf16[96,256]{1,0:T(8,128)(2,1)S(1)}, u32[]{:S(2)}, u32[]{:S(2)}) collective-permute-start(bf16[96,256]{1,0:T(8,128)(2,1)} %get-tuple-element.112), channel_id=1, source_target_pairs={{1,0},{2,1},{3,2},{4,3},{5,4},{6,5},{7,6},{8,7},{9,8},{10,9},{11,1... | collective-permute-start | bytes 147464 | tf_op jit(solution)/shard_map/ppermute | solution.py:988
  13.3 15.3 %radial_basis.1 = (bf16[6,608,4096]{2,1,0:T(8,128)(2,1)}, f32[6,32,128]{2,1,0:T(8,128)S(1)}) custom-call(f32[64,384]{1,0:T(8,128)S(1)} %bitcast.9, s32[64,384]{1,0:T(8,128)S(1)} %bitcast.10), custom_call_target="tpu_custom_call" | custom-call | flops 119537664 | bytes 29884416 | tf_op jit(solution)/shard_map/radial_basis/pallas_call | solution.py:256
  29.2 1.7 %collective-permute-start.7 = (bf16[832,256]{1,0:T(8,128)(2,1)S(1)}, bf16[832,256]{1,0:T(8,128)(2,1)S(1)}, u32[]{:S(2)}, u32[]{:S(2)}) collective-permute-start(bf16[832,256]{1,0:T(8,128)(2,1)S(1)} %copy-done.19), channel_id=1, source_target_pairs={{0,3},{1,2},{2,1},{3,0},{4,7},{5,6},{6,5},{7,4},{8,11},{9,10},{10,... | collective-permute-start | bytes 1277960 | tf_op jit(solution)/shard_map/ppermute | solution.py:981
  32.2 32.5 %attention_forward.1 = (bf16[6,256,4096]{2,1,0:T(8,128)(2,1)}, bf16[6,256,128]{2,1,0:T(8,128)(2,1)}, f32[3072,128]{1,0:T(8,128)}, bf16[3072,256]{1,0:T(8,128)(2,...) custom-call(s32[1]{0:T(128)} %bitcast.index_ref.refs_7_, ...), custom_call_target="tpu_custom_call" | custom-call | flops 11676942336 | bytes 42467328 | tf_op jit(solution)/shard_map/attention_forward/pallas_call | solution.py:419
  65.8 6.9 %feed_forward.1 = (f32[384,256]{1,0:T(8,128)}, f32[1,384]{1,0:T(1,128)}, f32[384,256]{1,0:T(8,128)}, bf16[384,256]{1,0:T(8,128)(2,1)}, f32[8,256]{1,0:T(8,128)},...) custom-call(s32[1]{0:T(128)} %bitcast.index_ref.refs_7_, ...), custom_call_target="tpu_custom_call" | custom-call | flops 1811939328 | bytes 8388608 | tf_op jit(solution)/shard_map/feed_forward/pallas_call | solution.py:578
  74.8 19.8 %score_backward.1 = (f32[6,256,128]{2,1,0:T(8,128)}, bf16[24,256,256]{2,1,0:T(8,128)(2,1)}, bf16[384,256]{1,0:T(8,128)(2,1)}, bf16[192,256]{1,0:T(8,128)(2,1)}, ...) custom-call(s32[1]{0:T(128)} %bitcast.index_ref.refs_7_, ...), custom_call_target="tpu_custom_call" | custom-call | flops 3221225472 | bytes 12582912 | tf_op jit(solution)/shard_map/score_backward/pallas_call | solution.py:724
  97.3 9.7 %edge_backward.3 = (f32[608,256]{1,0:T(8,128)}, f32[576,256]{1,0:T(8,128)}) custom-call(f32[6,32,128]{2,1,0:T(8,128)} %copy-done, bf16[6,256,128]{2,1,0:T(8,128)(2,1)} %get-tuple-element.132.power_ref.refs_1_, f32[6,256,128]{2,1,0:T(8,128)} %get-tuple-element.145.refs_2_, bf16[24,256,256]{2,1,0:T(8,128)(2,1)} %get-tuple-element.146.refs_3_, ...), custom_call_target="tpu_custom_call" | custom-call | flops 4697620480 | bytes 9961472 | tf_op jit(solution)/shard_map/edge_backward/pallas_call | solution.py:882
  107.0 1.6 collective-permute-done.11
  109.1 2.2 %collective-permute-start.15 = (bf16[832,256]{1,0:T(8,128)(2,1)S(1)}, bf16[832,256]{1,0:T(8,128)(2,1)S(1)}, u32[]{:S(2)}, u32[]{:S(2)}) collective-permute-start(bf16[832,256]{1,0:T(8,128)(2,1)S(1)} %add_convert_fusion.1), channel_id=1, source_target_pairs={{0,8},{4,12},{8,0},{12,4},{16,24},{20,28},{24,16},{28,20},{1,9},{5... | collective-permute-start | bytes 1277960 | tf_op jit(solution)/shard_map/ppermute | solution.py:981
  111.3 10.0 %edge_backward.4 = (f32[608,256]{1,0:T(8,128)}, f32[576,256]{1,0:T(8,128)}) custom-call(f32[6,32,128]{2,1,0:T(8,128)} %copy-done, bf16[6,256,128]{2,1,0:T(8,128)(2,1)} %get-tuple-element.132.power_ref.refs_1_, f32[6,256,128]{2,1,0:T(8,128)} %get-tuple-element.145.refs_2_, bf16[24,256,256]{2,1,0:T(8,128)(2,1)} %get-tuple-element.146.refs_3_, ...), custom_call_target="tpu_custom_call" | custom-call | flops 4697620480 | bytes 9961472 | tf_op jit(solution)/shard_map/edge_backward/pallas_call | solution.py:882
  121.5 2.4 %collective-permute-start.22 = (bf16[832,256]{1,0:T(8,128)(2,1)S(1)}, bf16[832,256]{1,0:T(8,128)(2,1)S(1)}, u32[]{:S(2)}, u32[]{:S(2)}) collective-permute-start(bf16[832,256]{1,0:T(8,128)(2,1)S(1)} %add_convert_fusion.first), channel_id=1, source_target_pairs={{0,16},{4,20},{8,24},{12,28},{16,0},{20,4},{24,8},{28,12},{1,17},{... | collective-permute-start | bytes 1277960 | tf_op jit(solution)/shard_map/ppermute | solution.py:981
  123.9 11.1 %edge_backward.5 = (f32[384,256]{1,0:T(8,128)}, bf16[96,256]{1,0:T(8,128)(2,1)}, bf16[96,256]{1,0:T(8,128)(2,1)}, bf16[176,256]{1,0:T(8,128)(2,1)}, bf16[176,256...) custom-call(f32[6,32,128]{2,1,0:T(8,128)} %copy-done, ...), custom_call_target="tpu_custom_call" | custom-call | flops 4697620480 | bytes 9961472 | tf_op jit(solution)/shard_map/edge_backward/pallas_call | solution.py:882
  135.0 1.6 collective-permute-start.19
  138.3 5.0 %collective-permute-done.22.second = bf16[832,256]{1,0:T(8,128)(2,1)S(1)} collective-permute-done((bf16[832,256]{1,0:T(8,128)(2,1)S(1)}, bf16[832,256]{1,0:T(8,128)(2,1)S(1)}, u32[]{:S(2)}, u32[]{:S(2)}) %collective-permute-start.22) | collective-permute-done | bytes 426016 | tf_op jit(solution)/shard_map/ppermute | solution.py:981
  144.1 2.1 %feed_forward_results.1 = (f32[64,1024]{1,0:T(8,128)}, f32[64,1024]{1,0:T(8,128)}, f32[256,256]{1,0:T(8,128)}, f32[64,256]{1,0:T(8,128)}) custom-call(bf16[832,256]{1,0:T(8,128)(2,1)} %copy-done.3, bf16[832,256]{1,0:T(8,128)(2,1)} %copy-done.5), custom_call_target="tpu_custom_call" | custom-call | tf_op jit(solution)/shard_map/feed_forward_results/pallas_call | solution.py:918
  147.5 3.0 %collective-permute-done.23 = bf16[176,256]{1,0:T(8,128)(2,1)S(1)} collective-permute-done((bf16[176,256]{1,0:T(8,128)(2,1)S(1)}, bf16[176,256]{1,0:T(8,128)(2,1)S(1)}, u32[]{:S(2)}, u32[]{:S(2)}) %collective-permute-start.23) | collective-permute-done | bytes 90144 | tf_op jit(solution)/shard_map/ppermute | solution.py:981
  151.3 1.3 collective-permute-start.18
  152.6 1.5 collective-permute-done.24
  154.5 8.6 %collective-permute-start.26 = (bf16[96,256]{1,0:T(8,128)(2,1)}, bf16[96,256]{1,0:T(8,128)(2,1)S(1)}, u32[]{:S(2)}, u32[]{:S(2)}) collective-permute-start(bf16[96,256]{1,0:T(8,128)(2,1)} %get-tuple-element.194), channel_id=1, source_target_pairs={{0,1},{1,2},{2,3},{3,4},{4,5},{5,6},{6,7},{7,8},{8,9},{9,10},{10,1... | collective-permute-start | bytes 147464 | tf_op jit(solution)/shard_map/ppermute | solution.py:988
  163.1 1.9 %collective-permute-start.27 = (bf16[96,256]{1,0:T(8,128)(2,1)}, bf16[96,256]{1,0:T(8,128)(2,1)S(1)}, u32[]{:S(2)}, u32[]{:S(2)}) collective-permute-start(bf16[96,256]{1,0:T(8,128)(2,1)} %get-tuple-element.195), channel_id=1, source_target_pairs={{1,0},{2,1},{3,2},{4,3},{5,4},{6,5},{7,6},{8,7},{9,8},{10,9},{11,1... | collective-permute-start | bytes 147464 | tf_op jit(solution)/shard_map/ppermute | solution.py:988
  165.6 4.9 %collective-permute-done.27.from_upper = bf16[96,256]{1,0:T(8,128)(2,1)S(1)} collective-permute-done((bf16[96,256]{1,0:T(8,128)(2,1)}, bf16[96,256]{1,0:T(8,128)(2,1)S(1)}, u32[]{:S(2)}, u32[]{:S(2)}) %collective-permute-start.27) | collective-permute-done | bytes 49184 | tf_op jit(solution)/shard_map/ppermute | solution.py:988
  171.2 2.1 %edge_results.1 = (f32[150,256]{1,0:T(8,128)}, f32[64,256]{1,0:T(8,128)}, f32[64,256]{1,0:T(8,128)}, f32[64,256]{1,0:T(8,128)}, f32[1,64]{1,0:T(1,128)}, /*index...) custom-call(s32[1]{0:T(128)} %bitcast.index_ref.refs_7_, bf16[192,256]{1,0:T(8,128)(2,1)} %copy-done.6, ...), custom_call_target="tpu_custom_call" | custom-call | tf_op jit(solution)/shard_map/edge_results/pallas_call | solution.py:970
  (99 shorter events, 19.8 us)
Async XLA Ops:
  2.8 28.5 %collective-permute-start.4 = (bf16[368,256]{1,0:T(8,128)(2,1)}, bf16[368,256]{1,0:T(8,128)(2,1)S(1)}, u32[]{:S(2)}, u32[]{:S(2)}) collective-permute-start(bf16[368,256]{1,0:T(8,128)(2,1)} %get-tuple-element.113.pack0.small0.refs_15_), channel_id=1, source_target_pairs={{0,3},{1,2},{2,1},{3,0},{4,7},{5,6},{6,5},{7,4},{8,11},{9,10},{10,... | collective-permute-start | bytes 565256 | tf_op jit(solution)/shard_map/ppermute | solution.py:981
  3.6 27.9 %collective-permute-start.3 = (bf16[368,256]{1,0:T(8,128)(2,1)}, bf16[368,256]{1,0:T(8,128)(2,1)S(1)}, u32[]{:S(2)}, u32[]{:S(2)}) collective-permute-start(bf16[368,256]{1,0:T(8,128)(2,1)} %get-tuple-element.113.pack0.small0.refs_15_), channel_id=1, source_target_pairs={{0,2},{1,3},{2,0},{3,1},{4,6},{5,7},{6,4},{7,5},{8,10},{9,11},{10,... | collective-permute-start | bytes 565256 | tf_op jit(solution)/shard_map/ppermute | solution.py:981
  4.8 26.7 %collective-permute-start.2 = (bf16[368,256]{1,0:T(8,128)(2,1)}, bf16[368,256]{1,0:T(8,128)(2,1)S(1)}, u32[]{:S(2)}, u32[]{:S(2)}) collective-permute-start(bf16[368,256]{1,0:T(8,128)(2,1)} %get-tuple-element.113.pack0.small0.refs_15_), channel_id=1, source_target_pairs={{0,1},{1,0},{2,3},{3,2},{4,5},{5,4},{6,7},{7,6},{8,9},{9,8},{10,11... | collective-permute-start | bytes 565256 | tf_op jit(solution)/shard_map/ppermute | solution.py:981
  4.9 24.3 %collective-permute-start = (bf16[96,256]{1,0:T(8,128)(2,1)}, bf16[96,256]{1,0:T(8,128)(2,1)S(1)}, u32[]{:S(2)}, u32[]{:S(2)}) collective-permute-start(bf16[96,256]{1,0:T(8,128)(2,1)} %get-tuple-element.111), channel_id=1, source_target_pairs={{0,1},{1,2},{2,3},{3,4},{4,5},{5,6},{6,7},{7,8},{8,9},{9,10},{10,1... | collective-permute-start | bytes 147464 | tf_op jit(solution)/shard_map/ppermute | solution.py:988
  8.3 22.6 %collective-permute-start.1 = (bf16[96,256]{1,0:T(8,128)(2,1)}, bf16[96,256]{1,0:T(8,128)(2,1)S(1)}, u32[]{:S(2)}, u32[]{:S(2)}) collective-permute-start(bf16[96,256]{1,0:T(8,128)(2,1)} %get-tuple-element.112), channel_id=1, source_target_pairs={{1,0},{2,1},{3,2},{4,3},{5,4},{6,5},{7,6},{8,7},{9,8},{10,9},{11,1... | collective-permute-start | bytes 147464 | tf_op jit(solution)/shard_map/ppermute | solution.py:988
  29.2 35.4 %collective-permute-start.7 = (bf16[832,256]{1,0:T(8,128)(2,1)S(1)}, bf16[832,256]{1,0:T(8,128)(2,1)S(1)}, u32[]{:S(2)}, u32[]{:S(2)}) collective-permute-start(bf16[832,256]{1,0:T(8,128)(2,1)S(1)} %copy-done.19), channel_id=1, source_target_pairs={{0,3},{1,2},{2,1},{3,0},{4,7},{5,6},{6,5},{7,4},{8,11},{9,10},{10,... | collective-permute-start | bytes 1277960 | tf_op jit(solution)/shard_map/ppermute | solution.py:981
  31.0 33.7 %collective-permute-start.6 = (bf16[832,256]{1,0:T(8,128)(2,1)S(1)}, bf16[832,256]{1,0:T(8,128)(2,1)S(1)}, u32[]{:S(2)}, u32[]{:S(2)}) collective-permute-start(bf16[832,256]{1,0:T(8,128)(2,1)S(1)} %copy-done.19), channel_id=1, source_target_pairs={{0,2},{1,3},{2,0},{3,1},{4,6},{5,7},{6,4},{7,5},{8,10},{9,11},{10,... | collective-permute-start | bytes 1277960 | tf_op jit(solution)/shard_map/ppermute | solution.py:981
  31.3 33.4 %collective-permute-start.5 = (bf16[832,256]{1,0:T(8,128)(2,1)S(1)}, bf16[832,256]{1,0:T(8,128)(2,1)S(1)}, u32[]{:S(2)}, u32[]{:S(2)}) collective-permute-start(bf16[832,256]{1,0:T(8,128)(2,1)S(1)} %copy-done.19), channel_id=1, source_target_pairs={{0,1},{1,0},{2,3},{3,2},{4,5},{5,4},{6,7},{7,6},{8,9},{9,8},{10,11... | collective-permute-start | bytes 1277960 | tf_op jit(solution)/shard_map/ppermute | solution.py:981
  72.7 23.2 %collective-permute-start.8 = (bf16[832,256]{1,0:T(8,128)(2,1)}, bf16[832,256]{1,0:T(8,128)(2,1)S(1)}, u32[]{:S(2)}, u32[]{:S(2)}) collective-permute-start(bf16[832,256]{1,0:T(8,128)(2,1)} %get-tuple-element.123), channel_id=1, source_target_pairs={{0,1},{1,0},{2,3},{3,2},{4,5},{5,4},{6,7},{7,6},{8,9},{9,8},{10,11... | collective-permute-start | bytes 1277960 | tf_op jit(solution)/shard_map/ppermute | solution.py:981
  73.0 23.8 %collective-permute-start.9 = (bf16[832,256]{1,0:T(8,128)(2,1)}, bf16[832,256]{1,0:T(8,128)(2,1)S(1)}, u32[]{:S(2)}, u32[]{:S(2)}) collective-permute-start(bf16[832,256]{1,0:T(8,128)(2,1)} %get-tuple-element.124), channel_id=1, source_target_pairs={{0,2},{1,3},{2,0},{3,1},{4,6},{5,7},{6,4},{7,5},{8,10},{9,11},{10,... | collective-permute-start | bytes 1277960 | tf_op jit(solution)/shard_map/ppermute | solution.py:981
  74.2 22.7 %collective-permute-start.10 = (bf16[832,256]{1,0:T(8,128)(2,1)}, bf16[832,256]{1,0:T(8,128)(2,1)S(1)}, u32[]{:S(2)}, u32[]{:S(2)}) collective-permute-start(bf16[832,256]{1,0:T(8,128)(2,1)} %get-tuple-element.125), channel_id=1, source_target_pairs={{0,3},{1,2},{2,1},{3,0},{4,7},{5,6},{6,5},{7,4},{8,11},{9,10},{10,... | collective-permute-start | bytes 1277960 | tf_op jit(solution)/shard_map/ppermute | solution.py:981
  94.6 12.4 %collective-permute-start.12 = (bf16[192,256]{1,0:T(8,128)(2,1)}, bf16[192,256]{1,0:T(8,128)(2,1)S(1)}, u32[]{:S(2)}, u32[]{:S(2)}) collective-permute-start(bf16[192,256]{1,0:T(8,128)(2,1)} %get-tuple-element.142), channel_id=1, source_target_pairs={{0,1},{1,0},{2,3},{3,2},{4,5},{5,4},{6,7},{7,6},{8,9},{9,8},{10,11... | collective-permute-start | bytes 294920 | tf_op jit(solution)/shard_map/ppermute | solution.py:981
  94.7 12.3 %collective-permute-start.13 = (bf16[192,256]{1,0:T(8,128)(2,1)}, bf16[192,256]{1,0:T(8,128)(2,1)S(1)}, u32[]{:S(2)}, u32[]{:S(2)}) collective-permute-start(bf16[192,256]{1,0:T(8,128)(2,1)} %get-tuple-element.143), channel_id=1, source_target_pairs={{0,2},{1,3},{2,0},{3,1},{4,6},{5,7},{6,4},{7,5},{8,10},{9,11},{10,... | collective-permute-start | bytes 294920 | tf_op jit(solution)/shard_map/ppermute | solution.py:981
  95.9 11.2 %collective-permute-start.14 = (bf16[192,256]{1,0:T(8,128)(2,1)}, bf16[192,256]{1,0:T(8,128)(2,1)S(1)}, u32[]{:S(2)}, u32[]{:S(2)}) collective-permute-start(bf16[192,256]{1,0:T(8,128)(2,1)} %get-tuple-element.144), channel_id=1, source_target_pairs={{0,3},{1,2},{2,1},{3,0},{4,7},{5,6},{6,5},{7,4},{8,11},{9,10},{10,... | collective-permute-start | bytes 294920 | tf_op jit(solution)/shard_map/ppermute | solution.py:981
  97.0 11.6 %collective-permute-start.11 = (bf16[832,256]{1,0:T(8,128)(2,1)S(1)}, bf16[832,256]{1,0:T(8,128)(2,1)S(1)}, u32[]{:S(2)}, u32[]{:S(2)}) collective-permute-start(bf16[832,256]{1,0:T(8,128)(2,1)S(1)} %add_convert_fusion.2), channel_id=1, source_target_pairs={{0,4},{4,0},{8,12},{12,8},{16,20},{20,16},{24,28},{28,24},{1,5},{5... | collective-permute-start | bytes 1277960 | tf_op jit(solution)/shard_map/ppermute | solution.py:981
  108.9 12.5 %collective-permute-start.16 = (bf16[192,256]{1,0:T(8,128)(2,1)S(1)}, bf16[192,256]{1,0:T(8,128)(2,1)S(1)}, u32[]{:S(2)}, u32[]{:S(2)}) collective-permute-start(bf16[192,256]{1,0:T(8,128)(2,1)S(1)} %add_convert_fusion.5), channel_id=1, source_target_pairs={{0,4},{4,0},{8,12},{12,8},{16,20},{20,16},{24,28},{28,24},{1,5},{5... | collective-permute-start | bytes 294920 | tf_op jit(solution)/shard_map/ppermute | solution.py:981
  109.1 12.2 %collective-permute-start.15 = (bf16[832,256]{1,0:T(8,128)(2,1)S(1)}, bf16[832,256]{1,0:T(8,128)(2,1)S(1)}, u32[]{:S(2)}, u32[]{:S(2)}) collective-permute-start(bf16[832,256]{1,0:T(8,128)(2,1)S(1)} %add_convert_fusion.1), channel_id=1, source_target_pairs={{0,8},{4,12},{8,0},{12,4},{16,24},{20,28},{24,16},{28,20},{1,9},{5... | collective-permute-start | bytes 1277960 | tf_op jit(solution)/shard_map/ppermute | solution.py:981
  121.5 21.8 %collective-permute-start.22 = (bf16[832,256]{1,0:T(8,128)(2,1)S(1)}, bf16[832,256]{1,0:T(8,128)(2,1)S(1)}, u32[]{:S(2)}, u32[]{:S(2)}) collective-permute-start(bf16[832,256]{1,0:T(8,128)(2,1)S(1)} %add_convert_fusion.first), channel_id=1, source_target_pairs={{0,16},{4,20},{8,24},{12,28},{16,0},{20,4},{24,8},{28,12},{1,17},{... | collective-permute-start | bytes 1277960 | tf_op jit(solution)/shard_map/ppermute | solution.py:981
  135.0 11.1 %collective-permute-start.19 = (bf16[176,256]{1,0:T(8,128)(2,1)}, bf16[176,256]{1,0:T(8,128)(2,1)S(1)}, u32[]{:S(2)}, u32[]{:S(2)}) collective-permute-start(bf16[176,256]{1,0:T(8,128)(2,1)} %get-tuple-element.176), channel_id=1, source_target_pairs={{0,1},{1,0},{2,3},{3,2},{4,5},{5,4},{6,7},{7,6},{8,9},{9,8},{10,11... | collective-permute-start | bytes 270344 | tf_op jit(solution)/shard_map/ppermute | solution.py:981
  136.6 9.6 %collective-permute-start.20 = (bf16[176,256]{1,0:T(8,128)(2,1)}, bf16[176,256]{1,0:T(8,128)(2,1)S(1)}, u32[]{:S(2)}, u32[]{:S(2)}) collective-permute-start(bf16[176,256]{1,0:T(8,128)(2,1)} %get-tuple-element.177), channel_id=1, source_target_pairs={{0,2},{1,3},{2,0},{3,1},{4,6},{5,7},{6,4},{7,5},{8,10},{9,11},{10,... | collective-permute-start | bytes 270344 | tf_op jit(solution)/shard_map/ppermute | solution.py:981
  137.6 8.5 %collective-permute-start.21 = (bf16[176,256]{1,0:T(8,128)(2,1)}, bf16[176,256]{1,0:T(8,128)(2,1)S(1)}, u32[]{:S(2)}, u32[]{:S(2)}) collective-permute-start(bf16[176,256]{1,0:T(8,128)(2,1)} %get-tuple-element.178), channel_id=1, source_target_pairs={{0,3},{1,2},{2,1},{3,0},{4,7},{5,6},{6,5},{7,4},{8,11},{9,10},{10,... | collective-permute-start | bytes 270344 | tf_op jit(solution)/shard_map/ppermute | solution.py:981
  151.3 19.2 %collective-permute-start.18 = (bf16[192,256]{1,0:T(8,128)(2,1)S(1)}, bf16[192,256]{1,0:T(8,128)(2,1)S(1)}, u32[]{:S(2)}, u32[]{:S(2)}) collective-permute-start(bf16[192,256]{1,0:T(8,128)(2,1)S(1)} %add_convert_fusion.3.score_first), channel_id=1, source_target_pairs={{0,16},{4,20},{8,24},{12,28},{16,0},{20,4},{24,8},{28,12},{1,17},{... | collective-permute-start | bytes 294920 | tf_op jit(solution)/shard_map/ppermute | solution.py:981
  154.1 16.4 %collective-permute-start.25 = (bf16[176,256]{1,0:T(8,128)(2,1)S(1)}, bf16[176,256]{1,0:T(8,128)(2,1)S(1)}, u32[]{:S(2)}, u32[]{:S(2)}) collective-permute-start(bf16[176,256]{1,0:T(8,128)(2,1)S(1)} %add_convert_fusion.6.edge_first), channel_id=1, source_target_pairs={{0,16},{4,20},{8,24},{12,28},{16,0},{20,4},{24,8},{28,12},{1,17},{... | collective-permute-start | bytes 270344 | tf_op jit(solution)/shard_map/ppermute | solution.py:981
  154.5 11.1 %collective-permute-start.26 = (bf16[96,256]{1,0:T(8,128)(2,1)}, bf16[96,256]{1,0:T(8,128)(2,1)S(1)}, u32[]{:S(2)}, u32[]{:S(2)}) collective-permute-start(bf16[96,256]{1,0:T(8,128)(2,1)} %get-tuple-element.194), channel_id=1, source_target_pairs={{0,1},{1,2},{2,3},{3,4},{4,5},{5,6},{6,7},{7,8},{8,9},{9,10},{10,1... | collective-permute-start | bytes 147464 | tf_op jit(solution)/shard_map/ppermute | solution.py:988
  (27 other events, 175.5 us)

commit v3 on v2

--- a/solution.py
+++ b/solution.py
@@ -97,38 +97,42 @@
     return jnp.where(low_half, low, high)
 
 
-def fetch(source, buffer, semaphores, step, first=0):
-    slot = lax.rem(step, 2)
-    rows = source.shape[1]
-    return pltpu.make_async_copy(
-        source.at[step], buffer.at[slot, pl.ds(first, rows)], semaphores.at[slot]
-    )
-
-
-def fetch_next(source, buffer, semaphores, step, steps, first=0):
-    @pl.when(step + 1 < steps)
-    def _():
-        fetch(source, buffer, semaphores, step + 1, first).start()
-
-    fetch(source, buffer, semaphores, step, first).wait()
-    return buffer.at[lax.rem(step, 2)]
-
-
-def write_onehot(relative_ref, window, out_ref):
-    relative = relative_ref[...].astype(BF16)
+def write_onehot(relative, window, out_ref):
+    relative = relative.astype(BF16)
     one, zero = jnp.ones((), BF16), jnp.zeros((), BF16)
     place = lax.broadcasted_iota(jnp.int32, (16, LANES), 0).astype(F32)
-    for first in range(0, PAIRS, 8):
-        rows = [
-            jnp.broadcast_to(relative[pair : pair + 1, :], (16, LANES))
-            for pair in range(first, first + 8)
-        ]
-        for row in range(0, window, 16):
-            here = (place + float(row)).astype(BF16)
-            for pair, wanted in enumerate(rows, first):
-                out_ref[row : row + 16, pair * LANES : (pair + 1) * LANES] = jnp.where(
-                    here == wanted, one, zero
-                )
+    pairs = range(relative.shape[0])
+    wanted = [jnp.broadcast_to(relative[pair : pair + 1, :], (16, LANES)) for pair in pairs]
+    for row in range(0, window, 16):
+        here = (place + float(row)).astype(BF16)
+        for pair in pairs:
+            out_ref[row : row + 16, pair * LANES : (pair + 1) * LANES] = jnp.where(
+                here == wanted[pair], one, zero
+            )
+
+
+def write_basis(scaled, heights, shard, padded, step, window, out_ref):
+    iota = lax.broadcasted_iota(jnp.int32, (8, LANES), 0).astype(F32) * step
+    center = lambda row: ((row // padded) * shard + row % padded) * step
+    pairs = range(scaled.shape[0])
+    bases = [scaled[pair : pair + 1, :] - iota for pair in pairs]
+    tops = [
+        jnp.broadcast_to(heights[pair : pair + 1, :], (16, LANES)).astype(BF16) for pair in pairs
+    ]
+    for row in range(0, out_ref.shape[0] - window, 16):
+        for pair, base, top in zip(pairs, bases, tops):
+            delta = jnp.concatenate([base - center(row), base - center(row + 8)], axis=0)
+            low = delta.astype(BF16)
+            value = jnp.exp2(-(low * low)) * top
+            out_ref[window + row : window + row + 16, pair * LANES : (pair + 1) * LANES] = value
+
+
+def write_group(geometry, group, basis, window, out_ref):
+    scaled, heights, relative = (
+        ref[group * (GROUP // LANES) : (group + 1) * (GROUP // LANES), :] for ref in geometry
+    )
+    write_onehot(relative, window, out_ref)
+    write_basis(scaled, heights, *basis, window, out_ref)
 
 
 def diagonal(tile, low_half, less=None):
@@ -216,70 +220,35 @@
     )(index, rbf, query, key, value, out, gate, up, down, *rest)
 
 
-def basis_kernel(
-    shard, padded, spread, step, dist_ref, rows_ref, out_ref, relative_ref, by_atom, scaled, envelopes
-):
-    block = pl.program_id(0)
-    factor = math.sqrt(0.5 / math.log(2.0)) / spread
-
-    @pl.when(block == 0)
-    def _():
-        by_atom[0] = dist_ref[...].T
-        by_atom[1] = rows_ref[...].astype(F32).T
-
-    place = pl.ds(pl.multiple_of(block * BLOCK, BLOCK), BLOCK)
-    dist = pair_rows(by_atom[0, place, :])
-    scaled[...] = dist * factor
-    envelopes[...] = 0.5 * (jnp.cos(jnp.pi * dist / CUTOFF) + 1.0)
-    relative_ref[...] = pair_rows(by_atom[1, place, :]) - (block * BLOCK).astype(F32)
-    rows = out_ref.shape[0]
-    iota = lax.broadcasted_iota(jnp.int32, (8, LANES), 0).astype(F32) * (step * factor)
-    center = lambda row: ((row // padded) * shard + row % padded) * step * factor
-
-    for first in range(0, PAIRS, 8):
-        pairs = range(first, first + 8)
-        bases = [scaled[pair : pair + 1, :] - iota for pair in pairs]
-        heights = [jnp.broadcast_to(envelopes[pair : pair + 1, :], (16, LANES)) for pair in pairs]
-        for row in range(0, rows, 16):
-            for pair, base, height in zip(pairs, bases, heights):
-                delta = jnp.concatenate([base - center(row), base - center(row + 8)], axis=0)
-                value = jnp.exp2(-(delta * delta)) * height
-                out_ref[row : row + 16, pair * LANES : (pair + 1) * LANES] = value.astype(BF16)
-
-
-def basis_call(distances, neighbours, shard, padded, members, basis_count):
+def geometry_kernel(factor, dist_ref, rows_ref, scaled_ref, heights_ref, relative_ref):
+    dist = dist_ref[...].T
+    rows = rows_ref[...].astype(F32).T
+    for block in range(scaled_ref.shape[0]):
+        place = slice(block * BLOCK, (block + 1) * BLOCK)
+        pairs = pair_rows(dist[place])
+        scaled_ref[block] = pairs * factor
+        heights_ref[block] = 0.5 * (jnp.cos(jnp.pi * pairs / CUTOFF) + 1.0)
+        relative_ref[block] = pair_rows(rows[place]) - float(block * BLOCK)
+
+
+def geometry_call(distances, neighbours, factor):
     slots, atoms = distances.shape
     blocks = atoms // BLOCK
-    rows = members * padded
-    edges = BLOCK * slots
-    whole = pl.BlockSpec((slots, atoms), lambda b: (0, 0))
+    vmem = pl.BlockSpec(memory_space=pltpu.VMEM)
     return pl.pallas_call(
-        functools.partial(
-            basis_kernel, shard, padded, 2.0 * CUTOFF / basis_count, CUTOFF / basis_count
+        functools.partial(geometry_kernel, factor),
+        out_shape=(jax.ShapeDtypeStruct((blocks, PAIRS, LANES), F32),) * 3,
+        in_specs=[vmem, vmem],
+        out_specs=(vmem,) * 3,
+        cost_estimate=pl.CostEstimate(
+            flops=40 * atoms * slots, bytes_accessed=20 * atoms * slots, transcendentals=0
         ),
-        grid=(blocks,),
-        out_shape=(
-            jax.ShapeDtypeStruct((blocks, rows, edges), BF16),
-            jax.ShapeDtypeStruct((blocks, PAIRS, LANES), F32),
-        ),
-        in_specs=[whole, whole],
-        out_specs=(
-            pl.BlockSpec((None, rows, edges), lambda b: (b, 0, 0)),
-            pl.BlockSpec((None, PAIRS, LANES), lambda b: (b, 0, 0)),
-        ),
-        scratch_shapes=[
-            pltpu.VMEM((2, atoms, slots), F32),
-            pltpu.VMEM((PAIRS, LANES), F32),
-            pltpu.VMEM((PAIRS, LANES), F32),
-        ],
-        compiler_params=pltpu.CompilerParams(vmem_limit_bytes=40 * 2**20),
-        cost_estimate=pl.CostEstimate(
-            flops=8 * atoms * slots * rows,
-            bytes_accessed=2 * atoms * slots * rows,
-            transcendentals=atoms * slots * rows,
-        ),
-        name="radial_basis",
+        name="edge_geometry",
     )(distances, neighbours)
+
+
+def basis_factor(basis_count):
+    return math.sqrt(0.5 / math.log(2.0)) * basis_count / (2.0 * CUTOFF)
 
 
 def place_shards(index_ref, packs, row, count, out_ref):
@@ -298,7 +267,7 @@
 
 
 def forward_kernel(
-    padded,
+    basis,
     quarter,
     scale,
     index_ref,
@@ -310,8 +279,9 @@
     pack1,
     pack2,
     pack3,
+    scaled_ref,
+    heights_ref,
     relative_ref,
-    basis_hbm,
     edge_ref,
     power_ref,
     inverse_ref,
@@ -320,14 +290,13 @@
     lookup_ref,
     query_ref,
     kvq_ref,
-    weight_t,
     assembled,
     spread,
     keyed,
+    pooled,
+    weight_t,
     bands,
-    pooled,
-    phi_buffer,
-    semaphores,
+    *phis,
 ):
     step = pl.program_id(0)
     steps = pl.num_programs(0)
@@ -337,10 +306,17 @@
     lane = lax.broadcasted_iota(jnp.int32, (1, LANES), 1)
     edges = edge_ref.shape[1]
     window = BLOCK + 2 * HALO
+    group_rows = bands.shape[1]
+    groups = edges // GROUP
+    pairs = GROUP // LANES
+
+    def inputs_of(group):
+        part = slice(group * GROUP, (group + 1) * GROUP)
+        edge_ref[:, part] = nn(weight_t[...], phis[group][...]).astype(BF16)
 
     @pl.when(step == 0)
     def _():
-        fetch(basis_hbm, phi_buffer, semaphores, 0, window).start()
+        padded = basis[1]
         place_shards(index_ref, packs, 0, padded, assembled)
         weight_t[:, window:] = assembled[...].T.astype(BF16)
         start = round_up(padded, 16)
@@ -358,15 +334,14 @@
 
     table = lookup_ref[pl.ds(pl.multiple_of(step * BLOCK, BLOCK), window), :]
     weight_t[:, :window] = table.astype(F32).T.astype(BF16)
-    phi = phi_buffer.at[lax.rem(step, 2)]
-    write_onehot(relative_ref, window, phi)
-    fetch_next(basis_hbm, phi_buffer, semaphores, step, steps, window)
-    wide_part = 2 * GROUP
-    for start in range(0, edges, wide_part):
-        part = slice(start, start + wide_part)
-        edge_ref[:, part] = nn(weight_t[...], phi[:, part]).astype(BF16)
-    rows = BLOCK * HEADS
-    base = pl.multiple_of(step * rows, rows)
+    geometry = (scaled_ref, heights_ref, relative_ref)
+    write_group(geometry, 0, basis, window, phis[0])
+    for group in range(groups):
+        if group + 1 < groups:
+            write_group(geometry, group + 1, basis, window, phis[group + 1])
+        inputs_of(group)
+
+    base = pl.multiple_of(step * BLOCK * HEADS, BLOCK * HEADS)
     scores = []
     for tile in range(edges // TILE):
         left = keyed[pl.ds(base + tile * 32, 32), :]
@@ -380,44 +355,47 @@
     score = jnp.concatenate(scores, axis=0)
     power = jnp.exp(score - half_max(score, low_half))
     power_ref[...] = power.astype(BF16)
-    group_rows = bands.shape[1]
-    pairs = GROUP // LANES
     ones = jnp.ones((GROUP, LANES), BF16)
     for pair in range(PAIRS):
         group, place = pair // pairs, pair % pairs
         bands[
             group, place * 16 : (place + 1) * 16, place * LANES : (place + 1) * LANES
         ] = block_rows(power[pair * 8 : (pair + 1) * 8], low_half)
-    for group in range(edges // GROUP):
-        part = slice(group * GROUP, (group + 1) * GROUP)
+    for group in range(groups):
         band = bands[group]
         inverse = 1.0 / nn(band, ones)
-        result = nt(band, edge_ref[:, part])
+        result = nt(band, edge_ref[:, group * GROUP : (group + 1) * GROUP])
         rows = slice(group * group_rows, (group + 1) * group_rows)
-        place = pl.ds(base + group * group_rows, group_rows)
         inverse_ref[rows, :] = inverse
         for half in range(width // LANES):
             lanes = slice(half * LANES, (half + 1) * LANES)
             value = result[:, lanes] * inverse
-            pooled[half, place, :] = value
+            pooled[half, pl.ds(base + group * group_rows, group_rows), :] = value
             pooled_ref[rows, lanes] = value.astype(BF16)
 
-    @pl.when(step == steps - 1)
+    @pl.when(step + 1 == steps)
     def _():
         attended_ref[...] = gather_heads(pooled, kvq_ref[2], atoms).astype(BF16)
 
 
-def forward_call(index, counts, features, before, after, packs, relative, basis, padded, quarter):
+def forward_call(index, counts, features, before, after, packs, geometry, basis, quarter):
     atoms, width = features.shape
-    blocks, rows, edges = basis.shape
-    slots = edges // BLOCK
+    blocks = atoms // BLOCK
+    rows = len(packs) * basis[1]
+    slots = LANES // 2
+    edges = BLOCK * slots
     table = atoms + 2 * HALO
     full = lambda shape: pl.BlockSpec(shape, lambda b: (0,) * len(shape))
     head_rows = atoms * HEADS
     window = BLOCK + 2 * HALO
     group_rows = GROUP // slots * HEADS
     return pl.pallas_call(
-        functools.partial(forward_kernel, padded, quarter, (width // HEADS) ** -0.5),
+        functools.partial(
+            forward_kernel,
+            basis,
+            quarter,
+            (width // HEADS) ** -0.5,
+        ),
         grid=(blocks,),
         out_shape=(
             jax.ShapeDtypeStruct((blocks, width, edges), BF16),
@@ -437,10 +415,7 @@
             full((HALO, width)),
         ]
         + [full(pack.shape) for pack in packs]
-        + [
-            pl.BlockSpec((None, PAIRS, LANES), lambda b: (b, 0, 0)),
-            pl.BlockSpec(memory_space=pl.ANY),
-        ],
+        + [pl.BlockSpec((None, PAIRS, LANES), lambda b: (b, 0, 0))] * 3,
         out_specs=(
             pl.BlockSpec((None, width, edges), lambda b: (b, 0, 0)),
             pl.BlockSpec((None, PAIRS * HEADS, LANES), lambda b: (b, 0, 0)),
@@ -452,23 +427,22 @@
             full((3, width, width)),
         ),
         scratch_shapes=[
-            pltpu.VMEM((width, window + rows), BF16),
             pltpu.VMEM((rows, width), F32),
             pltpu.VMEM((width // LANES, head_rows, LANES), F32),
             pltpu.VMEM((head_rows, width), BF16),
+            pltpu.VMEM((width // LANES, head_rows, LANES), F32),
+            pltpu.VMEM((width, window + rows), BF16),
             pltpu.VMEM((edges // GROUP, group_rows, GROUP), BF16),
-            pltpu.VMEM((width // LANES, head_rows, LANES), F32),
-            pltpu.VMEM((2, window + rows, edges), BF16),
-            pltpu.SemaphoreType.DMA((2,)),
-        ],
-        compiler_params=pltpu.CompilerParams(vmem_limit_bytes=58 * 2**20),
+        ]
+        + [pltpu.VMEM((window + rows, GROUP), BF16)] * (edges // GROUP),
+        compiler_params=pltpu.CompilerParams(vmem_limit_bytes=24 * 2**20),
         cost_estimate=pl.CostEstimate(
             flops=2 * atoms * slots * width * (rows + window + 64),
             bytes_accessed=2 * atoms * slots * (rows + width),
-            transcendentals=atoms * slots * HEADS,
+            transcendentals=atoms * slots * rows,
         ),
         name="attention_forward",
-    )(index, counts, features, before, after, *packs, relative, basis)
+    )(index, counts, features, before, after, *packs, *geometry)
 
 
 def ffn_kernel(
@@ -592,7 +566,7 @@
             for dtype in (BF16, F32)
             for shape in ((width, hidden), (width, hidden), (hidden, width), (width, width))
         ],
-        compiler_params=pltpu.CompilerParams(vmem_limit_bytes=58 * 2**20),
+        compiler_params=pltpu.CompilerParams(vmem_limit_bytes=24 * 2**20),
         cost_estimate=pl.CostEstimate(
             flops=18 * atoms * width * hidden, bytes_accessed=2**23, transcendentals=atoms * hidden
         ),
@@ -749,7 +723,7 @@
             pltpu.VMEM((width // LANES, head_rows, LANES), F32),
             pltpu.VMEM((3, width, width), F32),
         ],
-        compiler_params=pltpu.CompilerParams(vmem_limit_bytes=58 * 2**20),
+        compiler_params=pltpu.CompilerParams(vmem_limit_bytes=24 * 2**20),
         cost_estimate=pl.CostEstimate(
             flops=2 * atoms * edges // BLOCK * width * 256,
             bytes_accessed=2 * blocks * width * edges,
@@ -759,10 +733,10 @@
     )(index, *whole, power, edge)
 
 
-def edge_kernel(padded, gain_row, first_block, last_block, carried, final, *refs):
+def edge_kernel(basis, gain_row, first_block, last_block, carried, final, *refs):
     refs = list(refs)
     take = lambda count: [refs.pop(0) for _ in range(count)]
-    relative_ref, power_ref, grad_score_ref, mixed_ref, basis_hbm = take(5)
+    geometry, (power_ref, grad_score_ref, mixed_ref) = take(3), take(3)
     before = take(2 if carried else 0)
     if final:
         index_ref, features_ref, before_ref, after_ref, grad_query_ref, kvq_ref = take(6)
@@ -771,18 +745,19 @@
         grad_own_ref, grad_lower_ref, grad_upper_ref = take(3)
         grads_refs = take(4)
     grad_rbf, grad_lookup = take(2)
-    bands, grad_edge, phi_buffer, semaphores = take(4)
+    (bands,), grad_edges = take(1), take(len(refs) // 2)
+    phis = refs
     block = pl.program_id(0) + first_block
-    width, edges = grad_edge.shape
+    width = mixed_ref.shape[1]
+    padded = basis[1]
     window = BLOCK + 2 * HALO
     low_half = lax.broadcasted_iota(jnp.int32, (1, LANES), 1) < LANES // 2
     group_rows = bands.shape[1] // 2
-    groups = edges // GROUP
+    groups = len(phis)
     pairs = GROUP // LANES
 
     @pl.when(block == first_block)
     def _():
-        fetch(basis_hbm, phi_buffer, semaphores, block, window).start()
         bands[...] = jnp.zeros_like(bands)
         if carried:
             grad_rbf[...] = before[0][...]
@@ -801,12 +776,14 @@
             row = start + column * 16
             bands[group, row : row + 16, lanes] = block_rows(value, low_half)
     for group in range(groups):
-        part = slice(group * GROUP, (group + 1) * GROUP)
-        grad_edge[:, part] = nn(mixed_ref[group], bands[group]).astype(BF16)
-    phi = phi_buffer.at[lax.rem(block, 2)]
-    write_onehot(relative_ref, window, phi)
-    fetch_next(basis_hbm, phi_buffer, semaphores, block, last_block, window)
-    total = nt(phi[...], grad_edge[...])
+        grad_edges[group][...] = nn(mixed_ref[group], bands[group]).astype(BF16)
+    write_group(geometry, 0, basis, window, phis[0])
+    total = None
+    for group in range(groups):
+        if group + 1 < groups:
+            write_group(geometry, group + 1, basis, window, phis[group + 1])
+        term = nt(phis[group][...], grad_edges[group][...])
+        total = term if total is None else total + term
     grad_lookup[pl.ds(pl.multiple_of(block * BLOCK, BLOCK), window), :] += total[:window]
     grad_rbf[...] += total[window:]
 
@@ -843,9 +820,10 @@
             grads[after_rbf:, :] = vectors.astype(BF16)
 
 
-def edge_call(arrays, basis, carry, last, padded, gain_row, first_block, last_block):
-    blocks, rows, edges = basis.shape
-    width = arrays[3].shape[1]
+def edge_call(arrays, carry, last, basis, members, gain_row, first_block, last_block):
+    width = arrays[-1].shape[1]
+    blocks = arrays[0].shape[0]
+    rows, edges = members * basis[1], PAIRS * LANES
     groups = edges // GROUP
     group_rows = GROUP // (edges // BLOCK) * HEADS
     table = blocks * BLOCK + 2 * HALO
@@ -854,45 +832,43 @@
     here = lambda b: (b + first_block, 0, 0)
     in_specs = [
         pl.BlockSpec((None, PAIRS, LANES), here),
+        pl.BlockSpec((None, PAIRS, LANES), here),
+        pl.BlockSpec((None, PAIRS, LANES), here),
         pl.BlockSpec((None, PAIRS * HEADS, LANES), here),
         pl.BlockSpec((None, PAIRS * HEADS, LANES), here),
         pl.BlockSpec((groups, width, 2 * group_rows), here),
-        pl.BlockSpec(memory_space=pl.ANY),
     ]
-    operands = [*arrays, basis]
+    operands = list(arrays)
     sums = [(rows, width), (table, width)]
     if carry is not None:
         in_specs += [full(value.shape) for value in carry]
         operands += list(carry)
-    scratch = [
-        pltpu.VMEM((groups, 2 * group_rows, GROUP), BF16),
-        pltpu.VMEM((width, edges), BF16),
-        pltpu.VMEM((2, window + rows, edges), BF16),
-        pltpu.SemaphoreType.DMA((2,)),
-    ]
+    scratch = [pltpu.VMEM((groups, 2 * group_rows, GROUP), BF16)]
+    scratch += [pltpu.VMEM((width, GROUP), BF16)] * groups
+    scratch += [pltpu.VMEM((window + rows, GROUP), BF16)] * groups
     if last is None:
         shapes = [(shape, F32) for shape in sums]
     else:
         in_specs += [pl.BlockSpec(memory_space=pltpu.SMEM)]
         in_specs += [full(value.shape) for value in last[1:]]
         operands += list(last)
-        grads = (round_up(padded, 16) + 16, width)
+        grads = (round_up(basis[1], 16) + 16, width)
         shapes = [((blocks * BLOCK, width), F32)] + [((HALO, width), BF16)] * 2 + [(grads, BF16)] * 4
         scratch = [pltpu.VMEM(shape, F32) for shape in sums] + scratch
     return pl.pallas_call(
         functools.partial(
-            edge_kernel, padded, gain_row, first_block, last_block, carry is not None, last is not None
+            edge_kernel, basis, gain_row, first_block, last_block, carry is not None, last is not None
         ),
         grid=(last_block - first_block,),
         out_shape=[jax.ShapeDtypeStruct(shape, dtype) for shape, dtype in shapes],
         in_specs=in_specs,
         out_specs=[full(shape) for shape, _ in shapes],
         scratch_shapes=scratch,
-        compiler_params=pltpu.CompilerParams(vmem_limit_bytes=58 * 2**20),
+        compiler_params=pltpu.CompilerParams(vmem_limit_bytes=24 * 2**20),
         cost_estimate=pl.CostEstimate(
             flops=2 * (last_block - first_block) * edges * width * (rows + window + 256),
-            bytes_accessed=2 * (last_block - first_block) * rows * edges,
-            transcendentals=0,
+            bytes_accessed=2**22,
+            transcendentals=(last_block - first_block) * rows * edges,
         ),
         name="edge_backward",
     )(*operands)
@@ -1061,6 +1037,8 @@
     atoms, width = features.shape
     shard = rbf_weight.shape[0]
     padded = round_up(shard, 8)
+    factor = basis_factor(members * shard)
+    basis = (shard, padded, factor * CUTOFF / (members * shard))
     gain_row = round_up(shard, 16) + 3 * query_weight.shape[0]
     quarter = query_weight.shape[0]
     hidden = gate_weight.shape[1]
@@ -1084,15 +1062,12 @@
     small_all = gathered(small)
     before = shifted(final, 1)
     after = shifted(initial, -1)
-    basis, relative = basis_call(
-        distances.T, neighbours.T, shard, padded, members, members * shard
-    )
-
-    large, basis = lax.optimization_barrier((large, basis))
+    geometry = geometry_call(distances.T, neighbours.T, factor)
+    large, geometry = lax.optimization_barrier((large, geometry))
     large_all = gathered(large)
 
     edge, power, inverse, pooled, attended, lookup, query, kvq = forward_call(
-        index, counts, features, before, after, small_all, relative, basis, padded, quarter
+        index, counts, features, before, after, small_all, geometry, basis, quarter
     )
     outputs, energy, grad_residual, grad_attended, sums, *large_grads = ffn_call(
         index,
@@ -1117,13 +1092,13 @@
             grad_score = between([large_sum], grad_score)
         else:
             carry = between([large_sum, score_sum], carry)
-        final = block + count == basis.shape[0]
+        final = block + count == edge.shape[0]
         carry = edge_call(
-            (relative, power, grad_score, mixed),
-            basis,
+            (*geometry, power, grad_score, mixed),
             carry,
             last if final else None,
-            padded,
+            basis,
+            members,
             gain_row,
             block,
             block + count,

time: 174 us -> 152 us (0.87)
  Pallas kernels: 111 us -> 78.1 us
  starting transfers between devices: 35.1 us -> 41.6 us
  waiting for transfers between devices: 16.7 us -> 21.4 us
    pallas_call x5, Pallas kernels: 78.5 us -> 52.5 us  [the longest x1 28.2 us: forward_call(): pl.pallas_call(functools.partial(forward_kernel, basis, quarter, (width /...]
    ppermute x24, starting transfers between devices: 19.3 us -> 26.7 us  [exchange(): return lax.ppermute(value, axis, [(i, i ^ offset) for i in range(size)])]
    pallas_call x1, Pallas kernels: 19.8 us -> 15.1 us  [score_call(): pl.pallas_call(functools.partial(score_kernel, quarter, (width // HEADS)...]
    ppermute x24, waiting for transfers between devices: 11.8 us -> 15.7 us  [exchange(): return lax.ppermute(value, axis, [(i, i ^ offset) for i in range(size)])]
    pallas_call x1, Pallas kernels: 6.87 us -> 4.26 us  [ffn_call(): pl.pallas_call(functools.partial(ffn_kernel, quarter, row), out_shape=(ja...]
    unnamed x46 -> x44, local copies, waits for them, and re-layouts: 5.64 us -> 7.44 us
  transfers between devices with their start and end apart: 28 -> 28, of which waited for: 6 -> 7; matrix products, arithmetic and copies ran while one was open for 1% -> 1% of each run, Pallas kernels for 58% -> 46%
where the time goes in v3:
time: 152 us
  Pallas kernels  78.1 us (51%)
  starting transfers between devices  41.6 us (27%)
  waiting for transfers between devices  21.4 us (14%)
  local copies, waits for them, and re-layouts  8.13 us (5%)
    pallas_call x1, Pallas kernels, forward_call(): pl.pallas_call(functools.partial(forward_kernel, basis, quarter, (width /...  28.2 us
    ppermute x24, starting transfers between devices, exchange(): return lax.ppermute(value, axis, [(i, i ^ offset) for i in range(size)])  26.7 us
    pallas_call x3, Pallas kernels, edge_call(): pl.pallas_call(functools.partial(edge_kernel, basis, gain_row, first_bloc...  22 us
    ppermute x24, waiting for transfers between devices, exchange(): return lax.ppermute(value, axis, [(i, i ^ offset) for i in range(size)])  15.7 us
    pallas_call x1, Pallas kernels, score_call(): pl.pallas_call(functools.partial(score_kernel, quarter, (width // HEADS)...  15.1 us
    ppermute x4, starting transfers between devices, shifted(): return lax.ppermute(value, axes, pairs)  15 us
    unnamed x44, local copies, waits for them, and re-layouts  7.44 us
    ppermute x4, waiting for transfers between devices, shifted(): return lax.ppermute(value, axes, pairs)  5.61 us
  transfers between devices with their start and end apart: 28, of which 7 were waited for; matrix products, arithmetic and copies ran while one was open for 1% of the time, Pallas kernels for 46%

profile of v3, /device:TPU:7, one launch (start us, length us, event | category | flops | bytes accessed | tf_op | source)
XLA Modules:
  0.0 151.6 jit_solution(14839000520157916305)
XLA Ops:
  0.7 2.1 %pack_weights.1 = (bf16[368,256]{1,0:T(8,128)(2,1)}, bf16[832,256]{1,0:T(8,128)(2,1)}, bf16[96,256]{1,0:T(8,128)(2,1)}, bf16[96,256]{1,0:T(8,128)(2,1)}) custom-call(s32[1]{0:T(128)} %bitcast.index_ref.refs_8_, bf16[150,256]{1,0:T(8,128)(2,1)} %rbf_ref.1, bf16[64,256]{1,0:T(8,128)(2,1)} %query_ref.1, bf16[64,256]{1,0:T(8,128)(2,1)} %key_ref.1, ...), custom_call_target="tpu_custom_call" | custom-call | bytes 2097152 | tf_op jit(solution)/shard_map/pack_weights/pallas_call | solution.py:208
  4.9 3.4 %collective-permute-start = (bf16[96,256]{1,0:T(8,128)(2,1)}, bf16[96,256]{1,0:T(8,128)(2,1)S(1)}, u32[]{:S(2)}, u32[]{:S(2)}) collective-permute-start(bf16[96,256]{1,0:T(8,128)(2,1)} %get-tuple-element.114), channel_id=1, source_target_pairs={{0,1},{1,2},{2,3},{3,4},{4,5},{5,6},{6,7},{7,8},{8,9},{9,10},{10,1... | collective-permute-start | bytes 147464 | tf_op jit(solution)/shard_map/ppermute | solution.py:964
  8.3 1.9 %collective-permute-start.1 = (bf16[96,256]{1,0:T(8,128)(2,1)}, bf16[96,256]{1,0:T(8,128)(2,1)S(1)}, u32[]{:S(2)}, u32[]{:S(2)}) collective-permute-start(bf16[96,256]{1,0:T(8,128)(2,1)} %get-tuple-element.115), channel_id=1, source_target_pairs={{1,0},{2,1},{3,2},{4,3},{5,4},{6,5},{7,6},{8,7},{9,8},{10,9},{11,1... | collective-permute-start | bytes 147464 | tf_op jit(solution)/shard_map/ppermute | solution.py:964
  10.9 2.2 %edge_geometry.1 = (f32[6,32,128]{2,1,0:T(8,128)}, f32[6,32,128]{2,1,0:T(8,128)}, f32[6,32,128]{2,1,0:T(8,128)}) custom-call(f32[64,384]{1,0:T(8,128)} %bitcast.9, s32[64,384]{1,0:T(8,128)} %bitcast.10), custom_call_target="tpu_custom_call" | custom-call | flops 983040 | bytes 491520 | tf_op jit(solution)/shard_map/edge_geometry/pallas_call | solution.py:238
  22.4 28.2 %attention_forward.1 = (bf16[6,256,4096]{2,1,0:T(8,128)(2,1)S(1)}, bf16[6,256,128]{2,1,0:T(8,128)(2,1)S(1)}, f32[3072,128]{1,0:T(8,128)S(1)}, bf16[3072,256]{1,0...) custom-call(s32[1]{0:T(128)} %bitcast.index_ref.refs_8_, ...), custom_call_target="tpu_custom_call" | custom-call | flops 11676942336 | bytes 42467328 | tf_op jit(solution)/shard_map/attention_forward/pallas_call | solution.py:392
  50.7 4.3 %feed_forward.1 = (f32[384,256]{1,0:T(8,128)}, f32[1,384]{1,0:T(1,128)S(1)}, f32[384,256]{1,0:T(8,128)S(1)}, bf16[384,256]{1,0:T(8,128)(2,1)S(1)}, f32[8,256]{1,...) custom-call(s32[1]{0:T(128)} %bitcast.index_ref.refs_8_, ...), custom_call_target="tpu_custom_call" | custom-call | flops 1811939328 | bytes 8388608 | tf_op jit(solution)/shard_map/feed_forward/pallas_call | solution.py:552
  57.1 15.1 %score_backward.1 = (f32[6,256,128]{2,1,0:T(8,128)S(1)}, bf16[24,256,256]{2,1,0:T(8,128)(2,1)S(1)}, bf16[384,256]{1,0:T(8,128)(2,1)S(1)}, bf16[192,256]{1,0:T(8,...) custom-call(s32[1]{0:T(128)} %bitcast.index_ref.refs_8_, ...), custom_call_target="tpu_custom_call" | custom-call | flops 3221225472 | bytes 12582912 | tf_op jit(solution)/shard_map/score_backward/pallas_call | solution.py:698
  74.4 2.1 %collective-permute-done.10 = bf16[832,256]{1,0:T(8,128)(2,1)S(1)} collective-permute-done((bf16[832,256]{1,0:T(8,128)(2,1)S(1)}, bf16[832,256]{1,0:T(8,128)(2,1)S(1)}, u32[]{:S(2)}, u32[]{:S(2)}) %collective-permute-start.10) | collective-permute-done | bytes 426016 | tf_op jit(solution)/shard_map/ppermute | solution.py:957
  76.8 7.2 %edge_backward.3 = (f32[608,256]{1,0:T(8,128)S(1)}, f32[576,256]{1,0:T(8,128)S(1)}) custom-call(f32[6,32,128]{2,1,0:T(8,128)S(1)} %copy-done.8, f32[6,32,128]{2,1,0:T(8,128)S(1)} %copy-done.10, f32[6,32,128]{2,1,0:T(8,128)S(1)} %copy-done.12, bf16[6,256,128]{2,1,0:T(8,128)(2,1)S(1)} %get-tuple-element.138.power_ref.refs_3_, ...), custom_call_target="tpu_custom_call" | custom-call | flops 4697620480 | bytes 4194304 | tf_op jit(solution)/shard_map/edge_backward/pallas_call | solution.py:858
  84.1 4.3 %collective-permute-done.11 = bf16[832,256]{1,0:T(8,128)(2,1)S(1)} collective-permute-done((bf16[832,256]{1,0:T(8,128)(2,1)S(1)}, bf16[832,256]{1,0:T(8,128)(2,1)S(1)}, u32[]{:S(2)}, u32[]{:S(2)}) %collective-permute-start.11) | collective-permute-done | bytes 426016 | tf_op jit(solution)/shard_map/ppermute | solution.py:957
  90.1 7.2 %edge_backward.4 = (f32[608,256]{1,0:T(8,128)S(1)}, f32[576,256]{1,0:T(8,128)S(1)}) custom-call(f32[6,32,128]{2,1,0:T(8,128)S(1)} %copy-done.8, f32[6,32,128]{2,1,0:T(8,128)S(1)} %copy-done.10, f32[6,32,128]{2,1,0:T(8,128)S(1)} %copy-done.12, bf16[6,256,128]{2,1,0:T(8,128)(2,1)S(1)} %get-tuple-element.138.power_ref.refs_3_, ...), custom_call_target="tpu_custom_call" | custom-call | flops 4697620480 | bytes 4194304 | tf_op jit(solution)/shard_map/edge_backward/pallas_call | solution.py:858
  97.3 2.1 %collective-permute-done.15 = bf16[832,256]{1,0:T(8,128)(2,1)S(1)} collective-permute-done((bf16[832,256]{1,0:T(8,128)(2,1)S(1)}, bf16[832,256]{1,0:T(8,128)(2,1)S(1)}, u32[]{:S(2)}, u32[]{:S(2)}) %collective-permute-start.15) | collective-permute-done | bytes 426016 | tf_op jit(solution)/shard_map/ppermute | solution.py:957
  99.6 2.4 %collective-permute-start.22 = (bf16[832,256]{1,0:T(8,128)(2,1)S(1)}, bf16[832,256]{1,0:T(8,128)(2,1)S(1)}, u32[]{:S(2)}, u32[]{:S(2)}) collective-permute-start(bf16[832,256]{1,0:T(8,128)(2,1)S(1)} %add_convert_fusion.first), channel_id=1, source_target_pairs={{0,16},{4,20},{8,24},{12,28},{16,0},{20,4},{24,8},{28,12},{1,17},{... | collective-permute-start | bytes 1277960 | tf_op jit(solution)/shard_map/ppermute | solution.py:957
  102.0 7.6 %edge_backward.5 = (f32[384,256]{1,0:T(8,128)S(1)}, bf16[96,256]{1,0:T(8,128)(2,1)S(1)}, bf16[96,256]{1,0:T(8,128)(2,1)S(1)}, bf16[176,256]{1,0:T(8,128)(2,1)S(1...) custom-call(f32[6,32,128]{2,1,0:T(8,128)S(1)} %copy-done.8, ...), custom_call_target="tpu_custom_call" | custom-call | flops 4697620480 | bytes 4194304 | tf_op jit(solution)/shard_map/edge_backward/pallas_call | solution.py:858
  110.4 1.9 %collective-permute-start.19 = (bf16[176,256]{1,0:T(8,128)(2,1)S(1)}, bf16[176,256]{1,0:T(8,128)(2,1)S(1)}, u32[]{:S(2)}, u32[]{:S(2)}) collective-permute-start(bf16[176,256]{1,0:T(8,128)(2,1)S(1)} %get-tuple-element.182), channel_id=1, source_target_pairs={{0,1},{1,0},{2,3},{3,2},{4,5},{5,4},{6,7},{7,6},{8,9},{9,8},{10,11... | collective-permute-start | bytes 270344 | tf_op jit(solution)/shard_map/ppermute | solution.py:957
  113.9 6.4 %collective-permute-done.22.second = bf16[832,256]{1,0:T(8,128)(2,1)S(1)} collective-permute-done((bf16[832,256]{1,0:T(8,128)(2,1)S(1)}, bf16[832,256]{1,0:T(8,128)(2,1)S(1)}, u32[]{:S(2)}, u32[]{:S(2)}) %collective-permute-start.22) | collective-permute-done | bytes 426016 | tf_op jit(solution)/shard_map/ppermute | solution.py:957
  121.1 2.1 %feed_forward_results.1 = (f32[64,1024]{1,0:T(8,128)}, f32[64,1024]{1,0:T(8,128)}, f32[256,256]{1,0:T(8,128)}, f32[64,256]{1,0:T(8,128)}) custom-call(bf16[832,256]{1,0:T(8,128)(2,1)} %copy-done.14, bf16[832,256]{1,0:T(8,128)(2,1)} %copy-done.15), custom_call_target="tpu_custom_call" | custom-call | tf_op jit(solution)/shard_map/feed_forward_results/pallas_call | solution.py:894
  126.7 1.9 %collective-permute-start.24 = (bf16[176,256]{1,0:T(8,128)(2,1)S(1)}, bf16[176,256]{1,0:T(8,128)(2,1)S(1)}, u32[]{:S(2)}, u32[]{:S(2)}) collective-permute-start(bf16[176,256]{1,0:T(8,128)(2,1)S(1)} %add_convert_fusion.7), channel_id=1, source_target_pairs={{0,8},{4,12},{8,0},{12,4},{16,24},{20,28},{24,16},{28,20},{1,9},{5... | collective-permute-start | bytes 270344 | tf_op jit(solution)/shard_map/ppermute | solution.py:957
  128.6 3.2 %collective-permute-start.18 = (bf16[192,256]{1,0:T(8,128)(2,1)S(1)}, bf16[192,256]{1,0:T(8,128)(2,1)S(1)}, u32[]{:S(2)}, u32[]{:S(2)}) collective-permute-start(bf16[192,256]{1,0:T(8,128)(2,1)S(1)} %add_convert_fusion.3.score_first), channel_id=1, source_target_pairs={{0,16},{4,20},{8,24},{12,28},{16,0},{20,4},{24,8},{28,12},{1,17},{... | collective-permute-start | bytes 294920 | tf_op jit(solution)/shard_map/ppermute | solution.py:957
  131.8 1.9 %collective-permute-start.25 = (bf16[176,256]{1,0:T(8,128)(2,1)S(1)}, bf16[176,256]{1,0:T(8,128)(2,1)S(1)}, u32[]{:S(2)}, u32[]{:S(2)}) collective-permute-start(bf16[176,256]{1,0:T(8,128)(2,1)S(1)} %add_convert_fusion.6.edge_first), channel_id=1, source_target_pairs={{0,16},{4,20},{8,24},{12,28},{16,0},{20,4},{24,8},{28,12},{1,17},{... | collective-permute-start | bytes 270344 | tf_op jit(solution)/shard_map/ppermute | solution.py:957
  133.7 7.8 %collective-permute-start.26 = (bf16[96,256]{1,0:T(8,128)(2,1)S(1)}, bf16[96,256]{1,0:T(8,128)(2,1)S(1)}, u32[]{:S(2)}, u32[]{:S(2)}) collective-permute-start(bf16[96,256]{1,0:T(8,128)(2,1)S(1)} %get-tuple-element.200), channel_id=1, source_target_pairs={{0,1},{1,2},{2,3},{3,4},{4,5},{5,6},{6,7},{7,8},{8,9},{9,10},{10,1... | collective-permute-start | bytes 147464 | tf_op jit(solution)/shard_map/ppermute | solution.py:964
  141.5 1.9 %collective-permute-start.27 = (bf16[96,256]{1,0:T(8,128)(2,1)S(1)}, bf16[96,256]{1,0:T(8,128)(2,1)S(1)}, u32[]{:S(2)}, u32[]{:S(2)}) collective-permute-start(bf16[96,256]{1,0:T(8,128)(2,1)S(1)} %get-tuple-element.201), channel_id=1, source_target_pairs={{1,0},{2,1},{3,2},{4,3},{5,4},{6,5},{7,6},{8,7},{9,8},{10,9},{11,1... | collective-permute-start | bytes 147464 | tf_op jit(solution)/shard_map/ppermute | solution.py:964
  144.0 4.7 %collective-permute-done.27.from_upper = bf16[96,256]{1,0:T(8,128)(2,1)S(1)} collective-permute-done((bf16[96,256]{1,0:T(8,128)(2,1)S(1)}, bf16[96,256]{1,0:T(8,128)(2,1)S(1)}, u32[]{:S(2)}, u32[]{:S(2)}) %collective-permute-start.27) | collective-permute-done | bytes 49184 | tf_op jit(solution)/shard_map/ppermute | solution.py:964
  149.4 2.1 %edge_results.1 = (f32[150,256]{1,0:T(8,128)}, f32[64,256]{1,0:T(8,128)}, f32[64,256]{1,0:T(8,128)}, f32[64,256]{1,0:T(8,128)}, f32[1,64]{1,0:T(1,128)}, /*index...) custom-call(s32[1]{0:T(128)} %bitcast.index_ref.refs_8_, bf16[192,256]{1,0:T(8,128)(2,1)} %copy-done.16, ...), custom_call_target="tpu_custom_call" | custom-call | tf_op jit(solution)/shard_map/edge_results/pallas_call | solution.py:946
  (97 shorter events, 26.6 us)
Async XLA Ops:
  2.8 14.3 %collective-permute-start.4 = (bf16[368,256]{1,0:T(8,128)(2,1)}, bf16[368,256]{1,0:T(8,128)(2,1)S(1)}, u32[]{:S(2)}, u32[]{:S(2)}) collective-permute-start(bf16[368,256]{1,0:T(8,128)(2,1)} %get-tuple-element.116.pack0.small0.refs_16_), channel_id=1, source_target_pairs={{0,3},{1,2},{2,1},{3,0},{4,7},{5,6},{6,5},{7,4},{8,11},{9,10},{10,... | collective-permute-start | bytes 565256 | tf_op jit(solution)/shard_map/ppermute | solution.py:957
  3.6 13.5 %collective-permute-start.3 = (bf16[368,256]{1,0:T(8,128)(2,1)}, bf16[368,256]{1,0:T(8,128)(2,1)S(1)}, u32[]{:S(2)}, u32[]{:S(2)}) collective-permute-start(bf16[368,256]{1,0:T(8,128)(2,1)} %get-tuple-element.116.pack0.small0.refs_16_), channel_id=1, source_target_pairs={{0,2},{1,3},{2,0},{3,1},{4,6},{5,7},{6,4},{7,5},{8,10},{9,11},{10,... | collective-permute-start | bytes 565256 | tf_op jit(solution)/shard_map/ppermute | solution.py:957
  4.8 12.3 %collective-permute-start.2 = (bf16[368,256]{1,0:T(8,128)(2,1)}, bf16[368,256]{1,0:T(8,128)(2,1)S(1)}, u32[]{:S(2)}, u32[]{:S(2)}) collective-permute-start(bf16[368,256]{1,0:T(8,128)(2,1)} %get-tuple-element.116.pack0.small0.refs_16_), channel_id=1, source_target_pairs={{0,1},{1,0},{2,3},{3,2},{4,5},{5,4},{6,7},{7,6},{8,9},{9,8},{10,11... | collective-permute-start | bytes 565256 | tf_op jit(solution)/shard_map/ppermute | solution.py:957
  4.9 8.2 %collective-permute-start = (bf16[96,256]{1,0:T(8,128)(2,1)}, bf16[96,256]{1,0:T(8,128)(2,1)S(1)}, u32[]{:S(2)}, u32[]{:S(2)}) collective-permute-start(bf16[96,256]{1,0:T(8,128)(2,1)} %get-tuple-element.114), channel_id=1, source_target_pairs={{0,1},{1,2},{2,3},{3,4},{4,5},{5,6},{6,7},{7,8},{8,9},{9,10},{10,1... | collective-permute-start | bytes 147464 | tf_op jit(solution)/shard_map/ppermute | solution.py:964
  8.3 7.4 %collective-permute-start.1 = (bf16[96,256]{1,0:T(8,128)(2,1)}, bf16[96,256]{1,0:T(8,128)(2,1)S(1)}, u32[]{:S(2)}, u32[]{:S(2)}) collective-permute-start(bf16[96,256]{1,0:T(8,128)(2,1)} %get-tuple-element.115), channel_id=1, source_target_pairs={{1,0},{2,1},{3,2},{4,3},{5,4},{6,5},{7,6},{8,7},{9,8},{10,9},{11,1... | collective-permute-start | bytes 147464 | tf_op jit(solution)/shard_map/ppermute | solution.py:964
  13.1 37.5 %collective-permute-start.7 = (bf16[832,256]{1,0:T(8,128)(2,1)}, bf16[832,256]{1,0:T(8,128)(2,1)S(1)}, u32[]{:S(2)}, u32[]{:S(2)}) collective-permute-start(bf16[832,256]{1,0:T(8,128)(2,1)} %get-tuple-element.125.pack0), channel_id=1, source_target_pairs={{0,3},{1,2},{2,1},{3,0},{4,7},{5,6},{6,5},{7,4},{8,11},{9,10},{10,... | collective-permute-start | bytes 1277960 | tf_op jit(solution)/shard_map/ppermute | solution.py:957
  15.7 34.9 %collective-permute-start.6 = (bf16[832,256]{1,0:T(8,128)(2,1)}, bf16[832,256]{1,0:T(8,128)(2,1)S(1)}, u32[]{:S(2)}, u32[]{:S(2)}) collective-permute-start(bf16[832,256]{1,0:T(8,128)(2,1)} %get-tuple-element.125.pack0), channel_id=1, source_target_pairs={{0,2},{1,3},{2,0},{3,1},{4,6},{5,7},{6,4},{7,5},{8,10},{9,11},{10,... | collective-permute-start | bytes 1277960 | tf_op jit(solution)/shard_map/ppermute | solution.py:957
  17.1 33.5 %collective-permute-start.5 = (bf16[832,256]{1,0:T(8,128)(2,1)}, bf16[832,256]{1,0:T(8,128)(2,1)S(1)}, u32[]{:S(2)}, u32[]{:S(2)}) collective-permute-start(bf16[832,256]{1,0:T(8,128)(2,1)} %get-tuple-element.125.pack0), channel_id=1, source_target_pairs={{0,1},{1,0},{2,3},{3,2},{4,5},{5,4},{6,7},{7,6},{8,9},{9,8},{10,11... | collective-permute-start | bytes 1277960 | tf_op jit(solution)/shard_map/ppermute | solution.py:957
  54.9 17.8 %collective-permute-start.8 = (bf16[832,256]{1,0:T(8,128)(2,1)S(1)}, bf16[832,256]{1,0:T(8,128)(2,1)S(1)}, u32[]{:S(2)}, u32[]{:S(2)}) collective-permute-start(bf16[832,256]{1,0:T(8,128)(2,1)S(1)} %get-tuple-element.129), channel_id=1, source_target_pairs={{0,1},{1,0},{2,3},{3,2},{4,5},{5,4},{6,7},{7,6},{8,9},{9,8},{10,11... | collective-permute-start | bytes 1277960 | tf_op jit(solution)/shard_map/ppermute | solution.py:957
  55.4 19.0 %collective-permute-start.9 = (bf16[832,256]{1,0:T(8,128)(2,1)S(1)}, bf16[832,256]{1,0:T(8,128)(2,1)S(1)}, u32[]{:S(2)}, u32[]{:S(2)}) collective-permute-start(bf16[832,256]{1,0:T(8,128)(2,1)S(1)} %get-tuple-element.130), channel_id=1, source_target_pairs={{0,2},{1,3},{2,0},{3,1},{4,6},{5,7},{6,4},{7,5},{8,10},{9,11},{10,... | collective-permute-start | bytes 1277960 | tf_op jit(solution)/shard_map/ppermute | solution.py:957
  55.5 21.0 %collective-permute-start.10 = (bf16[832,256]{1,0:T(8,128)(2,1)S(1)}, bf16[832,256]{1,0:T(8,128)(2,1)S(1)}, u32[]{:S(2)}, u32[]{:S(2)}) collective-permute-start(bf16[832,256]{1,0:T(8,128)(2,1)S(1)} %get-tuple-element.131), channel_id=1, source_target_pairs={{0,3},{1,2},{2,1},{3,0},{4,7},{5,6},{6,5},{7,4},{8,11},{9,10},{10,... | collective-permute-start | bytes 1277960 | tf_op jit(solution)/shard_map/ppermute | solution.py:957
  72.2 11.9 %collective-permute-start.12 = (bf16[192,256]{1,0:T(8,128)(2,1)S(1)}, bf16[192,256]{1,0:T(8,128)(2,1)S(1)}, u32[]{:S(2)}, u32[]{:S(2)}) collective-permute-start(bf16[192,256]{1,0:T(8,128)(2,1)S(1)} %get-tuple-element.148), channel_id=1, source_target_pairs={{0,1},{1,0},{2,3},{3,2},{4,5},{5,4},{6,7},{7,6},{8,9},{9,8},{10,11... | collective-permute-start | bytes 294920 | tf_op jit(solution)/shard_map/ppermute | solution.py:957
  72.5 11.6 %collective-permute-start.13 = (bf16[192,256]{1,0:T(8,128)(2,1)S(1)}, bf16[192,256]{1,0:T(8,128)(2,1)S(1)}, u32[]{:S(2)}, u32[]{:S(2)}) collective-permute-start(bf16[192,256]{1,0:T(8,128)(2,1)S(1)} %get-tuple-element.149), channel_id=1, source_target_pairs={{0,2},{1,3},{2,0},{3,1},{4,6},{5,7},{6,4},{7,5},{8,10},{9,11},{10,... | collective-permute-start | bytes 294920 | tf_op jit(solution)/shard_map/ppermute | solution.py:957
  72.7 11.3 %collective-permute-start.14 = (bf16[192,256]{1,0:T(8,128)(2,1)S(1)}, bf16[192,256]{1,0:T(8,128)(2,1)S(1)}, u32[]{:S(2)}, u32[]{:S(2)}) collective-permute-start(bf16[192,256]{1,0:T(8,128)(2,1)S(1)} %get-tuple-element.150), channel_id=1, source_target_pairs={{0,3},{1,2},{2,1},{3,0},{4,7},{5,6},{6,5},{7,4},{8,11},{9,10},{10,... | collective-permute-start | bytes 294920 | tf_op jit(solution)/shard_map/ppermute | solution.py:957
  76.7 11.6 %collective-permute-start.11 = (bf16[832,256]{1,0:T(8,128)(2,1)S(1)}, bf16[832,256]{1,0:T(8,128)(2,1)S(1)}, u32[]{:S(2)}, u32[]{:S(2)}) collective-permute-start(bf16[832,256]{1,0:T(8,128)(2,1)S(1)} %add_convert_fusion.2), channel_id=1, source_target_pairs={{0,4},{4,0},{8,12},{12,8},{16,20},{20,16},{24,28},{28,24},{1,5},{5... | collective-permute-start | bytes 1277960 | tf_op jit(solution)/shard_map/ppermute | solution.py:957
  88.6 8.8 %collective-permute-start.16 = (bf16[192,256]{1,0:T(8,128)(2,1)S(1)}, bf16[192,256]{1,0:T(8,128)(2,1)S(1)}, u32[]{:S(2)}, u32[]{:S(2)}) collective-permute-start(bf16[192,256]{1,0:T(8,128)(2,1)S(1)} %add_convert_fusion.5), channel_id=1, source_target_pairs={{0,4},{4,0},{8,12},{12,8},{16,20},{20,16},{24,28},{28,24},{1,5},{5... | collective-permute-start | bytes 294920 | tf_op jit(solution)/shard_map/ppermute | solution.py:957
  88.8 10.6 %collective-permute-start.15 = (bf16[832,256]{1,0:T(8,128)(2,1)S(1)}, bf16[832,256]{1,0:T(8,128)(2,1)S(1)}, u32[]{:S(2)}, u32[]{:S(2)}) collective-permute-start(bf16[832,256]{1,0:T(8,128)(2,1)S(1)} %add_convert_fusion.1), channel_id=1, source_target_pairs={{0,8},{4,12},{8,0},{12,4},{16,24},{20,28},{24,16},{28,20},{1,9},{5... | collective-permute-start | bytes 1277960 | tf_op jit(solution)/shard_map/ppermute | solution.py:957
  99.6 20.7 %collective-permute-start.22 = (bf16[832,256]{1,0:T(8,128)(2,1)S(1)}, bf16[832,256]{1,0:T(8,128)(2,1)S(1)}, u32[]{:S(2)}, u32[]{:S(2)}) collective-permute-start(bf16[832,256]{1,0:T(8,128)(2,1)S(1)} %add_convert_fusion.first), channel_id=1, source_target_pairs={{0,16},{4,20},{8,24},{12,28},{16,0},{20,4},{24,8},{28,12},{1,17},{... | collective-permute-start | bytes 1277960 | tf_op jit(solution)/shard_map/ppermute | solution.py:957
  110.4 12.8 %collective-permute-start.19 = (bf16[176,256]{1,0:T(8,128)(2,1)S(1)}, bf16[176,256]{1,0:T(8,128)(2,1)S(1)}, u32[]{:S(2)}, u32[]{:S(2)}) collective-permute-start(bf16[176,256]{1,0:T(8,128)(2,1)S(1)} %get-tuple-element.182), channel_id=1, source_target_pairs={{0,1},{1,0},{2,3},{3,2},{4,5},{5,4},{6,7},{7,6},{8,9},{9,8},{10,11... | collective-permute-start | bytes 270344 | tf_op jit(solution)/shard_map/ppermute | solution.py:957
  112.3 10.9 %collective-permute-start.20 = (bf16[176,256]{1,0:T(8,128)(2,1)S(1)}, bf16[176,256]{1,0:T(8,128)(2,1)S(1)}, u32[]{:S(2)}, u32[]{:S(2)}) collective-permute-start(bf16[176,256]{1,0:T(8,128)(2,1)S(1)} %get-tuple-element.183), channel_id=1, source_target_pairs={{0,2},{1,3},{2,0},{3,1},{4,6},{5,7},{6,4},{7,5},{8,10},{9,11},{10,... | collective-permute-start | bytes 270344 | tf_op jit(solution)/shard_map/ppermute | solution.py:957
  112.8 10.4 %collective-permute-start.21 = (bf16[176,256]{1,0:T(8,128)(2,1)S(1)}, bf16[176,256]{1,0:T(8,128)(2,1)S(1)}, u32[]{:S(2)}, u32[]{:S(2)}) collective-permute-start(bf16[176,256]{1,0:T(8,128)(2,1)S(1)} %get-tuple-element.184), channel_id=1, source_target_pairs={{0,3},{1,2},{2,1},{3,0},{4,7},{5,6},{6,5},{7,4},{8,11},{9,10},{10,... | collective-permute-start | bytes 270344 | tf_op jit(solution)/shard_map/ppermute | solution.py:957
  128.6 20.1 %collective-permute-start.18 = (bf16[192,256]{1,0:T(8,128)(2,1)S(1)}, bf16[192,256]{1,0:T(8,128)(2,1)S(1)}, u32[]{:S(2)}, u32[]{:S(2)}) collective-permute-start(bf16[192,256]{1,0:T(8,128)(2,1)S(1)} %add_convert_fusion.3.score_first), channel_id=1, source_target_pairs={{0,16},{4,20},{8,24},{12,28},{16,0},{20,4},{24,8},{28,12},{1,17},{... | collective-permute-start | bytes 294920 | tf_op jit(solution)/shard_map/ppermute | solution.py:957
  131.8 16.9 %collective-permute-start.25 = (bf16[176,256]{1,0:T(8,128)(2,1)S(1)}, bf16[176,256]{1,0:T(8,128)(2,1)S(1)}, u32[]{:S(2)}, u32[]{:S(2)}) collective-permute-start(bf16[176,256]{1,0:T(8,128)(2,1)S(1)} %add_convert_fusion.6.edge_first), channel_id=1, source_target_pairs={{0,16},{4,20},{8,24},{12,28},{16,0},{20,4},{24,8},{28,12},{1,17},{... | collective-permute-start | bytes 270344 | tf_op jit(solution)/shard_map/ppermute | solution.py:957
  133.7 10.3 %collective-permute-start.26 = (bf16[96,256]{1,0:T(8,128)(2,1)S(1)}, bf16[96,256]{1,0:T(8,128)(2,1)S(1)}, u32[]{:S(2)}, u32[]{:S(2)}) collective-permute-start(bf16[96,256]{1,0:T(8,128)(2,1)S(1)} %get-tuple-element.200), channel_id=1, source_target_pairs={{0,1},{1,2},{2,3},{3,4},{4,5},{5,6},{6,7},{7,8},{8,9},{9,10},{10,1... | collective-permute-start | bytes 147464 | tf_op jit(solution)/shard_map/ppermute | solution.py:964
  (26 other events, 234.6 us)

commit v4 on v3

--- a/solution.py
+++ b/solution.py
@@ -128,8 +128,9 @@
 
 
 def write_group(geometry, group, basis, window, out_ref):
+    pairs = GROUP // LANES
     scaled, heights, relative = (
-        ref[group * (GROUP // LANES) : (group + 1) * (GROUP // LANES), :] for ref in geometry
+        geometry[which, group * pairs : (group + 1) * pairs, :] for which in range(3)
     )
     write_onehot(relative, window, out_ref)
     write_basis(scaled, heights, *basis, window, out_ref)
@@ -220,15 +221,16 @@
     )(index, rbf, query, key, value, out, gate, up, down, *rest)
 
 
-def geometry_kernel(factor, dist_ref, rows_ref, scaled_ref, heights_ref, relative_ref):
+def geometry_kernel(factor, dist_ref, rows_ref, out_ref, done_ref):
     dist = dist_ref[...].T
     rows = rows_ref[...].astype(F32).T
-    for block in range(scaled_ref.shape[0]):
+    for block in range(out_ref.shape[0]):
         place = slice(block * BLOCK, (block + 1) * BLOCK)
         pairs = pair_rows(dist[place])
-        scaled_ref[block] = pairs * factor
-        heights_ref[block] = 0.5 * (jnp.cos(jnp.pi * pairs / CUTOFF) + 1.0)
-        relative_ref[block] = pair_rows(rows[place]) - float(block * BLOCK)
+        out_ref[block, 0] = pairs * factor
+        out_ref[block, 1] = 0.5 * (jnp.cos(jnp.pi * pairs / CUTOFF) + 1.0)
+        out_ref[block, 2] = pair_rows(rows[place]) - float(block * BLOCK)
+    done_ref[...] = jnp.zeros_like(done_ref)
 
 
 def geometry_call(distances, neighbours, factor):
@@ -237,9 +239,12 @@
     vmem = pl.BlockSpec(memory_space=pltpu.VMEM)
     return pl.pallas_call(
         functools.partial(geometry_kernel, factor),
-        out_shape=(jax.ShapeDtypeStruct((blocks, PAIRS, LANES), F32),) * 3,
+        out_shape=(
+            jax.ShapeDtypeStruct((blocks, 3, PAIRS, LANES), F32),
+            jax.ShapeDtypeStruct((8, LANES), F32),
+        ),
         in_specs=[vmem, vmem],
-        out_specs=(vmem,) * 3,
+        out_specs=(vmem,) * 2,
         cost_estimate=pl.CostEstimate(
             flops=40 * atoms * slots, bytes_accessed=20 * atoms * slots, transcendentals=0
         ),
@@ -279,9 +284,7 @@
     pack1,
     pack2,
     pack3,
-    scaled_ref,
-    heights_ref,
-    relative_ref,
+    geometry,
     edge_ref,
     power_ref,
     inverse_ref,
@@ -334,7 +337,6 @@
 
     table = lookup_ref[pl.ds(pl.multiple_of(step * BLOCK, BLOCK), window), :]
     weight_t[:, :window] = table.astype(F32).T.astype(BF16)
-    geometry = (scaled_ref, heights_ref, relative_ref)
     write_group(geometry, 0, basis, window, phis[0])
     for group in range(groups):
         if group + 1 < groups:
@@ -415,7 +417,7 @@
             full((HALO, width)),
         ]
         + [full(pack.shape) for pack in packs]
-        + [pl.BlockSpec((None, PAIRS, LANES), lambda b: (b, 0, 0))] * 3,
+        + [pl.BlockSpec((None, 3, PAIRS, LANES), lambda b: (b, 0, 0, 0))],
         out_specs=(
             pl.BlockSpec((None, width, edges), lambda b: (b, 0, 0)),
             pl.BlockSpec((None, PAIRS * HEADS, LANES), lambda b: (b, 0, 0)),
@@ -442,13 +444,14 @@
             transcendentals=atoms * slots * rows,
         ),
         name="attention_forward",
-    )(index, counts, features, before, after, *packs, *geometry)
+    )(index, counts, features, before, after, *packs, geometry)
 
 
 def ffn_kernel(
     quarter,
     small_row,
     index_ref,
+    side_ref,
     features_ref,
     attended_ref,
     grad_out_ref,
@@ -528,25 +531,32 @@
     grad_proj = grad_residual.astype(BF16)
     grad_attended_ref[...] = nt(grad_proj, w_out[...]).astype(BF16)
     g_out[...] = tn(attended, grad_proj)
+    half = grads0.shape[0] // 2
+    first = side_ref[0] * half
     for offset, grads in enumerate((grads0, grads1, grads2, grads3)):
         owner = lax.bitwise_xor(me, offset)
         rows = pl.ds(pl.multiple_of(owner * quarter, 16), quarter)
-        row = 0
+        pieces = []
         for grad in (g_gate, g_up):
             for part in range(parts):
-                lanes = slice(part * width, (part + 1) * width)
-                grads[row : row + quarter, :] = grad[rows, lanes].astype(BF16)
-                row += quarter
-        down = pl.ds(pl.multiple_of(owner * down_rows, 16), down_rows)
-        grads[row : row + down_rows, :] = g_down[down, :].astype(BF16)
-        row += down_rows
-        grads[row : row + quarter, :] = g_out[rows, :].astype(BF16)
+                pieces.append(grad[rows, part * width : (part + 1) * width])
+        down = pl.multiple_of(owner * down_rows, 16)
+        pieces += [g_down[pl.ds(down, down_rows), :], g_out[rows, :]]
+        row = 0
+        for piece in pieces:
+            for start in range(0, piece.shape[0], quarter // 2):
+                other = row + half if row < half else row - half
+                place = pl.multiple_of(jnp.where(first == 0, row, other), 16)
+                grads[pl.ds(place, quarter // 2), :] = piece[start : start + quarter // 2].astype(
+                    BF16
+                )
+                row += quarter // 2
     sums_ref[...] = jnp.zeros_like(sums_ref)
     sums_ref[1:2, :] = jnp.sum(grad_hidden * normed, 0, keepdims=True)
     sums_ref[2:3, :] = jnp.sum(grad_energy * outputs, 0, keepdims=True)
 
 
-def ffn_call(index, features, attended, grad_out, grad_energy, small, packs, hidden, quarter, row):
+def ffn_call(index, side, features, attended, grad_out, grad_energy, small, packs, hidden, quarter, row):
     atoms, width = features.shape
     vmem = pl.BlockSpec(memory_space=pltpu.VMEM)
     return pl.pallas_call(
@@ -559,7 +569,7 @@
             jax.ShapeDtypeStruct((8, width), F32),
         )
         + (jax.ShapeDtypeStruct(packs[0].shape, BF16),) * 4,
-        in_specs=[pl.BlockSpec(memory_space=pltpu.SMEM)] + [vmem] * 12,
+        in_specs=[pl.BlockSpec(memory_space=pltpu.SMEM)] * 2 + [vmem] * 12,
         out_specs=(vmem,) * 9,
         scratch_shapes=[
             pltpu.VMEM(shape, dtype)
@@ -571,7 +581,7 @@
             flops=18 * atoms * width * hidden, bytes_accessed=2**23, transcendentals=atoms * hidden
         ),
         name="feed_forward",
-    )(index, features, attended, grad_out, grad_energy, *small, *packs)
+    )(index, side, features, attended, grad_out, grad_energy, *small, *packs)
 
 
 def score_kernel(
@@ -736,7 +746,7 @@
 def edge_kernel(basis, gain_row, first_block, last_block, carried, final, *refs):
     refs = list(refs)
     take = lambda count: [refs.pop(0) for _ in range(count)]
-    geometry, (power_ref, grad_score_ref, mixed_ref) = take(3), take(3)
+    geometry, power_ref, grad_score_ref, mixed_ref = take(4)
     before = take(2 if carried else 0)
     if final:
         index_ref, features_ref, before_ref, after_ref, grad_query_ref, kvq_ref = take(6)
@@ -831,9 +841,7 @@
     full = lambda shape: pl.BlockSpec(shape, lambda b: (0,) * len(shape))
     here = lambda b: (b + first_block, 0, 0)
     in_specs = [
-        pl.BlockSpec((None, PAIRS, LANES), here),
-        pl.BlockSpec((None, PAIRS, LANES), here),
-        pl.BlockSpec((None, PAIRS, LANES), here),
+        pl.BlockSpec((None, 3, PAIRS, LANES), lambda b: (b + first_block, 0, 0, 0)),
         pl.BlockSpec((None, PAIRS * HEADS, LANES), here),
         pl.BlockSpec((None, PAIRS * HEADS, LANES), here),
         pl.BlockSpec((groups, width, 2 * group_rows), here),
@@ -874,58 +882,66 @@
     )(*operands)
 
 
-def large_kernel(first, second, gate, up, down, out):
-    total = lambda rows: first[rows, :].astype(F32) + second[rows, :].astype(F32)
+def early_kernel(
+    side_ref,
+    own_half,
+    other_half,
+    score_first,
+    score_second,
+    grad_own,
+    from_lower,
+    from_upper,
+    gate,
+    up,
+    down,
+    out,
+    query,
+    key,
+    value,
+    features,
+    total,
+):
+    half = own_half.shape[0]
+    own = side_ref[0]
+    total[pl.ds(pl.multiple_of(own * half, 16), half), :] = own_half[...].astype(F32)
+    total[pl.ds(pl.multiple_of((1 - own) * half, 16), half), :] = other_half[...].astype(F32)
     quarter, width = out.shape
     row = 0
     for ref in (gate, up):
         for part in range(ref.shape[1] // width):
-            ref[:, part * width : (part + 1) * width] = total(slice(row, row + quarter))
+            ref[:, part * width : (part + 1) * width] = total[row : row + quarter, :]
             row += quarter
     for ref in (down, out):
-        ref[...] = total(slice(row, row + ref.shape[0]))
+        ref[...] = total[row : row + ref.shape[0], :]
         row += ref.shape[0]
-
-
-def large_call(first, second, quarter, hidden, down_rows):
-    width = first.shape[1]
-    vmem = pl.BlockSpec(memory_space=pltpu.VMEM)
-    shapes = ((quarter, hidden), (quarter, hidden), (down_rows, width), (quarter, width))
-    return pl.pallas_call(
-        large_kernel,
-        out_shape=[jax.ShapeDtypeStruct(shape, F32) for shape in shapes],
-        in_specs=[vmem] * 2,
-        out_specs=[vmem] * 4,
-        name="feed_forward_results",
-    )(first, second)
-
-
-def small_kernel(
-    index_ref,
-    score_first,
-    score_second,
-    edge_first,
-    edge_second,
-    grad_own,
-    from_lower,
-    from_upper,
-    rbf,
-    query,
-    key,
-    value,
-    gain_attn,
-    gain_ffn,
-    readout,
-    features,
-):
-    quarter = query.shape[0]
-    width = query.shape[1]
     for which, ref in enumerate((query, key, value)):
         rows = slice(which * quarter, (which + 1) * quarter)
         ref[...] = score_first[rows, :].astype(F32) + score_second[rows, :].astype(F32)
-    total = edge_first[...].astype(F32) + edge_second[...].astype(F32)
+    features[...] = grad_own[...]
+    features[:HALO, :] += from_lower[...].astype(F32)
+    features[features.shape[0] - HALO :, :] += from_upper[...].astype(F32)
+
+
+def early_call(side, halves, score, grad_own, from_lower, from_upper, quarter, hidden, down_rows):
+    rows, width = halves[0].shape
+    vmem = pl.BlockSpec(memory_space=pltpu.VMEM)
+    shapes = [(quarter, hidden)] * 2 + [(down_rows, width)] + [(quarter, width)] * 4
+    shapes += [grad_own.shape]
+    return pl.pallas_call(
+        early_kernel,
+        out_shape=[jax.ShapeDtypeStruct(shape, F32) for shape in shapes],
+        in_specs=[pl.BlockSpec(memory_space=pltpu.SMEM)] + [vmem] * 7,
+        out_specs=[vmem] * 8,
+        scratch_shapes=[pltpu.VMEM((2 * rows, width), F32)],
+        name="early_results",
+    )(side, *halves, *score, grad_own, from_lower, from_upper)
+
+
+def last_kernel(index_ref, first, second, rbf, gain_attn, gain_ffn, readout):
+    total = first[...].astype(F32) + second[...].astype(F32)
     rbf[...] = total[: rbf.shape[0]]
-    start = edge_first.shape[0] - 16
+    start, width = first.shape[0] - 16, first.shape[1]
+    quarter = readout.shape[1]
     me = index_ref[0]
     for which, ref in enumerate((gain_attn, gain_ffn, readout)):
         row = total[start + which : start + which + 1]
@@ -934,22 +950,19 @@
             piece = row[:, owner * quarter : (owner + 1) * quarter]
             picked = picked + jnp.where(me == owner, piece, 0.0)
         ref[...] = picked
-    features[...] = grad_own[...]
-    features[:HALO, :] += from_lower[...].astype(F32)
-    features[features.shape[0] - HALO :, :] += from_upper[...].astype(F32)
-
-
-def small_call(index, score, edge, grad_own, from_lower, from_upper, shard, quarter):
-    width = grad_own.shape[1]
+
+
+def last_call(index, terms, shard, quarter):
+    width = terms[0].shape[1]
     vmem = pl.BlockSpec(memory_space=pltpu.VMEM)
-    shapes = [(shard, width)] + [(quarter, width)] * 3 + [(1, quarter)] * 3 + [grad_own.shape]
+    shapes = [(shard, width)] + [(1, quarter)] * 3
     return pl.pallas_call(
-        small_kernel,
+        last_kernel,
         out_shape=[jax.ShapeDtypeStruct(shape, F32) for shape in shapes],
-        in_specs=[pl.BlockSpec(memory_space=pltpu.SMEM)] + [vmem] * 7,
-        out_specs=[vmem] * 8,
-        name="edge_results",
-    )(index, *score, *edge, grad_own, from_lower, from_upper)
+        in_specs=[pl.BlockSpec(memory_space=pltpu.SMEM)] + [vmem] * 2,
+        out_specs=[vmem] * 4,
+        name="last_results",
+    )(index, *terms)
 
 
 def exchange(value, axis, offset):
@@ -976,22 +989,36 @@
 
 
 class Reduction:
-    def __init__(self, chunks):
-        self.offsets = [1 << bit for bit in range(lax.axis_size("space").bit_length() - 1)]
+    def __init__(self, chunks, halved=False):
+        self.halved = halved
+        self.sent = 0
+        self.steps = lax.axis_size("space").bit_length() - 1
         self.terms = [chunks[0]] + [
             exchange(chunk, "wt", offset) for offset, chunk in enumerate(chunks[1:], 1)
         ]
 
+    def done(self):
+        return self.sent == self.steps + (1 if self.halved else 0)
+
     def add(self):
-        if self.offsets:
+        if not self.done():
             self.terms = [added(*self.terms)]
 
     def send(self):
-        if self.offsets:
-            self.terms.append(exchange(self.terms[0], "space", self.offsets.pop(0)))
+        if self.done():
+            return
+        (value,) = self.terms
+        if self.sent == self.steps:
+            self.terms.append(exchange(value, "space", 1))
+        elif self.sent == 0 and self.halved:
+            rows = value.shape[0] // 2
+            self.terms = [value[:rows], exchange(value[rows:], "space", 1)]
+        else:
+            self.terms.append(exchange(value, "space", 1 << self.sent))
+        self.sent += 1
 
     def finish(self):
-        while self.offsets:
+        while not self.done():
             self.add()
             self.send()
         return self.terms
@@ -1043,6 +1070,7 @@
     quarter = query_weight.shape[0]
     hidden = gate_weight.shape[1]
     index = lax.axis_index("wt").astype(jnp.int32)[None]
+    side = (lax.axis_index("space") % 2).astype(jnp.int32)[None]
 
     small, large, initial, final = pack_call(
         index,
@@ -1062,8 +1090,8 @@
     small_all = gathered(small)
     before = shifted(final, 1)
     after = shifted(initial, -1)
-    geometry = geometry_call(distances.T, neighbours.T, factor)
-    large, geometry = lax.optimization_barrier((large, geometry))
+    geometry, done = geometry_call(distances.T, neighbours.T, factor)
+    large, _ = lax.optimization_barrier((large, done))
     large_all = gathered(large)
 
     edge, power, inverse, pooled, attended, lookup, query, kvq = forward_call(
@@ -1071,6 +1099,7 @@
     )
     outputs, energy, grad_residual, grad_attended, sums, *large_grads = ffn_call(
         index,
+        side,
         features,
         attended,
         grad_out,
@@ -1084,7 +1113,7 @@
     grad_score, mixed, grad_query, *score_grads = score_call(
         index, lookup, query, kvq, pooled, inverse, attended, grad_attended, power, edge, quarter
     )
-    large_sum, score_sum = Reduction(large_grads), Reduction(score_grads)
+    large_sum, score_sum = Reduction(large_grads, True), Reduction(score_grads)
     carry, block = None, 0
     last = (index, features, before, after, grad_query, kvq, grad_residual, sums, *small_all)
     for count in SPLIT:
@@ -1094,7 +1123,7 @@
             carry = between([large_sum, score_sum], carry)
         final = block + count == edge.shape[0]
         carry = edge_call(
-            (*geometry, power, grad_score, mixed),
+            (geometry, power, grad_score, mixed),
             carry,
             last if final else None,
             basis,
@@ -1108,12 +1137,26 @@
     edge_sum = Reduction(edge_grads)
     from_upper = shifted(grad_lower, -1)
     from_lower = shifted(grad_upper, 1)
-    score_sum = score_sum.finish()
-    results = large_call(*large_sum.finish(), quarter, hidden, down_weight.shape[0])
-    grad_gate, grad_up, grad_down, grad_out_w = between([edge_sum], results)
-    edge_sum = edge_sum.finish()
-    grad_rbf, grad_q, grad_k, grad_v, grad_attn, grad_ffn, grad_read, grad_features = small_call(
-        index, score_sum, edge_sum, grad_own, from_lower, from_upper, shard, quarter
+    between([edge_sum, large_sum], ())
+    large_sum, score_sum, from_upper, from_lower = between(
+        [edge_sum], (large_sum.finish(), score_sum.finish(), from_upper, from_lower)
+    )
+    results = early_call(
+        side,
+        large_sum,
+        score_sum,
+        grad_own,
+        from_lower,
+        from_upper,
+        quarter,
+        hidden,
+        down_weight.shape[0],
+    )
+    grad_gate, grad_up, grad_down, grad_out_w, grad_q, grad_k, grad_v, grad_features = between(
+        [edge_sum], results
+    )
+    grad_rbf, grad_attn, grad_ffn, grad_read = last_call(
+        index, edge_sum.finish(), shard, quarter
     )
     return (
         outputs,

time: 152 us -> 139 us (0.914)
  the two profiles are of different devices: /device:TPU:7 before, /device:TPU:0 now
where the time goes in v4:
time: 139 us; the launch traced here: 138 us
  Pallas kernels  78.1 us (56%)
  starting transfers between devices  39.3 us (28%)
  waiting for transfers between devices  12.9 us (9%)
  local copies, waits for them, and re-layouts  5.64 us (4%)
    ppermute x25, starting transfers between devices, exchange(): return lax.ppermute(value, axis, [(i, i ^ offset) for i in range(size)])  31.3 us
    pallas_call x1, Pallas kernels, forward_call(): pl.pallas_call(functools.partial(forward_kernel, basis, quarter, (width /...  28.3 us
    pallas_call x3, Pallas kernels, edge_call(): pl.pallas_call(functools.partial(edge_kernel, basis, gain_row, first_bloc...  22 us
    pallas_call x1, Pallas kernels, score_call(): pl.pallas_call(functools.partial(score_kernel, quarter, (width // HEADS)...  15.1 us
    ppermute x25, waiting for transfers between devices, exchange(): return lax.ppermute(value, axis, [(i, i ^ offset) for i in range(size)])  12 us
    ppermute x4, starting transfers between devices, shifted(): return lax.ppermute(value, axes, pairs)  7.96 us
    unnamed x34, local copies, waits for them, and re-layouts  4.93 us
    pallas_call x1, Pallas kernels, ffn_call(): pl.pallas_call(functools.partial(ffn_kernel, quarter, row), out_shape=(ja...  4.3 us
  transfers between devices with their start and end apart: 29, of which 8 were waited for; matrix products, arithmetic and copies ran while one was open for 1% of the time, Pallas kernels for 51%

profile of v4, /device:TPU:0, one launch (start us, length us, event | category | flops | bytes accessed | tf_op | source)
XLA Modules:
  0.0 138.1 jit_solution(10864149065158338585)
XLA Ops:
  0.7 2.1 %pack_weights.1 = (bf16[368,256]{1,0:T(8,128)(2,1)}, bf16[832,256]{1,0:T(8,128)(2,1)}, bf16[96,256]{1,0:T(8,128)(2,1)}, bf16[96,256]{1,0:T(8,128)(2,1)}) custom-call(s32[1]{0:T(128)} %bitcast.index_ref.refs_6_, bf16[150,256]{1,0:T(8,128)(2,1)} %rbf_ref.1, bf16[64,256]{1,0:T(8,128)(2,1)} %query_ref.1, bf16[64,256]{1,0:T(8,128)(2,1)} %key_ref.1, ...), custom_call_target="tpu_custom_call" | custom-call | bytes 2097152 | tf_op jit(solution)/shard_map/pack_weights/pallas_call | solution.py:209
  2.8 2.4 %collective-permute-start.4 = (bf16[368,256]{1,0:T(8,128)(2,1)}, bf16[368,256]{1,0:T(8,128)(2,1)S(1)}, u32[]{:S(2)}, u32[]{:S(2)}) collective-permute-start(bf16[368,256]{1,0:T(8,128)(2,1)} %get-tuple-element.139.pack0.small0.refs_14_), channel_id=1, source_target_pairs={{0,3},{1,2},{2,1},{3,0},{4,7},{5,6},{6,5},{7,4},{8,11},{9,10},{10,... | collective-permute-start | bytes 565256 | tf_op jit(solution)/shard_map/ppermute | solution.py:970
  5.8 2.4 %collective-permute-start = (bf16[96,256]{1,0:T(8,128)(2,1)}, bf16[96,256]{1,0:T(8,128)(2,1)S(1)}, u32[]{:S(2)}, u32[]{:S(2)}) collective-permute-start(bf16[96,256]{1,0:T(8,128)(2,1)} %get-tuple-element.137), channel_id=1, source_target_pairs={{0,1},{1,2},{2,3},{3,4},{4,5},{5,6},{6,7},{7,8},{8,9},{9,10},{10,1... | collective-permute-start | bytes 147464 | tf_op jit(solution)/shard_map/ppermute | solution.py:977
  10.2 2.2 %edge_geometry.1 = (f32[6,3,32,128]{3,2,1,0:T(8,128)}, f32[8,128]{1,0:T(8,128)}) custom-call(f32[64,384]{1,0:T(8,128)} %bitcast.10, s32[64,384]{1,0:T(8,128)} %bitcast.11), custom_call_target="tpu_custom_call" | custom-call | flops 983040 | bytes 491520 | tf_op jit(solution)/shard_map/edge_geometry/pallas_call | solution.py:240
  12.4 3.1 %collective-permute-start.7 = (bf16[832,256]{1,0:T(8,128)(2,1)}, bf16[832,256]{1,0:T(8,128)(2,1)S(1)}, u32[]{:S(2)}, u32[]{:S(2)}) collective-permute-start(bf16[832,256]{1,0:T(8,128)(2,1)} %get-tuple-element.142.pack0), channel_id=1, source_target_pairs={{0,3},{1,2},{2,1},{3,0},{4,7},{5,6},{6,5},{7,4},{8,11},{9,10},{10,... | collective-permute-start | bytes 1277960 | tf_op jit(solution)/shard_map/ppermute | solution.py:970
  15.5 2.0 %collective-permute-start.6 = (bf16[832,256]{1,0:T(8,128)(2,1)}, bf16[832,256]{1,0:T(8,128)(2,1)S(1)}, u32[]{:S(2)}, u32[]{:S(2)}) collective-permute-start(bf16[832,256]{1,0:T(8,128)(2,1)} %get-tuple-element.142.pack0), channel_id=1, source_target_pairs={{0,2},{1,3},{2,0},{3,1},{4,6},{5,7},{6,4},{7,5},{8,10},{9,11},{10,... | collective-permute-start | bytes 1277960 | tf_op jit(solution)/shard_map/ppermute | solution.py:970
  22.1 28.3 %attention_forward.1 = (bf16[6,256,4096]{2,1,0:T(8,128)(2,1)S(1)}, bf16[6,256,128]{2,1,0:T(8,128)(2,1)S(1)}, f32[3072,128]{1,0:T(8,128)S(1)}, bf16[3072,256]{1,0...) custom-call(s32[1]{0:T(128)} %bitcast.index_ref.refs_6_, ...), custom_call_target="tpu_custom_call" | custom-call | flops 11676942336 | bytes 42467328 | tf_op jit(solution)/shard_map/attention_forward/pallas_call | solution.py:394
  50.4 4.3 %feed_forward.1 = (f32[384,256]{1,0:T(8,128)}, f32[1,384]{1,0:T(1,128)S(1)}, f32[384,256]{1,0:T(8,128)S(1)}, bf16[384,256]{1,0:T(8,128)(2,1)S(1)}, f32[8,256]{1,...) custom-call(s32[1]{0:T(128)} %bitcast.index_ref.refs_6_, ...), custom_call_target="tpu_custom_call" | custom-call | flops 1811939328 | bytes 8388608 | tf_op jit(solution)/shard_map/feed_forward/pallas_call | solution.py:562
  56.6 15.1 %score_backward.1 = (f32[6,256,128]{2,1,0:T(8,128)S(1)}, bf16[24,256,256]{2,1,0:T(8,128)(2,1)S(1)}, bf16[384,256]{1,0:T(8,128)(2,1)S(1)}, bf16[192,256]{1,0:T(8,...) custom-call(s32[1]{0:T(128)} %bitcast.index_ref.refs_6_, ...), custom_call_target="tpu_custom_call" | custom-call | flops 3221225472 | bytes 12582912 | tf_op jit(solution)/shard_map/score_backward/pallas_call | solution.py:708
  73.6 2.0 %collective-permute-done.10 = bf16[832,256]{1,0:T(8,128)(2,1)S(1)} collective-permute-done((bf16[832,256]{1,0:T(8,128)(2,1)S(1)}, bf16[832,256]{1,0:T(8,128)(2,1)S(1)}, u32[]{:S(2)}, u32[]{:S(2)}) %collective-permute-start.10) | collective-permute-done | bytes 426016 | tf_op jit(solution)/shard_map/ppermute | solution.py:970
  77.2 7.2 %edge_backward.3 = (f32[608,256]{1,0:T(8,128)S(1)}, f32[576,256]{1,0:T(8,128)S(1)}) custom-call(f32[6,3,32,128]{3,2,1,0:T(8,128)S(1)} %copy-done.5, bf16[6,256,128]{2,1,0:T(8,128)(2,1)S(1)} %get-tuple-element.145.power_ref.refs_1_, f32[6,256,128]{2,1,0:T(8,128)S(1)} %get-tuple-element.163.refs_2_, bf16[24,256,256]{2,1,0:T(8,128)(2,1)S(1)} %get-tuple-element.164.refs_3_), custom_call_target="tpu_custom_call" | custom-call | flops 4697620480 | bytes 4194304 | tf_op jit(solution)/shard_map/edge_backward/pallas_call | solution.py:866
  85.5 1.6 %collective-permute-start.15 = (bf16[416,256]{1,0:T(8,128)(2,1)S(1)}, bf16[416,256]{1,0:T(8,128)(2,1)S(1)}, u32[]{:S(2)}, u32[]{:S(2)}) collective-permute-start(bf16[416,256]{1,0:T(8,128)(2,1)S(1)} %add_convert_fusion.3), channel_id=1, source_target_pairs={{0,8},{4,12},{8,0},{12,4},{16,24},{20,28},{24,16},{28,20},{1,9},{5... | collective-permute-start | bytes 638984 | tf_op jit(solution)/shard_map/ppermute | solution.py:970
  87.1 7.2 %edge_backward.4 = (f32[608,256]{1,0:T(8,128)S(1)}, f32[576,256]{1,0:T(8,128)S(1)}) custom-call(f32[6,3,32,128]{3,2,1,0:T(8,128)S(1)} %copy-done.5, bf16[6,256,128]{2,1,0:T(8,128)(2,1)S(1)} %get-tuple-element.145.power_ref.refs_1_, f32[6,256,128]{2,1,0:T(8,128)S(1)} %get-tuple-element.163.refs_2_, bf16[24,256,256]{2,1,0:T(8,128)(2,1)S(1)} %get-tuple-element.164.refs_3_, ...), custom_call_target="tpu_custom_call" | custom-call | flops 4697620480 | bytes 4194304 | tf_op jit(solution)/shard_map/edge_backward/pallas_call | solution.py:866
  94.4 2.7 %collective-permute-start.20 = (bf16[416,256]{1,0:T(8,128)(2,1)S(1)}, bf16[416,256]{1,0:T(8,128)(2,1)S(1)}, u32[]{:S(2)}, u32[]{:S(2)}) collective-permute-start(bf16[416,256]{1,0:T(8,128)(2,1)S(1)} %add_convert_fusion.2), channel_id=1, source_target_pairs={{0,16},{4,20},{8,24},{12,28},{16,0},{20,4},{24,8},{28,12},{1,17},{... | collective-permute-start | bytes 638984 | tf_op jit(solution)/shard_map/ppermute | solution.py:970
  97.0 7.6 %edge_backward.5 = (f32[384,256]{1,0:T(8,128)S(1)}, bf16[96,256]{1,0:T(8,128)(2,1)S(1)}, bf16[96,256]{1,0:T(8,128)(2,1)S(1)}, bf16[176,256]{1,0:T(8,128)(2,1)S(1...) custom-call(f32[6,3,32,128]{3,2,1,0:T(8,128)S(1)} %copy-done.5, ...), custom_call_target="tpu_custom_call" | custom-call | flops 4697620480 | bytes 4194304 | tf_op jit(solution)/shard_map/edge_backward/pallas_call | solution.py:866
  105.4 1.4 collective-permute-start.18
  107.7 3.1 %collective-permute-done.18 = bf16[176,256]{1,0:T(8,128)(2,1)S(1)} collective-permute-done((bf16[176,256]{1,0:T(8,128)(2,1)S(1)}, bf16[176,256]{1,0:T(8,128)(2,1)S(1)}, u32[]{:S(2)}, u32[]{:S(2)}) %collective-permute-start.18) | collective-permute-done | bytes 90144 | tf_op jit(solution)/shard_map/ppermute | solution.py:970
  116.0 3.0 %collective-permute-start.26 = (bf16[96,256]{1,0:T(8,128)(2,1)S(1)}, bf16[96,256]{1,0:T(8,128)(2,1)S(1)}, u32[]{:S(2)}, u32[]{:S(2)}) collective-permute-start(bf16[96,256]{1,0:T(8,128)(2,1)S(1)} %get-tuple-element.212), channel_id=1, source_target_pairs={{0,1},{1,2},{2,3},{3,4},{4,5},{5,6},{6,7},{7,8},{8,9},{9,10},{10,1... | collective-permute-start | bytes 147464 | tf_op jit(solution)/shard_map/ppermute | solution.py:977
  119.9 1.3 collective-permute-done.24.score_second
  121.7 5.1 %collective-permute-start.27 = (bf16[176,256]{1,0:T(8,128)(2,1)S(1)}, bf16[176,256]{1,0:T(8,128)(2,1)S(1)}, u32[]{:S(2)}, u32[]{:S(2)}) collective-permute-start(bf16[176,256]{1,0:T(8,128)(2,1)S(1)} %add_convert_fusion.8), channel_id=1, source_target_pairs={{0,8},{4,12},{8,0},{12,4},{16,24},{20,28},{24,16},{28,20},{1,9},{5... | collective-permute-start | bytes 270344 | tf_op jit(solution)/shard_map/ppermute | solution.py:970
  126.9 2.5 %early_results.1 = (f32[64,1024]{1,0:T(8,128)}, f32[64,1024]{1,0:T(8,128)}, f32[256,256]{1,0:T(8,128)}, f32[64,256]{1,0:T(8,128)}, f32[64,256]{1,0:T(8,128)}, /*...) custom-call(s32[1]{0:T(128)} %bitcast.1.side_ref, bf16[416,256]{1,0:T(8,128)(2,1)} %copy-done.9, ...), custom_call_target="tpu_custom_call" | custom-call | tf_op jit(solution)/shard_map/early_results/pallas_call | solution.py:930
  130.4 2.0 %collective-permute-start.28 = (bf16[176,256]{1,0:T(8,128)(2,1)S(1)}, bf16[176,256]{1,0:T(8,128)(2,1)S(1)}, u32[]{:S(2)}, u32[]{:S(2)}) collective-permute-start(bf16[176,256]{1,0:T(8,128)(2,1)S(1)} %add_convert_fusion.7.first), channel_id=1, source_target_pairs={{0,16},{4,20},{8,24},{12,28},{16,0},{20,4},{24,8},{28,12},{1,17},{... | collective-permute-start | bytes 270344 | tf_op jit(solution)/shard_map/ppermute | solution.py:970
  132.9 2.9 %collective-permute-done.28.second = bf16[176,256]{1,0:T(8,128)(2,1)S(1)} collective-permute-done((bf16[176,256]{1,0:T(8,128)(2,1)S(1)}, bf16[176,256]{1,0:T(8,128)(2,1)S(1)}, u32[]{:S(2)}, u32[]{:S(2)}) %collective-permute-start.28) | collective-permute-done | bytes 90144 | tf_op jit(solution)/shard_map/ppermute | solution.py:970
  136.5 1.6 %last_results.1 = (f32[150,256]{1,0:T(8,128)}, f32[1,64]{1,0:T(1,128)}, f32[1,64]{1,0:T(1,128)}, f32[1,64]{1,0:T(1,128)}) custom-call(s32[1]{0:T(128)} %bitcast.index_ref.refs_6_, bf16[176,256]{1,0:T(8,128)(2,1)} %copy-done.11, bf16[176,256]{1,0:T(8,128)(2,1)} %copy-done.14), custom_call_target="tpu_custom_call" | custom-call | tf_op jit(solution)/shard_map/last_results/pallas_call | solution.py:959
  (91 shorter events, 24.0 us)
Async XLA Ops:
  2.8 14.8 %collective-permute-start.4 = (bf16[368,256]{1,0:T(8,128)(2,1)}, bf16[368,256]{1,0:T(8,128)(2,1)S(1)}, u32[]{:S(2)}, u32[]{:S(2)}) collective-permute-start(bf16[368,256]{1,0:T(8,128)(2,1)} %get-tuple-element.139.pack0.small0.refs_14_), channel_id=1, source_target_pairs={{0,3},{1,2},{2,1},{3,0},{4,7},{5,6},{6,5},{7,4},{8,11},{9,10},{10,... | collective-permute-start | bytes 565256 | tf_op jit(solution)/shard_map/ppermute | solution.py:970
  5.2 13.4 %collective-permute-start.3 = (bf16[368,256]{1,0:T(8,128)(2,1)}, bf16[368,256]{1,0:T(8,128)(2,1)S(1)}, u32[]{:S(2)}, u32[]{:S(2)}) collective-permute-start(bf16[368,256]{1,0:T(8,128)(2,1)} %get-tuple-element.139.pack0.small0.refs_14_), channel_id=1, source_target_pairs={{0,2},{1,3},{2,0},{3,1},{4,6},{5,7},{6,4},{7,5},{8,10},{9,11},{10,... | collective-permute-start | bytes 565256 | tf_op jit(solution)/shard_map/ppermute | solution.py:970
  5.8 12.8 %collective-permute-start.2 = (bf16[368,256]{1,0:T(8,128)(2,1)}, bf16[368,256]{1,0:T(8,128)(2,1)S(1)}, u32[]{:S(2)}, u32[]{:S(2)}) collective-permute-start(bf16[368,256]{1,0:T(8,128)(2,1)} %get-tuple-element.139.pack0.small0.refs_14_), channel_id=1, source_target_pairs={{0,1},{1,0},{2,3},{3,2},{4,5},{5,4},{6,7},{7,6},{8,9},{9,8},{10,11... | collective-permute-start | bytes 565256 | tf_op jit(solution)/shard_map/ppermute | solution.py:970
  5.8 6.6 %collective-permute-start = (bf16[96,256]{1,0:T(8,128)(2,1)}, bf16[96,256]{1,0:T(8,128)(2,1)S(1)}, u32[]{:S(2)}, u32[]{:S(2)}) collective-permute-start(bf16[96,256]{1,0:T(8,128)(2,1)} %get-tuple-element.137), channel_id=1, source_target_pairs={{0,1},{1,2},{2,3},{3,4},{4,5},{5,6},{6,7},{7,8},{8,9},{9,10},{10,1... | collective-permute-start | bytes 147464 | tf_op jit(solution)/shard_map/ppermute | solution.py:977
  8.2 7.3 %collective-permute-start.1 = (bf16[96,256]{1,0:T(8,128)(2,1)}, bf16[96,256]{1,0:T(8,128)(2,1)S(1)}, u32[]{:S(2)}, u32[]{:S(2)}) collective-permute-start(bf16[96,256]{1,0:T(8,128)(2,1)} %get-tuple-element.138), channel_id=1, source_target_pairs={{1,0},{2,1},{3,2},{4,3},{5,4},{6,5},{7,6},{8,7},{9,8},{10,9},{11,1... | collective-permute-start | bytes 147464 | tf_op jit(solution)/shard_map/ppermute | solution.py:977
  12.4 37.9 %collective-permute-start.7 = (bf16[832,256]{1,0:T(8,128)(2,1)}, bf16[832,256]{1,0:T(8,128)(2,1)S(1)}, u32[]{:S(2)}, u32[]{:S(2)}) collective-permute-start(bf16[832,256]{1,0:T(8,128)(2,1)} %get-tuple-element.142.pack0), channel_id=1, source_target_pairs={{0,3},{1,2},{2,1},{3,0},{4,7},{5,6},{6,5},{7,4},{8,11},{9,10},{10,... | collective-permute-start | bytes 1277960 | tf_op jit(solution)/shard_map/ppermute | solution.py:970
  15.5 34.8 %collective-permute-start.6 = (bf16[832,256]{1,0:T(8,128)(2,1)}, bf16[832,256]{1,0:T(8,128)(2,1)S(1)}, u32[]{:S(2)}, u32[]{:S(2)}) collective-permute-start(bf16[832,256]{1,0:T(8,128)(2,1)} %get-tuple-element.142.pack0), channel_id=1, source_target_pairs={{0,2},{1,3},{2,0},{3,1},{4,6},{5,7},{6,4},{7,5},{8,10},{9,11},{10,... | collective-permute-start | bytes 1277960 | tf_op jit(solution)/shard_map/ppermute | solution.py:970
  17.6 32.8 %collective-permute-start.5 = (bf16[832,256]{1,0:T(8,128)(2,1)}, bf16[832,256]{1,0:T(8,128)(2,1)S(1)}, u32[]{:S(2)}, u32[]{:S(2)}) collective-permute-start(bf16[832,256]{1,0:T(8,128)(2,1)} %get-tuple-element.142.pack0), channel_id=1, source_target_pairs={{0,1},{1,0},{2,3},{3,2},{4,5},{5,4},{6,7},{7,6},{8,9},{9,8},{10,11... | collective-permute-start | bytes 1277960 | tf_op jit(solution)/shard_map/ppermute | solution.py:970
  54.7 18.2 %collective-permute-start.8 = (bf16[832,256]{1,0:T(8,128)(2,1)S(1)}, bf16[832,256]{1,0:T(8,128)(2,1)S(1)}, u32[]{:S(2)}, u32[]{:S(2)}) collective-permute-start(bf16[832,256]{1,0:T(8,128)(2,1)S(1)} %get-tuple-element.147), channel_id=1, source_target_pairs={{0,1},{1,0},{2,3},{3,2},{4,5},{5,4},{6,7},{7,6},{8,9},{9,8},{10,11... | collective-permute-start | bytes 1277960 | tf_op jit(solution)/shard_map/ppermute | solution.py:970
  54.7 18.9 %collective-permute-start.9 = (bf16[832,256]{1,0:T(8,128)(2,1)S(1)}, bf16[832,256]{1,0:T(8,128)(2,1)S(1)}, u32[]{:S(2)}, u32[]{:S(2)}) collective-permute-start(bf16[832,256]{1,0:T(8,128)(2,1)S(1)} %get-tuple-element.148), channel_id=1, source_target_pairs={{0,2},{1,3},{2,0},{3,1},{4,6},{5,7},{6,4},{7,5},{8,10},{9,11},{10,... | collective-permute-start | bytes 1277960 | tf_op jit(solution)/shard_map/ppermute | solution.py:970
  55.6 20.1 %collective-permute-start.10 = (bf16[832,256]{1,0:T(8,128)(2,1)S(1)}, bf16[832,256]{1,0:T(8,128)(2,1)S(1)}, u32[]{:S(2)}, u32[]{:S(2)}) collective-permute-start(bf16[832,256]{1,0:T(8,128)(2,1)S(1)} %get-tuple-element.149), channel_id=1, source_target_pairs={{0,3},{1,2},{2,1},{3,0},{4,7},{5,6},{6,5},{7,4},{8,11},{9,10},{10,... | collective-permute-start | bytes 1277960 | tf_op jit(solution)/shard_map/ppermute | solution.py:970
  71.7 12.7 %collective-permute-start.12 = (bf16[192,256]{1,0:T(8,128)(2,1)S(1)}, bf16[192,256]{1,0:T(8,128)(2,1)S(1)}, u32[]{:S(2)}, u32[]{:S(2)}) collective-permute-start(bf16[192,256]{1,0:T(8,128)(2,1)S(1)} %get-tuple-element.167), channel_id=1, source_target_pairs={{0,1},{1,0},{2,3},{3,2},{4,5},{5,4},{6,7},{7,6},{8,9},{9,8},{10,11... | collective-permute-start | bytes 294920 | tf_op jit(solution)/shard_map/ppermute | solution.py:970
  72.1 12.4 %collective-permute-start.13 = (bf16[192,256]{1,0:T(8,128)(2,1)S(1)}, bf16[192,256]{1,0:T(8,128)(2,1)S(1)}, u32[]{:S(2)}, u32[]{:S(2)}) collective-permute-start(bf16[192,256]{1,0:T(8,128)(2,1)S(1)} %get-tuple-element.168), channel_id=1, source_target_pairs={{0,2},{1,3},{2,0},{3,1},{4,6},{5,7},{6,4},{7,5},{8,10},{9,11},{10,... | collective-permute-start | bytes 294920 | tf_op jit(solution)/shard_map/ppermute | solution.py:970
  72.9 11.5 %collective-permute-start.14 = (bf16[192,256]{1,0:T(8,128)(2,1)S(1)}, bf16[192,256]{1,0:T(8,128)(2,1)S(1)}, u32[]{:S(2)}, u32[]{:S(2)}) collective-permute-start(bf16[192,256]{1,0:T(8,128)(2,1)S(1)} %get-tuple-element.169), channel_id=1, source_target_pairs={{0,3},{1,2},{2,1},{3,0},{4,7},{5,6},{6,5},{7,4},{8,11},{9,10},{10,... | collective-permute-start | bytes 294920 | tf_op jit(solution)/shard_map/ppermute | solution.py:970
  75.9 8.5 %collective-permute-start.11 = (bf16[416,256]{1,0:T(8,128)(2,1)S(1)}, bf16[416,256]{1,0:T(8,128)(2,1)S(1)}, u32[]{:S(2)}, u32[]{:S(2)}) collective-permute-start(bf16[416,256]{1,0:T(8,128)(2,1)S(1)} %get-tuple-element.260), channel_id=1, source_target_pairs={{0,4},{4,0},{8,12},{12,8},{16,20},{20,16},{24,28},{28,24},{1,5},{5... | collective-permute-start | bytes 638984 | tf_op jit(solution)/shard_map/ppermute | solution.py:970
  84.6 9.7 %collective-permute-start.16 = (bf16[192,256]{1,0:T(8,128)(2,1)S(1)}, bf16[192,256]{1,0:T(8,128)(2,1)S(1)}, u32[]{:S(2)}, u32[]{:S(2)}) collective-permute-start(bf16[192,256]{1,0:T(8,128)(2,1)S(1)} %add_convert_fusion.6), channel_id=1, source_target_pairs={{0,4},{4,0},{8,12},{12,8},{16,20},{20,16},{24,28},{28,24},{1,5},{5... | collective-permute-start | bytes 294920 | tf_op jit(solution)/shard_map/ppermute | solution.py:970
  85.5 8.8 %collective-permute-start.15 = (bf16[416,256]{1,0:T(8,128)(2,1)S(1)}, bf16[416,256]{1,0:T(8,128)(2,1)S(1)}, u32[]{:S(2)}, u32[]{:S(2)}) collective-permute-start(bf16[416,256]{1,0:T(8,128)(2,1)S(1)} %add_convert_fusion.3), channel_id=1, source_target_pairs={{0,8},{4,12},{8,0},{12,4},{16,24},{20,28},{24,16},{28,20},{1,9},{5... | collective-permute-start | bytes 638984 | tf_op jit(solution)/shard_map/ppermute | solution.py:970
  94.4 17.7 %collective-permute-start.20 = (bf16[416,256]{1,0:T(8,128)(2,1)S(1)}, bf16[416,256]{1,0:T(8,128)(2,1)S(1)}, u32[]{:S(2)}, u32[]{:S(2)}) collective-permute-start(bf16[416,256]{1,0:T(8,128)(2,1)S(1)} %add_convert_fusion.2), channel_id=1, source_target_pairs={{0,16},{4,20},{8,24},{12,28},{16,0},{20,4},{24,8},{28,12},{1,17},{... | collective-permute-start | bytes 638984 | tf_op jit(solution)/shard_map/ppermute | solution.py:970
  107.3 6.1 %collective-permute-start.23 = (bf16[192,256]{1,0:T(8,128)(2,1)S(1)}, bf16[192,256]{1,0:T(8,128)(2,1)S(1)}, u32[]{:S(2)}, u32[]{:S(2)}) collective-permute-start(bf16[192,256]{1,0:T(8,128)(2,1)S(1)} %add_convert_fusion.5), channel_id=1, source_target_pairs={{0,8},{4,12},{8,0},{12,4},{16,24},{20,28},{24,16},{28,20},{1,9},{5... | collective-permute-start | bytes 294920 | tf_op jit(solution)/shard_map/ppermute | solution.py:970
  112.1 9.5 %collective-permute-start.22 = (bf16[416,256]{1,0:T(8,128)(2,1)S(1)}, bf16[416,256]{1,0:T(8,128)(2,1)S(1)}, u32[]{:S(2)}, u32[]{:S(2)}) collective-permute-start(bf16[416,256]{1,0:T(8,128)(2,1)S(1)} %add_convert_fusion.1.own_half), channel_id=1, source_target_pairs={{0,4},{4,0},{8,12},{12,8},{16,20},{20,16},{24,28},{28,24},{1,5},{5... | collective-permute-start | bytes 638984 | tf_op jit(solution)/shard_map/ppermute | solution.py:970
  113.5 7.7 %collective-permute-start.24 = (bf16[192,256]{1,0:T(8,128)(2,1)S(1)}, bf16[192,256]{1,0:T(8,128)(2,1)S(1)}, u32[]{:S(2)}, u32[]{:S(2)}) collective-permute-start(bf16[192,256]{1,0:T(8,128)(2,1)S(1)} %add_convert_fusion.4.score_first), channel_id=1, source_target_pairs={{0,16},{4,20},{8,24},{12,28},{16,0},{20,4},{24,8},{28,12},{1,17},{... | collective-permute-start | bytes 294920 | tf_op jit(solution)/shard_map/ppermute | solution.py:970
  113.9 7.8 %collective-permute-start.21 = (bf16[176,256]{1,0:T(8,128)(2,1)S(1)}, bf16[176,256]{1,0:T(8,128)(2,1)S(1)}, u32[]{:S(2)}, u32[]{:S(2)}) collective-permute-start(bf16[176,256]{1,0:T(8,128)(2,1)S(1)} %add_convert_fusion.9), channel_id=1, source_target_pairs={{0,4},{4,0},{8,12},{12,8},{16,20},{20,16},{24,28},{28,24},{1,5},{5... | collective-permute-start | bytes 270344 | tf_op jit(solution)/shard_map/ppermute | solution.py:970
  121.7 8.6 %collective-permute-start.27 = (bf16[176,256]{1,0:T(8,128)(2,1)S(1)}, bf16[176,256]{1,0:T(8,128)(2,1)S(1)}, u32[]{:S(2)}, u32[]{:S(2)}) collective-permute-start(bf16[176,256]{1,0:T(8,128)(2,1)S(1)} %add_convert_fusion.8), channel_id=1, source_target_pairs={{0,8},{4,12},{8,0},{12,4},{16,24},{20,28},{24,16},{28,20},{1,9},{5... | collective-permute-start | bytes 270344 | tf_op jit(solution)/shard_map/ppermute | solution.py:970
  130.4 5.5 %collective-permute-start.28 = (bf16[176,256]{1,0:T(8,128)(2,1)S(1)}, bf16[176,256]{1,0:T(8,128)(2,1)S(1)}, u32[]{:S(2)}, u32[]{:S(2)}) collective-permute-start(bf16[176,256]{1,0:T(8,128)(2,1)S(1)} %add_convert_fusion.7.first), channel_id=1, source_target_pairs={{0,16},{4,20},{8,24},{12,28},{16,0},{20,4},{24,8},{28,12},{1,17},{... | collective-permute-start | bytes 270344 | tf_op jit(solution)/shard_map/ppermute | solution.py:970
  (22 other events, 175.2 us)
